TPU v7x, 32 devices: a whole 2x2x4 slice. The times are simulated.
32 devices in a mesh: rep: 4 (over x, core), fsdp: 8 (over z, y).
Axes of the slice: x: 2, y: 2, z: 4, core: 2. Of those that a mesh axis runs over, the one named last changes fastest.
Arguments:
- hidden: bfloat16 [17408, 768], P(('rep', 'fsdp')), may hold values from -6 to 6
- region_counts: int32 [64], P(('rep', 'fsdp')), may hold values from 10 to 100, as said below
- w_qkv: bfloat16 [2, 768, 2304], P(None, 'fsdp'), may hold values from -0.21875 to 0.21875
- w_out: bfloat16 [2, 768, 768], P(None, 'fsdp'), may hold values from -0.875 to 0.875
- w_up: bfloat16 [2, 768, 3072], P(None, 'fsdp'), may hold values from -0.21875 to 0.21875
- w_down: bfloat16 [2, 3072, 768], P(None, 'fsdp'), may hold values from -0.109375 to 0.109375
- bias_up: bfloat16 [2, 3072], P(None, 'fsdp'), may hold values from -1.1953125 to 1.1953125
- biases: bfloat16 [2, 6, 768], P(None, None, 'fsdp'), may hold values from -1.1953125 to 1.1953125
- norm_gains: bfloat16 [2, 2, 768], P(None, None, 'fsdp'), may hold values from 0.5 to 1.5
- cotangent: bfloat16 [17408, 768], P(('rep', 'fsdp')), may hold values from -6 to 6
Outputs:
- output: bfloat16 [17408, 768], P(('rep', 'fsdp'))
- grad_hidden: float32 [17408, 768], P(('rep', 'fsdp'))
- grad_w_qkv: float32 [2, 768, 2304], P(None, 'fsdp')
- grad_w_out: float32 [2, 768, 768], P(None, 'fsdp')
- grad_w_up: float32 [2, 768, 3072], P(None, 'fsdp')
- grad_w_down: float32 [2, 3072, 768], P(None, 'fsdp')
- grad_bias_up: float32 [2, 3072], P(None, 'fsdp')
- grad_biases: float32 [2, 6, 768], P(None, None, 'fsdp')
- grad_norm_gains: float32 [2, 2, 768], P(None, None, 'fsdp')
Inputs may be any that keep to these rules, and one draw needn't show every extreme that they name: `region_counts`: each sequence's count of valid region slots; 10 and 100 are both reached in every draw, so region slots from 228 on are never valid.
All inputs are finite; a program needn't handle non-finite values.
Results may differ from a plain program's by a relative error of at most 0.023.
Values may be sent and summed in bfloat16 or wider, within the bound.
No kernel may reach another device: no remote copies, remote signals or barrier semaphores. Data moves between devices by JAX's collectives and lax.ppermute only.
A program may use at most 256 MiB of HBM per device.

v0:
```python
import jax
import jax.numpy as jnp
from jax import lax
from jax.sharding import PartitionSpec as P

HEADS = 12
HEAD_DIM = 64
LAYERS = 2
TEXT = 128
REGIONS = 144


EPSILON = 1e-12
MASKED = -1000000000.0


def layer_norm(states, gain_row, shift_row):
    row_mean = jnp.mean(states, axis=-1, keepdims=True)
    centered = states - row_mean
    variance = jnp.mean(centered * centered, axis=-1, keepdims=True)
    return centered * lax.rsqrt(variance + EPSILON) * gain_row + shift_row


def gelu_exact(pre_act):
    return jax.nn.gelu(pre_act, approximate=False)


def project(left, right):
    return jnp.dot(left, right, preferred_element_type=jnp.float32)


def left_transposed(left, right):
    return lax.dot_general(
        left, right, (((0,), (0,)), ((), ())), preferred_element_type=jnp.float32
    )


def right_transposed(left, right):
    return lax.dot_general(
        left, right, (((1,), (1,)), ((), ())), preferred_element_type=jnp.float32
    )


def attention_scores(queries, key_rows, valid_keys):
    scores = jnp.einsum("sqhd,skhd->shqk", queries, key_rows, preferred_element_type=jnp.float32)
    scores = scores * HEAD_DIM ** (-0.5)
    return jnp.where(valid_keys[:, None, None, :], scores, MASKED)


def layer_forward(states, weights, valid_keys):
    w_qkv, w_out, w_up, w_down, bias_up, biases, norm_gains = weights
    seq_count = valid_keys.shape[0]
    model_width = w_out.shape[0]
    bias_vec = bias_up.astype(jnp.float32)
    bias_rows = biases.astype(jnp.float32)
    gain_rows = norm_gains.astype(jnp.float32)
    states_low = states.astype(jnp.bfloat16)
    qkv_bias = jnp.concatenate([bias_rows[0], jnp.zeros_like(bias_rows[0]), bias_rows[1]])
    projected = (project(states_low, w_qkv) + qkv_bias).astype(jnp.bfloat16)
    heads_view = projected.reshape(seq_count, -1, 3, HEADS, HEAD_DIM)
    scores = attention_scores(heads_view[:, :, 0], heads_view[:, :, 1], valid_keys)
    row_max = jnp.max(scores, axis=-1, keepdims=True)
    exponent = jnp.exp(scores - row_max)
    row_sum = jnp.sum(exponent, axis=-1, keepdims=True)
    soft_weights = (exponent / row_sum).astype(jnp.bfloat16)
    log_total = row_max + jnp.log(row_sum)
    context = jnp.einsum(
        "shqk,skhd->sqhd", soft_weights, heads_view[:, :, 2], preferred_element_type=jnp.float32
    )
    context = context.reshape(-1, model_width).astype(jnp.bfloat16)
    attended = project(context, w_out) + bias_rows[2]
    first_in = states + attended
    first = layer_norm(first_in, gain_rows[0], bias_rows[3])
    first_low = first.astype(jnp.bfloat16)
    hidden_pre = project(first_low, w_up) + bias_vec
    activated = gelu_exact(hidden_pre).astype(jnp.bfloat16)
    second_in = first + project(activated, w_down) + bias_rows[4]
    result = layer_norm(second_in, gain_rows[1], bias_rows[5])
    kept_acts = (
        states_low,
        projected,
        log_total,
        context,
        first_in,
        first_low,
        hidden_pre,
        activated,
        second_in,
    )
    return (result, kept_acts)


def layer_backward(gradient, kept_acts, weights, valid_keys):
    w_qkv, w_out, w_up, w_down, bias_up, biases, norm_gains = weights
    (
        states_low,
        projected,
        log_total,
        context,
        first_in,
        first_low,
        hidden_pre,
        activated,
        second_in,
    ) = kept_acts
    seq_count = valid_keys.shape[0]
    model_width = w_out.shape[0]
    bias_rows = biases.astype(jnp.float32)
    gain_rows = norm_gains.astype(jnp.float32)
    norm_two_pull = jax.vjp(layer_norm, second_in, gain_rows[1], bias_rows[5])[1]
    grad_second_in, grad_gain_two, grad_shift_two = norm_two_pull(gradient)
    grad_ffn = grad_second_in.astype(jnp.bfloat16)
    grad_bias_down = jnp.sum(grad_ffn.astype(jnp.float32), axis=0)
    grad_w_down = left_transposed(activated, grad_ffn)
    grad_activated = right_transposed(grad_ffn, w_down)
    gelu_pull = jax.vjp(gelu_exact, hidden_pre)[1]
    grad_hidden_pre = gelu_pull(grad_activated)[0].astype(jnp.bfloat16)
    grad_bias_up = jnp.sum(grad_hidden_pre.astype(jnp.float32), axis=0)
    grad_w_up = left_transposed(first_low, grad_hidden_pre)
    grad_first = grad_second_in + right_transposed(grad_hidden_pre, w_up)
    norm_one_pull = jax.vjp(layer_norm, first_in, gain_rows[0], bias_rows[3])[1]
    grad_first_in, grad_gain_one, grad_shift_one = norm_one_pull(grad_first)
    grad_attended = grad_first_in.astype(jnp.bfloat16)
    grad_bias_out = jnp.sum(grad_attended.astype(jnp.float32), axis=0)
    grad_w_out = left_transposed(context, grad_attended)
    grad_context = right_transposed(grad_attended, w_out).astype(jnp.bfloat16)
    grad_context = grad_context.reshape(seq_count, -1, HEADS, HEAD_DIM)
    heads_view = projected.reshape(seq_count, -1, 3, HEADS, HEAD_DIM)
    queries = heads_view[:, :, 0]
    key_rows = heads_view[:, :, 1]
    values = heads_view[:, :, 2]
    scores = attention_scores(queries, key_rows, valid_keys)
    soft_probs = jnp.exp(scores - log_total)
    grad_probs = jnp.einsum(
        "sqhd,skhd->shqk", grad_context, values, preferred_element_type=jnp.float32
    )
    grad_values = jnp.einsum(
        "shqk,sqhd->skhd",
        soft_probs.astype(jnp.bfloat16),
        grad_context,
        preferred_element_type=jnp.float32,
    )
    row_dot = jnp.sum(soft_probs * grad_probs, axis=-1, keepdims=True)
    grad_scores = (soft_probs * (grad_probs - row_dot)).astype(jnp.bfloat16)
    grad_queries = jnp.einsum(
        "shqk,skhd->sqhd", grad_scores, key_rows, preferred_element_type=jnp.float32
    ) * HEAD_DIM ** (-0.5)
    grad_keys = jnp.einsum(
        "shqk,sqhd->skhd", grad_scores, queries, preferred_element_type=jnp.float32
    ) * HEAD_DIM ** (-0.5)
    grad_qkv = jnp.stack([grad_queries, grad_keys, grad_values], axis=2)
    grad_qkv = grad_qkv.reshape(-1, 3 * model_width).astype(jnp.bfloat16)
    column_sums = jnp.sum(grad_qkv.astype(jnp.float32), axis=0)
    grad_w_qkv = left_transposed(states_low, grad_qkv)
    grad_states = grad_first_in + right_transposed(grad_qkv, w_qkv)
    grad_biases = jnp.stack(
        [
            column_sums[:model_width],
            column_sums[2 * model_width :],
            grad_bias_out,
            grad_shift_one,
            grad_bias_down,
            grad_shift_two,
        ]
    )
    grad_gains = jnp.stack([grad_gain_one, grad_gain_two])
    return (
        grad_states,
        (grad_w_qkv, grad_w_out, grad_w_up, grad_w_down, grad_bias_up, grad_biases, grad_gains),
    )


def reduce_grads(local_grads):
    shares = (
        lax.psum_scatter(
            local_grads[0].astype(jnp.bfloat16), "fsdp", scatter_dimension=0, tiled=True
        ).astype(jnp.float32),
        lax.psum_scatter(
            local_grads[1].astype(jnp.bfloat16), "fsdp", scatter_dimension=0, tiled=True
        ).astype(jnp.float32),
        lax.psum_scatter(
            local_grads[2].astype(jnp.bfloat16), "fsdp", scatter_dimension=0, tiled=True
        ).astype(jnp.float32),
        lax.psum_scatter(
            local_grads[3].astype(jnp.bfloat16), "fsdp", scatter_dimension=0, tiled=True
        ).astype(jnp.float32),
        lax.psum_scatter(
            local_grads[4].astype(jnp.bfloat16), "fsdp", scatter_dimension=0, tiled=True
        ).astype(jnp.float32),
        lax.psum_scatter(
            local_grads[5].astype(jnp.bfloat16), "fsdp", scatter_dimension=1, tiled=True
        ).astype(jnp.float32),
        lax.psum_scatter(
            local_grads[6].astype(jnp.bfloat16), "fsdp", scatter_dimension=1, tiled=True
        ).astype(jnp.float32),
    )
    return (
        lax.psum(shares[0].astype(jnp.bfloat16), "rep").astype(jnp.float32),
        lax.psum(shares[1].astype(jnp.bfloat16), "rep").astype(jnp.float32),
        lax.psum(shares[2].astype(jnp.bfloat16), "rep").astype(jnp.float32),
        lax.psum(shares[3].astype(jnp.bfloat16), "rep").astype(jnp.float32),
        lax.psum(shares[4].astype(jnp.bfloat16), "rep").astype(jnp.float32),
        lax.psum(shares[5].astype(jnp.bfloat16), "rep").astype(jnp.float32),
        lax.psum(shares[6].astype(jnp.bfloat16), "rep").astype(jnp.float32),
    )


def shards(
    hidden, region_counts, w_qkv, w_out, w_up, w_down, bias_up, biases, norm_gains, cotangent
):
    slot_index = jnp.arange(TEXT + REGIONS)
    valid_keys = (slot_index[None, :] < TEXT) | (
        slot_index[None, :] - TEXT < region_counts[:, None]
    )
    states = hidden.astype(jnp.float32)
    kept_all = []
    gathered_all = []
    for layer_index in range(LAYERS):
        gathered = (
            lax.all_gather(w_qkv[layer_index], "fsdp", axis=0, tiled=True),
            lax.all_gather(w_out[layer_index], "fsdp", axis=0, tiled=True),
            lax.all_gather(w_up[layer_index], "fsdp", axis=0, tiled=True),
            lax.all_gather(w_down[layer_index], "fsdp", axis=0, tiled=True),
            lax.all_gather(bias_up[layer_index], "fsdp", axis=0, tiled=True),
            lax.all_gather(biases[layer_index], "fsdp", axis=1, tiled=True),
            lax.all_gather(norm_gains[layer_index], "fsdp", axis=1, tiled=True),
        )
        states, kept_acts = layer_forward(states, gathered, valid_keys)
        kept_all.append(kept_acts)
        gathered_all.append(gathered)
    output = states.astype(jnp.bfloat16)
    gradient = cotangent.astype(jnp.float32)
    grad_shares = [None] * LAYERS
    for layer_index in reversed(range(LAYERS)):
        gathered = (
            lax.all_gather(w_qkv[layer_index], "fsdp", axis=0, tiled=True),
            lax.all_gather(w_out[layer_index], "fsdp", axis=0, tiled=True),
            lax.all_gather(w_up[layer_index], "fsdp", axis=0, tiled=True),
            lax.all_gather(w_down[layer_index], "fsdp", axis=0, tiled=True),
            lax.all_gather(bias_up[layer_index], "fsdp", axis=0, tiled=True),
            lax.all_gather(biases[layer_index], "fsdp", axis=1, tiled=True),
            lax.all_gather(norm_gains[layer_index], "fsdp", axis=1, tiled=True),
        )
        gradient, local_grads = layer_backward(
            gradient, kept_all[layer_index], gathered, valid_keys
        )
        grad_shares[layer_index] = reduce_grads(local_grads)
    stacked = tuple(
        (
            jnp.stack([grad_shares[layer_index][member] for layer_index in range(LAYERS)])
            for member in range(7)
        )
    )
    return (output, gradient) + stacked


def solution(mesh):
    in_specs = (
        P(("rep", "fsdp"), None),
        P(("rep", "fsdp")),
        P(None, "fsdp", None),
        P(None, "fsdp", None),
        P(None, "fsdp", None),
        P(None, "fsdp", None),
        P(None, "fsdp"),
        P(None, None, "fsdp"),
        P(None, None, "fsdp"),
        P(("rep", "fsdp"), None),
    )
    out_specs = (
        P(("rep", "fsdp"), None),
        P(("rep", "fsdp"), None),
        P(None, "fsdp", None),
        P(None, "fsdp", None),
        P(None, "fsdp", None),
        P(None, "fsdp", None),
        P(None, "fsdp"),
        P(None, None, "fsdp"),
        P(None, None, "fsdp"),
    )
    return jax.shard_map(shards, mesh=mesh, in_specs=in_specs, out_specs=out_specs, check_vma=False)
```

profile of v0, /device:TPU:0, one launch (start us, length us, event | category | flops | bytes accessed | tf_op | source)
XLA Modules:
  0.0 1708.9 jit_solution(7620845838495898224)
XLA Ops:
  16.5 27.9 %all-gather.12 = bf16[1,3072]{1,0:T(2,128)(2,1)S(1)} all-gather(bf16[1,384]{1,0:T(2,128)(2,1)S(1)} %get-tuple-element.135), channel_id=14, replica_groups=mesh['rep'=4,'fsdp'=8] {'fsdp'}, dimensions={1}, use_global_device_ids=true | all-gather | bytes 6912 | tf_op jit(solution)/shard_map/all_gather | solution.py:224
  45.1 26.4 %all-gather.5 = bf16[1,3072]{1,0:T(2,128)(2,1)S(1)} all-gather(bf16[1,384]{1,0:T(2,128)(2,1)S(1)} %get-tuple-element.136), channel_id=7, replica_groups=mesh['rep'=4,'fsdp'=8] {'fsdp'}, dimensions={1}, use_global_device_ids=true | all-gather | bytes 6912 | tf_op jit(solution)/shard_map/all_gather | solution.py:224
  72.0 31.5 %all-gather.3 = bf16[1,2,768]{1,0,2:T(2,128)(2,1)S(1)} all-gather(bf16[1,2,96]{1,0,2:T(2,128)(2,1)S(1)} %copy.166), channel_id=5, replica_groups=mesh['rep'=4,'fsdp'=8] {'fsdp'}, dimensions={2}, use_global_device_ids=true | all-gather | bytes 3456 | tf_op jit(solution)/shard_map/all_gather | solution.py:226
  108.5 31.7 %all-gather.8 = bf16[1,6,768]{1,0,2:T(2,128)(2,1)S(1)} all-gather(bf16[1,6,96]{1,0,2:T(2,128)(2,1)S(1)} %copy.167), channel_id=10, replica_groups=mesh['rep'=4,'fsdp'=8] {'fsdp'}, dimensions={2}, use_global_device_ids=true | all-gather | bytes 10368 | tf_op jit(solution)/shard_map/all_gather | solution.py:225
  140.6 13.3 slice_reduce_fusion
  154.0 32.9 %all-gather.10 = bf16[1,2,768]{1,0,2:T(2,128)(2,1)S(1)} all-gather(bf16[1,2,96]{1,0,2:T(2,128)(2,1)S(1)} %copy.171), channel_id=12, replica_groups=mesh['rep'=4,'fsdp'=8] {'fsdp'}, dimensions={2}, use_global_device_ids=true | all-gather | bytes 3456 | tf_op jit(solution)/shard_map/all_gather | solution.py:226
  192.4 31.7 %all-gather.1 = bf16[1,6,768]{1,0,2:T(2,128)(2,1)S(1)} all-gather(bf16[1,6,96]{1,0,2:T(2,128)(2,1)S(1)} %copy.162), channel_id=3, replica_groups=mesh['rep'=4,'fsdp'=8] {'fsdp'}, dimensions={2}, use_global_device_ids=true | all-gather | bytes 10368 | tf_op jit(solution)/shard_map/all_gather | solution.py:225
  224.5 12.9 slice_reduce_fusion.8
  247.1 6.3 fusion.135
  279.1 20.9 %multiply_convert_fusion.3 = (bf16[544,3072]{1,0:T(8,128)(2,1)}, f32[544,3072]{1,0:T(8,128)}, f32[544,3072]{1,0:T(8,128)}) fusion(f32[3072]{0:T(1024)S(1)} %bitcast.233, bf16[1,768,3072]{2,1,0:T(8,128)(2,1)} %all-gather.27.cloned.1.call-done, f32[544,768]{1,0:T(8,128)S(1)} %get-tuple-element.142, f32[768]{0:T(1024)S(1)} %get-tuple-element.68, ...), kind=kOutput, calls=%fused_computation.37 | convolution fusion | flops 2679300096 | bytes 23124224 | tf_op jit(solution)/shard_map/dot_general | solution.py:29
  300.0 6.3 fusion.146
  306.7 54.9 %all-gather.31.cloned.1.call-done = bf16[1,768,2304]{2,1,0:T(8,128)(2,1)} async-done(((bf16[1,96,2304]{2,1,0:T(8,128)(2,1)}), bf16[1,768,2304]{2,1,0:T(8,128)(2,1)}) %all-gather.31.cloned.1.call-update) | async-done | bytes 3538960 | tf_op jit(solution)/shard_map/all_gather | solution.py:220
  367.3 8.7 reshape.336
  376.0 6.3 fusion.134
  388.6 7.1 fusion.42
  399.1 6.4 fusion.1
  420.8 63.9 %all-gather.35.cloned.1.call-done = bf16[1,768,3072]{2,1,0:T(8,128)(2,1)} async-done(((bf16[1,96,3072]{2,1,0:T(8,128)(2,1)}), bf16[1,768,3072]{2,1,0:T(8,128)(2,1)}) %all-gather.35.cloned.1.call-update) | async-done | bytes 4718608 | tf_op jit(solution)/shard_map/all_gather | solution.py:222
  484.7 22.0 %multiply_convert_fusion.2 = (bf16[544,3072]{1,0:T(8,128)(2,1)}, f32[544,3072]{1,0:T(8,128)}, f32[544,3072]{1,0:T(8,128)}) fusion(f32[3072]{0:T(1024)} %bitcast.235, bf16[1,768,3072]{2,1,0:T(8,128)(2,1)} %all-gather.35.cloned.1.call-done, f32[544,768]{1,0:T(8,128)} %copy-done.15, f32[768]{0:T(1024)} %get-tuple-element.60, f32[768]{0:T(1024)} %get-tuple-element.57, ...), kind=kOutput, calls=%fused_computation.24 | convolution fusion | flops 2679300096 | bytes 23124224 | tf_op jit(solution)/shard_map/dot_general | solution.py:29
  506.7 58.2 %all-gather.37.cloned.1.call-done = bf16[1,3072,768]{2,1,0:T(8,128)(2,1)} async-done(((bf16[1,384,768]{2,1,0:T(8,128)(2,1)}), bf16[1,3072,768]{2,1,0:T(8,128)(2,1)}) %all-gather.37.cloned.1.call-update) | async-done | bytes 4718608 | tf_op jit(solution)/shard_map/all_gather | solution.py:223
  564.9 6.8 fusion.148
  576.0 11.7 fusion.149
  607.2 7.8 fusion.55
  615.0 9.4 multiply_reduce_fusion.1
  624.4 11.9 multiply_convert_fusion.1
  651.4 7.6 convolution_convert_fusion
  659.0 6.7 multiply_reduce_fusion.3
  667.3 10.5 fusion.150
  692.6 11.7 multiply_reduce_fusion
  704.4 11.9 multiply_convert_fusion
  722.1 6.3 fusion.58
  753.9 7.8 convolution_convert_fusion.4
  762.8 7.9 convolution_convert_fusion.2
  772.2 7.8 convolution_convert_fusion.5
  781.2 7.7 convolution_convert_fusion.3
  796.8 29.4 %reduce-scatter.37.cloned.1.call-done = bf16[96,2304]{1,0:T(8,128)(2,1)} async-done(((bf16[768,2304]{1,0:T(8,128)(2,1)}), bf16[96,2304]{1,0:T(8,128)(2,1)}) %reduce-scatter.37.cloned.1.call-update) | async-done | bytes 442384
  828.2 65.6 %reduce-scatter.27.cloned.1.call-done = bf16[96,768]{1,0:T(8,128)(2,1)} async-done(((bf16[768,768]{1,0:T(8,128)(2,1)}), bf16[96,768]{1,0:T(8,128)(2,1)}) %reduce-scatter.27.cloned.1.call-update) | async-done | bytes 147472 | tf_op jit(solution)/shard_map/reduce_scatter | solution.py:178
  893.8 66.9 %reduce-scatter.25.cloned.1.call-done = bf16[96,768]{1,0:T(8,128)(2,1)} async-done(((bf16[768,768]{1,0:T(8,128)(2,1)}), bf16[96,768]{1,0:T(8,128)(2,1)}) %reduce-scatter.25.cloned.1.call-update) | async-done | bytes 147472 | tf_op jit(solution)/shard_map/reduce_scatter | solution.py:178
  960.7 98.1 %reduce-scatter.31.cloned.1.call-done = bf16[96,3072]{1,0:T(8,128)(2,1)} async-done(((bf16[768,3072]{1,0:T(8,128)(2,1)}), bf16[96,3072]{1,0:T(8,128)(2,1)}) %reduce-scatter.31.cloned.1.call-update) | async-done | bytes 589840 | tf_op jit(solution)/shard_map/reduce_scatter | solution.py:181
  1058.7 98.6 %reduce-scatter.35.cloned.1.call-done = bf16[384,768]{1,0:T(8,128)(2,1)} async-done(((bf16[3072,768]{1,0:T(8,128)(2,1)}), bf16[384,768]{1,0:T(8,128)(2,1)}) %reduce-scatter.35.cloned.1.call-update) | async-done | bytes 589840 | tf_op jit(solution)/shard_map/reduce_scatter | solution.py:184
  1157.4 98.7 %reduce-scatter.29.cloned.1.call-done = bf16[96,3072]{1,0:T(8,128)(2,1)} async-done(((bf16[768,3072]{1,0:T(8,128)(2,1)}), bf16[96,3072]{1,0:T(8,128)(2,1)}) %reduce-scatter.29.cloned.1.call-update) | async-done | bytes 589840 | tf_op jit(solution)/shard_map/reduce_scatter | solution.py:181
  1256.0 98.7 %reduce-scatter.33.cloned.1.call-done = bf16[384,768]{1,0:T(8,128)(2,1)} async-done(((bf16[3072,768]{1,0:T(8,128)(2,1)}), bf16[384,768]{1,0:T(8,128)(2,1)}) %reduce-scatter.33.cloned.1.call-update) | async-done | bytes 589840 | tf_op jit(solution)/shard_map/reduce_scatter | solution.py:184
  1356.0 35.9 %all-reduce.2 = (bf16[3072]{0:T(1024)(128)(2,1)S(1)}, bf16[3072]{0:T(1024)(128)(2,1)S(1)}) all-reduce(bf16[3072]{0:T(1024)(128)(2,1)S(1)} %copy-done.80, bf16[3072]{0:T(1024)(128)(2,1)S(1)} %copy-done.81), channel_id=25, replica_groups=mesh['rep'=4,'fsdp'=8] {'fsdp'}, use_global_device_ids=true, to_apply=%region_42.43.clone | all-reduce | flops 6144 | bytes 24576
  1392.1 6.7 add_add_fusion.8
  1398.8 20.0 %reduce-scatter.47.cloned.1.call-done = bf16[96,2]{1,0:T(8,128)(2,1)} async-done(((bf16[768,2]{1,0:T(8,128)(2,1)}), bf16[96,2]{1,0:T(8,128)(2,1)}) %reduce-scatter.47.cloned.1.call-update) | async-done | bytes 400
  1419.6 62.5 %reduce-scatter.45.cloned.1.call-done = bf16[96,2]{1,0:T(8,128)(2,1)} async-done(((bf16[768,2]{1,0:T(8,128)(2,1)}), bf16[96,2]{1,0:T(8,128)(2,1)}) %reduce-scatter.45.cloned.1.call-update) | async-done | bytes 400
  1482.9 62.6 %reduce-scatter.43.cloned.1.call-done = bf16[96,6]{1,0:T(8,128)(2,1)} async-done(((bf16[768,6]{1,0:T(8,128)(2,1)}), bf16[96,6]{1,0:T(8,128)(2,1)}) %reduce-scatter.43.cloned.1.call-update) | async-done | bytes 1168
  1546.3 62.5 %reduce-scatter.41.cloned.1.call-done = bf16[96,6]{1,0:T(8,128)(2,1)} async-done(((bf16[768,6]{1,0:T(8,128)(2,1)}), bf16[96,6]{1,0:T(8,128)(2,1)}) %reduce-scatter.41.cloned.1.call-update) | async-done | bytes 1168
  1617.1 75.1 %all-reduce.7.cloned.1.call-done = (bf16[1,96,2304]{1,2,0:T(8,128)(2,1)}, bf16[1,96,2304]{1,2,0:T(8,128)(2,1)}, bf16[1,96,768]{2,1,0:T(8,128)(2,1)}, bf16[1,96,7...) async-done(((bf16[1,96,2304]{1,2,0:T(8,128)(2,1)}, ...) | async-done | bytes 3538960 | tf_op jit(solution)/shard_map/psum | solution.py:198
  (402 shorter events, 208.3 us)
Async XLA Ops:
  7.2 230.3 %all-gather.23.cloned.1.call-start = ((), (), s32[]{:S(2)}) async-start(), calls=%async_computation.18 | async-start | bytes 3981312 | tf_op jit(solution)/shard_map/all_gather | solution.py:220
  9.5 266.3 %all-gather.25.cloned.1.call-start = ((), (), s32[]{:S(2)}) async-start(), calls=%async_computation.19 | async-start | bytes 1327104 | tf_op jit(solution)/shard_map/all_gather | solution.py:221
  11.4 267.7 %all-gather.27.cloned.1.call-start = ((), (), s32[]{:S(2)}) async-start(), calls=%async_computation.20 | async-start | bytes 5308416 | tf_op jit(solution)/shard_map/all_gather | solution.py:222
  12.6 287.4 %all-gather.29.cloned.1.call-start = ((), (), s32[]{:S(2)}) async-start(), calls=%async_computation.21 | async-start | bytes 5308416 | tf_op jit(solution)/shard_map/all_gather | solution.py:223
  13.7 347.9 %all-gather.31.cloned.1.call-start = ((), (), s32[]{:S(2)}) async-start(), calls=%async_computation.22 | async-start | bytes 3981312 | tf_op jit(solution)/shard_map/all_gather | solution.py:220
  14.3 400.4 %all-gather.33.cloned.1.call-start = ((), (), s32[]{:S(2)}) async-start(), calls=%async_computation.23 | async-start | bytes 1327104 | tf_op jit(solution)/shard_map/all_gather | solution.py:221
  14.9 469.8 %all-gather.35.cloned.1.call-start = ((), (), s32[]{:S(2)}) async-start(), calls=%async_computation.24 | async-start | bytes 5308416 | tf_op jit(solution)/shard_map/all_gather | solution.py:222
  15.6 549.3 %all-gather.37.cloned.1.call-start = ((), (), s32[]{:S(2)}) async-start(), calls=%async_computation.25 | async-start | bytes 5308416 | tf_op jit(solution)/shard_map/all_gather | solution.py:223
  16.4 778.3 %reduce-scatter.39.cloned.1.call-start = ((), (), s32[]{:S(2)}) async-start(), calls=%async_computation.27 | async-start | bytes 3981312
  71.5 207.6 %copy-start.71 = (f32[1,3072]{1,0:T(1,128)}, f32[1,3072]{1,0:T(1,128)S(1)}, u32[]{:S(2)}) copy-start(f32[1,3072]{1,0:T(1,128)S(1)} %convert_element_type.279) | copy-start | bytes 36868
  108.5 191.5 %copy-start.57 = (f32[768]{0:T(1024)}, f32[768]{0:T(1024)S(1)}, u32[]{:S(2)}) copy-start(f32[768]{0:T(1024)S(1)} %get-tuple-element.65) | copy-start | bytes 9220
  108.5 306.2 %copy-start.62 = (f32[768]{0:T(1024)}, f32[768]{0:T(1024)S(1)}, u32[]{:S(2)}) copy-start(f32[768]{0:T(1024)S(1)} %get-tuple-element.64) | copy-start | bytes 9220
  154.0 83.4 %copy-start.94 = (s32[2]{0:T(128)S(1)}, s32[2]{0:T(128)}, u32[]{:S(2)}) copy-start(s32[2]{0:T(128)} %param.11) | copy-start | bytes 28
  154.0 83.6 %copy-start.97 = (bf16[544,768]{1,0:T(8,128)(2,1)S(1)}, bf16[544,768]{1,0:T(8,128)(2,1)}, u32[]{:S(2)}) copy-start(bf16[544,768]{1,0:T(8,128)(2,1)} %param.10) | copy-start | bytes 2506756
  237.4 62.6 %copy-start.83 = (f32[768]{0:T(1024)}, f32[768]{0:T(1024)S(1)}, u32[]{:S(2)}) copy-start(f32[768]{0:T(1024)S(1)} %get-tuple-element.68) | copy-start | bytes 9220
  237.4 124.2 %copy-start.86 = (f32[768]{0:T(1024)}, f32[768]{0:T(1024)S(1)}, u32[]{:S(2)}) copy-start(f32[768]{0:T(1024)S(1)} %get-tuple-element.66) | copy-start | bytes 9220
  278.7 21.3 %copy-start.10 = (f32[544,768]{1,0:T(8,128)}, f32[544,768]{1,0:T(8,128)S(1)}, u32[]{:S(2)}) copy-start(f32[544,768]{1,0:T(8,128)S(1)} %get-tuple-element.142) | copy-start | bytes 5013508
  278.7 21.3 %copy-start.52 = (f32[544]{0:T(1024)}, f32[544]{0:T(1024)S(1)}, u32[]{:S(2)}) copy-start(f32[544]{0:T(1024)S(1)} %broadcast_multiply_fusion.3) | copy-start | bytes 6532
  279.0 20.9 %copy-start.48 = (f32[544]{0:T(1024)}, f32[544]{0:T(1024)S(1)}, u32[]{:S(2)}) copy-start(f32[544]{0:T(1024)S(1)} %multiply_reduce_fusion.11) | copy-start | bytes 6532
  279.1 21.0 %copy-start.64 = (f32[544]{0:T(1024)}, f32[544]{0:T(1024)S(1)}, u32[]{:S(2)}) copy-start(f32[544]{0:T(1024)S(1)} %fusion.104) | copy-start | bytes 6532
  306.3 61.0 %copy-start.18 = (f32[544,768]{1,0:T(8,128)}, f32[544,768]{1,0:T(8,128)S(1)}, u32[]{:S(2)}) copy-start(f32[544,768]{1,0:T(8,128)S(1)} %get-tuple-element.145) | copy-start | bytes 5013508
  306.7 60.6 %copy-start.50 = (f32[544]{0:T(1024)}, f32[544]{0:T(1024)S(1)}, u32[]{:S(2)}) copy-start(f32[544]{0:T(1024)S(1)} %multiply_reduce_fusion.10) | copy-start | bytes 6532
  306.7 108.0 %copy-start.69 = (f32[544]{0:T(1024)}, f32[544]{0:T(1024)S(1)}, u32[]{:S(2)}) copy-start(f32[544]{0:T(1024)S(1)} %fusion.105) | copy-start | bytes 6532
  575.1 12.6 slice-start.2
  575.9 11.8 copy-start.32
  575.9 11.8 copy-start.16
  575.9 11.8 copy-start.60
  575.9 11.8 copy-start.67
  576.0 11.8 slice-start.3
  666.4 11.4 slice-start
  666.4 159.7 %reduce-scatter.37.cloned.1.call-start = ((), (), s32[]{:S(2)}) async-start(), calls=%async_computation.26 | async-start | bytes 3981312
  667.3 10.5 copy-start.58
  704.4 11.9 copy-start.5
  746.8 147.0 %reduce-scatter.27.cloned.1.call-start = ((), (), s32[]{:S(2)}) async-start(), calls=%async_computation.13 | async-start | bytes 1327104 | tf_op jit(solution)/shard_map/reduce_scatter | solution.py:178
  750.3 210.3 %reduce-scatter.25.cloned.1.call-start = ((), (), s32[]{:S(2)}) async-start(), calls=%async_computation.12 | async-start | bytes 1327104 | tf_op jit(solution)/shard_map/reduce_scatter | solution.py:178
  753.8 305.0 %reduce-scatter.31.cloned.1.call-start = ((), (), s32[]{:S(2)}) async-start(), calls=%async_computation.15 | async-start | bytes 5308416 | tf_op jit(solution)/shard_map/reduce_scatter | solution.py:181
  761.7 395.7 %reduce-scatter.35.cloned.1.call-start = ((), (), s32[]{:S(2)}) async-start(), calls=%async_computation.17 | async-start | bytes 5308416 | tf_op jit(solution)/shard_map/reduce_scatter | solution.py:184
  770.8 485.3 %reduce-scatter.29.cloned.1.call-start = ((), (), s32[]{:S(2)}) async-start(), calls=%async_computation.14 | async-start | bytes 5308416 | tf_op jit(solution)/shard_map/reduce_scatter | solution.py:181
  780.1 574.6 %reduce-scatter.33.cloned.1.call-start = ((), (), s32[]{:S(2)}) async-start(), calls=%async_computation.16 | async-start | bytes 5308416 | tf_op jit(solution)/shard_map/reduce_scatter | solution.py:184
  789.0 629.8 %reduce-scatter.47.cloned.1.call-start = ((), (), s32[]{:S(2)}) async-start(), calls=%async_computation.31 | async-start | bytes 221184
  791.2 690.9 %reduce-scatter.45.cloned.1.call-start = ((), (), s32[]{:S(2)}) async-start(), calls=%async_computation.30 | async-start | bytes 221184
  792.1 753.3 %reduce-scatter.43.cloned.1.call-start = ((), (), s32[]{:S(2)}) async-start(), calls=%async_computation.29 | async-start | bytes 221184
  793.3 561.5 %copy-start.98 = (u32[32]{0:T(128)S(1)}, u32[32]{0:T(128)}, u32[]{:S(2)}) copy-start(u32[32]{0:T(128)} %constant.110) | copy-start | bytes 388
  793.3 562.7 %copy-start.80 = (bf16[3072]{0:T(1024)(128)(2,1)S(1)}, bf16[3072]{0:T(1024)(128)(2,1)}, u32[]{:S(2)}) copy-start(bf16[3072]{0:T(1024)(128)(2,1)} %get-tuple-element.160) | copy-start | bytes 18436
  793.3 562.7 %copy-start.81 = (bf16[3072]{0:T(1024)(128)(2,1)S(1)}, bf16[3072]{0:T(1024)(128)(2,1)}, u32[]{:S(2)}) copy-start(bf16[3072]{0:T(1024)(128)(2,1)} %get-tuple-element.162) | copy-start | bytes 18436
  793.3 598.8 %copy-start.14 = (f32[544,768]{1,0:T(8,128)S(1)}, f32[544,768]{1,0:T(8,128)}, u32[]{:S(2)}) copy-start(f32[544,768]{1,0:T(8,128)} %copy-done.13) | copy-start | bytes 5013508
  793.3 815.4 %reduce-scatter.41.cloned.1.call-start = ((), (), s32[]{:S(2)}) async-start(), calls=%async_computation.28 | async-start | bytes 221184
  794.6 897.6 %all-reduce.7.cloned.1.call-start = ((), (), s32[]{:S(2)}) async-start(), calls=%async_computation.32 | async-start | bytes 7667712 | tf_op jit(solution)/shard_map/psum | solution.py:198
  (77 other events, 331.3 us)
Sparse Core Ops, SparseCore 0:
  10.8 69.5 all-gather.22
  82.6 42.0 all-gather.24
  127.5 87.4 all-gather.26
  217.6 78.5 all-gather.28
  298.3 63.3 all-gather.30
  363.7 39.5 all-gather.32
  406.0 78.6 all-gather.34
  486.9 78.0 all-gather.36
  666.6 77.2 reduce-scatter.38
  747.3 78.7 reduce-scatter.36
  830.1 63.6 reduce-scatter.26
  897.6 62.9 reduce-scatter.24
  964.3 94.3 reduce-scatter.30
  1062.2 95.0 reduce-scatter.34
  1160.9 95.1 reduce-scatter.28
  1259.5 95.1 reduce-scatter.32
  1357.8 60.9 reduce-scatter.46
  1421.9 60.1 reduce-scatter.44
  1485.3 60.1 reduce-scatter.42
  1548.6 60.1 reduce-scatter.40
  1612.2 79.9 all-reduce.6
where the time goes:
time: 1720 us; the launch traced here: 1710 us
  waiting for transfers between devices  1020 us (59%)
  matrix products  232 us (13%)
  blocking collectives  224 us (13%)
  local copies, waits for them, and re-layouts  157 us (9%)
  other arithmetic  59.5 us (3%)
    unnamed x27, waiting for transfers between devices  240 us
    reduce_scatter x2, waiting for transfers between devices, reduce_grads(): lax.psum_scatter(local_grads[3].astype(jnp.bfloat16), 'fsdp', scatter_dim...  197 us
    reduce_scatter x2, waiting for transfers between devices, reduce_grads(): lax.psum_scatter(local_grads[2].astype(jnp.bfloat16), 'fsdp', scatter_dim...  197 us
    reduce_scatter x2, waiting for transfers between devices, reduce_grads(): lax.psum_scatter(local_grads[1].astype(jnp.bfloat16), 'fsdp', scatter_dim...  132 us
    psum x1, waiting for transfers between devices, reduce_grads(): lax.psum(shares[0].astype(jnp.bfloat16), 'rep').astype(jnp.float32)  75.1 us
    dot_general x8, matrix products, project(): return jnp.dot(left, right, preferred_element_type=jnp.float32)  71.9 us
    all_gather x2, blocking collectives, shards(): lax.all_gather(norm_gains[layer_index], 'fsdp', axis=1, tiled=True)  64.4 us
    all_gather x2, waiting for transfers between devices, shards(): lax.all_gather(w_up[layer_index], 'fsdp', axis=0, tiled=True)  63.9 us
  transfers between devices with their start and end apart: 21, of which 15 were waited for; matrix products, arithmetic and copies ran while one was open for 19% of the time, Pallas kernels for 0%

commit v1 on v0

v1 whole, which is shorter than its diff:
```python
import functools

import jax
import jax.numpy as jnp
from jax import lax
from jax.experimental import pallas as pl
from jax.experimental.pallas import tpu as pltpu
from jax.sharding import PartitionSpec as P

HEADS = 12
HEAD_DIM = 64
LAYERS = 2
TEXT = 128
KEYS = 256
WIDE = 768
HALF = WIDE // 2
PAIR = 2 * HEAD_DIM
PAIRS = HEADS // 2
EPSILON = 1e-12
MASKED = -1000000000.0
AXES = ("rep", "fsdp")
VMEM_LIMIT = 60 * 1024 * 1024


def low(value):
    return value.astype(jnp.bfloat16)


def full(value):
    return value.astype(jnp.float32)


def mm(left, right):
    return jnp.dot(left, right, preferred_element_type=jnp.float32)


def mm_t(left, right):
    return lax.dot_general(
        left, right, (((1,), (1,)), ((), ())), preferred_element_type=jnp.float32
    )


def t_mm(left, right):
    return lax.dot_general(
        left, right, (((0,), (0,)), ((), ())), preferred_element_type=jnp.float32
    )


def flip(at, by):
    return 1 - at if by else at


class Place:
    def __init__(self, pos_ref, depth):
        self.core, self.side = pos_ref[0], pos_ref[1]
        self.row, self.level = pos_ref[2], pos_ref[3]
        self.depth = depth

    def shard(self, far_row, far_level):
        return lax.rem(self.level + self.depth - far_level, self.depth) * 2 + flip(
            self.row, far_row
        )

    def far_level(self, level):
        return lax.rem(self.level + self.depth - level, self.depth)


def half_lanes(at):
    return pl.ds(pl.multiple_of(at * HALF, HALF), HALF)


def load_unit(place, own, other, whole, sem, by_rows, side_first):
    for far_core, part in ((0, own), (1, other)):
        core = flip(place.core, far_core)
        for first in range(2):
            for second in range(2):
                far_side, far_row = (second, first) if side_first else (first, second)
                side = flip(place.side, far_side)
                for far_level in range(place.depth):
                    shard = place.shard(far_row, far_level)
                    blocks = pl.ds(side * 2, 2)
                    if by_rows:
                        target = whole.at[shard, blocks, :, half_lanes(core)]
                    else:
                        target = whole.at[blocks, shard, :, half_lanes(core)]
                    pltpu.make_async_copy(
                        part.at[first, second, far_level], target, sem
                    ).start()


def wait_all(ref, sem):
    pltpu.make_async_copy(ref, ref, sem).wait()


def store_columns(place, block, held, out, sem, side_first):
    far_side = place.side if block // 2 == 0 else 1 - place.side
    for far_core in range(2):
        core = flip(place.core, far_core)
        for far_row in range(2):
            for far_level in range(place.depth):
                shard = place.shard(far_row, far_level)
                at = (far_side, far_row) if side_first else (far_row, far_side)
                pltpu.make_async_copy(
                    held.at[shard, :, half_lanes(core)],
                    out.at[far_core, at[0], at[1], far_level, block % 2],
                    sem,
                ).start()


def store_rows(place, tile, held, out, sem, side_first):
    count = held.shape[0]
    for inner in range(count):
        shard = tile * count + inner
        far_row = place.row if shard % 2 == 0 else 1 - place.row
        far_level = place.far_level(shard // 2)
        for block in range(4):
            far_side = place.side if block // 2 == 0 else 1 - place.side
            at = (far_side, far_row) if side_first else (far_row, far_side)
            for half in range(2):
                far_core = place.core if half == 0 else 1 - place.core
                pltpu.make_async_copy(
                    held.at[inner, block, :, pl.ds(half * HALF, HALF)],
                    out.at[far_core, at[0], at[1], far_level, block % 2],
                    sem,
                ).start()


def chunks(rows):
    size = rows // 4 if rows % 64 == 0 or (rows // 4) % 8 == 0 else rows
    return [(start, size) for start in range(0, rows, size)]


def normalize(value):
    centered = value - jnp.mean(value, axis=-1, keepdims=True)
    scale = lax.rsqrt(jnp.mean(centered * centered, axis=-1, keepdims=True) + EPSILON)
    return centered * scale, scale


def norm_backward(grad, hat, scale, gain):
    direct = grad * gain
    return (
        direct
        - jnp.mean(direct, axis=-1, keepdims=True)
        - hat * jnp.mean(direct * hat, axis=-1, keepdims=True)
    ) * scale


def gelu_and_slope(value):
    size = jnp.abs(value) * 0.7071067811865476
    t = 1.0 / (1.0 + 0.3275911 * size)
    series = t * (
        0.127414796
        + t * (-0.142248368 + t * (0.7107068705 + t * (-0.7265760135 + t * 0.5307027145)))
    )
    bell = jnp.exp(-0.5 * value * value)
    tail = series * bell
    below = jnp.where(value >= 0, 1.0 - tail, tail)
    return value * below, below + value * bell * 0.3989422804014327


def attention_forward(
    depth, side_first, seqs, pos_ref, counts_ref, x_ref, own_ref, other_ref,
    qkv_bias_ref, out_bias_ref, gain_ref, shift_ref,
    first_ref, hat_ref, scale_ref, x_t_ref, ctx_t_ref, first_t_ref, qkv_ref, probs_ref,
    weight, ctx, held, weight_sem, held_sem,
):
    place = Place(pos_ref, depth)
    load_unit(place, own_ref, other_ref, weight, weight_sem, False, side_first)
    tokens = x_ref.shape[0]
    slots = tokens // seqs
    x_low = low(x_ref[...])
    x_t_ref[...] = x_low.T
    wait_all(weight, weight_sem)
    for block in range(3):
        out = mm(x_low, weight[block].reshape(WIDE, WIDE))
        out = low(out + qkv_bias_ref[:, block * WIDE : (block + 1) * WIDE])
        for pair in range(PAIRS):
            qkv_ref[block * PAIRS + pair] = out[:, pair * PAIR : (pair + 1) * PAIR]
    lane = lax.broadcasted_iota(jnp.int32, (KEYS, PAIR), 1)
    key = lax.broadcasted_iota(jnp.int32, (slots, KEYS), 1)
    for seq in range(seqs):
        valid = key < TEXT + counts_ref[seq]

        def pair_step(pair, carry, seq=seq, valid=valid):
            start = seq * slots
            slot = lax.rem(pair, 2)
            q = qkv_ref[pair, start : start + slots, :] * jnp.bfloat16(HEAD_DIM**-0.5)
            k = qkv_ref[PAIRS + pair, start : start + KEYS, :]
            v = qkv_ref[2 * PAIRS + pair, start : start + KEYS, :]
            none = jnp.zeros_like(k)
            k_both = jnp.concatenate(
                [jnp.where(lane < HEAD_DIM, k, none), jnp.where(lane < HEAD_DIM, none, k)], 0
            )
            v_both = jnp.concatenate(
                [jnp.where(lane < HEAD_DIM, v, none), jnp.where(lane < HEAD_DIM, none, v)], 0
            )
            scores = mm_t(q, k_both)
            halves = []
            for half in range(2):
                part = jnp.where(valid, scores[:, half * KEYS : (half + 1) * KEYS], MASKED)
                part = jnp.exp(part - jnp.max(part, axis=-1, keepdims=True))
                halves.append(low(part / jnp.sum(part, axis=-1, keepdims=True)))
            probs = jnp.concatenate(halves, 1)

            @pl.when(pair >= 2)
            def _():
                wait_all(held.at[slot], held_sem.at[slot])

            held[slot] = probs
            pltpu.make_async_copy(
                held.at[slot], probs_ref.at[seq, pair], held_sem.at[slot]
            ).start()
            ctx[pair, start : start + slots, :] = low(mm(probs, v_both))
            return carry

        lax.fori_loop(0, PAIRS, pair_step, 0)
        for slot in range(2):
            wait_all(held.at[slot], held_sem.at[slot])
    context = jnp.concatenate([ctx[pair] for pair in range(PAIRS)], 1)
    ctx_t_ref[...] = context.T
    first_ref[...] = mm(context, weight[3].reshape(WIDE, WIDE))
    for start, size in chunks(tokens):
        rows = pl.ds(start, size)
        hat, scale = normalize(full(x_ref[rows, :]) + (first_ref[rows, :] + out_bias_ref[...]))
        hat_ref[rows, :] = hat
        scale_ref[rows, :] = jnp.broadcast_to(scale, (size, 128))
        first_ref[rows, :] = hat * gain_ref[...] + shift_ref[...]
    first_t_ref[...] = low(first_ref[...]).T


def mlp_forward(
    depth, up_side_first, down_side_first, pos_ref, first_ref, up_own_ref, up_other_ref, down_own_ref, down_other_ref,
    up_bias_ref, down_bias_ref, gain_ref, shift_ref,
    out_ref, hat_ref, scale_ref, act_t_ref, slope_ref,
    up, down, pre, act, act_t, slope, up_sem, down_sem, act_sem, slope_sem,
):
    place = Place(pos_ref, depth)
    load_unit(place, up_own_ref, up_other_ref, up, up_sem, False, up_side_first)
    load_unit(place, down_own_ref, down_other_ref, down, down_sem, True, down_side_first)
    tokens = first_ref.shape[0]
    first_low = low(first_ref[...])
    shards = down.shape[0] // 4
    wait_all(up, up_sem)
    total = None
    for tile in range(4):
        slot = tile % 2
        pre[...] = mm(first_low, up[tile].reshape(WIDE, WIDE))
        if tile >= 2:
            wait_all(slope.at[slot], slope_sem.at[slot])
            wait_all(act_t.at[slot], act_sem.at[slot])

        def row_step(step, carry, tile=tile, slot=slot):
            rows = pl.ds(pl.multiple_of(step * 32, 32), 32)
            value = pre[rows, :] + up_bias_ref[:, tile * WIDE : (tile + 1) * WIDE]
            gelu, rise = gelu_and_slope(value)
            act[rows, :] = low(gelu)
            slope[slot, rows, :] = low(rise)
            return carry

        lax.fori_loop(0, tokens // 32, row_step, 0)
        pltpu.make_async_copy(slope.at[slot], slope_ref.at[tile], slope_sem.at[slot]).start()
        act_t[slot] = act[...].T
        pltpu.make_async_copy(act_t.at[slot], act_t_ref.at[tile], act_sem.at[slot]).start()
        if tile == 0:
            wait_all(down, down_sem)
        part = mm(act[...], down[tile * shards : (tile + 1) * shards].reshape(WIDE, WIDE))
        if tile == 0:
            out_ref[...] = part
        else:
            out_ref[...] += part
    for start, size in chunks(tokens):
        rows = pl.ds(start, size)
        hat, scale = normalize(first_ref[rows, :] + out_ref[rows, :] + down_bias_ref[...])
        hat_ref[rows, :] = hat
        scale_ref[rows, :] = jnp.broadcast_to(scale, (size, 128))
        out_ref[rows, :] = hat * gain_ref[...] + shift_ref[...]
    for slot in range(2):
        wait_all(slope.at[slot], slope_sem.at[slot])
        wait_all(act_t.at[slot], act_sem.at[slot])


def norm_step(grad_ref, hat_ref, scale_ref, gain_ref, out_ref, gain_grad_ref, shift_grad_ref, bias_grad_ref):
    sums = [0.0, 0.0, 0.0]
    for start, size in chunks(grad_ref.shape[0]):
        rows = pl.ds(start, size)
        grad, hat = full(grad_ref[rows, :]), hat_ref[rows, :]
        grad_in = norm_backward(grad, hat, scale_ref[rows, :][:, :1], gain_ref[...])
        out_ref[rows, :] = grad_in
        for at, value in enumerate((grad * hat, grad, full(low(grad_in)))):
            sums[at] += jnp.sum(value, axis=0, keepdims=True)
    gain_grad_ref[...], shift_grad_ref[...], bias_grad_ref[...] = sums


def down_backward(
    depth, side_first, pos_ref, grad_ref, hat_ref, scale_ref, gain_ref, act_t_ref,
    second_ref, gain_grad_ref, shift_grad_ref, bias_grad_ref, out_ref,
    act_t, held, act_sem, held_sem,
):
    place = Place(pos_ref, depth)
    pltpu.make_async_copy(act_t_ref, act_t, act_sem).start()
    norm_step(
        grad_ref, hat_ref, scale_ref, gain_ref, second_ref, gain_grad_ref, shift_grad_ref, bias_grad_ref
    )
    grad_low = low(second_ref[...])
    wait_all(act_t, act_sem)
    for tile in range(4):
        slot = tile % 2
        if tile >= 2:
            wait_all(held.at[slot], held_sem.at[slot])
        held[slot] = low(mm(act_t[tile], grad_low)).reshape(held.shape[1:])
        store_rows(place, tile, held.at[slot], out_ref, held_sem.at[slot], side_first)
    for slot in range(2):
        wait_all(held.at[slot], held_sem.at[slot])


def up_backward(
    depth, up_side_first, down_side_first, out_side_first, pos_ref, second_ref, up_own_ref, up_other_ref, down_own_ref,
    down_other_ref, slope_ref, first_t_ref, hat_ref, scale_ref, gain_ref,
    first_in_ref, gain_grad_ref, shift_grad_ref, bias_grad_ref, up_grad_ref, out_ref,
    up, down, slope, total, held, up_sem, down_sem, slope_sem, held_sem,
):
    place = Place(pos_ref, depth)
    load_unit(place, down_own_ref, down_other_ref, down, down_sem, True, down_side_first)
    load_unit(place, up_own_ref, up_other_ref, up, up_sem, False, up_side_first)
    pltpu.make_async_copy(slope_ref, slope, slope_sem).start()
    shards = down.shape[0] // 4
    grad_low = low(second_ref[...])
    first_t = first_t_ref[...]
    total[...] = second_ref[...]
    wait_all(down, down_sem)
    wait_all(slope, slope_sem)
    wait_all(up, up_sem)
    for tile in range(4):
        slot = tile % 2
        grad = mm_t(grad_low, down[tile * shards : (tile + 1) * shards].reshape(WIDE, WIDE))
        grad = low(grad * full(slope[tile]))
        up_grad_ref[:, tile * WIDE : (tile + 1) * WIDE] = jnp.sum(
            full(grad), axis=0, keepdims=True
        )
        if tile >= 2:
            wait_all(held.at[slot], held_sem.at[slot])
        held[slot] = low(mm(first_t, grad)).reshape(held.shape[1:])
        store_columns(place, tile, held.at[slot], out_ref, held_sem.at[slot], out_side_first)
        total[...] += mm_t(grad, up[tile].reshape(WIDE, WIDE))
    norm_step(
        total, hat_ref, scale_ref, gain_ref, first_in_ref, gain_grad_ref, shift_grad_ref, bias_grad_ref
    )
    for slot in range(2):
        wait_all(held.at[slot], held_sem.at[slot])


def attention_backward(
    depth, side_first, out_side_first, seqs, pos_ref, grad_ref, own_ref, other_ref, ctx_t_ref, x_t_ref, qkv_ref, probs_ref,
    x_grad_ref, qkv_grad_ref, out_ref,
    weight, probs, ctx_grad, grads, held, weight_sem, probs_sem, held_sem,
):
    place = Place(pos_ref, depth)
    load_unit(place, own_ref, other_ref, weight, weight_sem, False, side_first)
    pltpu.make_async_copy(probs_ref, probs, probs_sem).start()
    tokens = grad_ref.shape[0]
    slots = tokens // seqs
    grad_low = low(grad_ref[...])
    held[0] = low(mm(ctx_t_ref[...], grad_low)).reshape(held.shape[1:])
    store_columns(place, 3, held.at[0], out_ref, held_sem.at[0], out_side_first)
    wait_all(weight, weight_sem)
    from_out = low(mm_t(grad_low, weight[3].reshape(WIDE, WIDE)))
    for pair in range(PAIRS):
        ctx_grad[pair] = from_out[:, pair * PAIR : (pair + 1) * PAIR]
    wait_all(probs, probs_sem)
    lane = lax.broadcasted_iota(jnp.int32, (KEYS, PAIR), 1)
    for seq in range(seqs):

        def pair_step(pair, carry, seq=seq):
            start = seq * slots
            q = qkv_ref[pair, start : start + slots, :]
            k = qkv_ref[PAIRS + pair, start : start + KEYS, :]
            v = qkv_ref[2 * PAIRS + pair, start : start + KEYS, :]
            out_grad = ctx_grad[pair, start : start + slots, :]
            none = jnp.zeros_like(k)
            k_both = jnp.concatenate(
                [jnp.where(lane < HEAD_DIM, k, none), jnp.where(lane < HEAD_DIM, none, k)], 0
            )
            v_both = jnp.concatenate(
                [jnp.where(lane < HEAD_DIM, v, none), jnp.where(lane < HEAD_DIM, none, v)], 0
            )
            weights = probs[seq, pair]
            probs_grad = mm_t(out_grad, v_both)
            halves = []
            for half in range(2):
                lanes = slice(half * KEYS, (half + 1) * KEYS)
                weight_part, grad_part = full(weights[:, lanes]), probs_grad[:, lanes]
                dot = jnp.sum(weight_part * grad_part, axis=-1, keepdims=True)
                halves.append(low(weight_part * (grad_part - dot)))
            scores_grad = jnp.concatenate(halves, 1)
            q_grad = mm(scores_grad, k_both) * HEAD_DIM**-0.5
            grads[pair, start : start + slots, :] = low(q_grad)
            k_grad = t_mm(q, scores_grad) * HEAD_DIM**-0.5
            v_grad = t_mm(out_grad, weights)
            for at, value in ((PAIRS, k_grad), (2 * PAIRS, v_grad)):
                value = jnp.concatenate(
                    [value[:HEAD_DIM, :KEYS], value[HEAD_DIM:, KEYS:]], 0
                )
                grads[at + pair, start : start + KEYS, :] = low(value.T)
                grads[at + pair, start + KEYS : start + slots, :] = jnp.zeros(
                    (slots - KEYS, PAIR), jnp.bfloat16
                )
            return carry

        lax.fori_loop(0, PAIRS, pair_step, 0)
    x_t = x_t_ref[...]
    x_grad_ref[...] = grad_ref[...]
    for block in range(3):
        slot = (block + 1) % 2
        grad = jnp.concatenate([grads[block * PAIRS + pair] for pair in range(PAIRS)], 1)
        qkv_grad_ref[:, block * WIDE : (block + 1) * WIDE] = jnp.sum(
            full(grad), axis=0, keepdims=True
        )
        if block >= 1:
            wait_all(held.at[slot], held_sem.at[slot])
        held[slot] = low(mm(x_t, grad)).reshape(held.shape[1:])
        store_columns(place, block, held.at[slot], out_ref, held_sem.at[slot], out_side_first)
        x_grad_ref[...] += mm_t(grad, weight[block].reshape(WIDE, WIDE))
    for slot in range(2):
        wait_all(held.at[slot], held_sem.at[slot])


VMEM = pltpu.MemorySpace.VMEM
SMEM = pltpu.MemorySpace.SMEM
ANY = pl.ANY
F32 = jnp.float32
BF16 = jnp.bfloat16


def call(kernel, spaces, outs, scratch, flops):
    return pl.pallas_call(
        kernel,
        in_specs=[pl.BlockSpec(memory_space=space) for space in spaces],
        out_specs=[pl.BlockSpec(memory_space=space) for _, _, space in outs],
        out_shape=[jax.ShapeDtypeStruct(shape, dtype) for shape, dtype, _ in outs],
        scratch_shapes=scratch,
        compiler_params=pltpu.CompilerParams(vmem_limit_bytes=VMEM_LIMIT),
        cost_estimate=pl.CostEstimate(flops=flops, bytes_accessed=1 << 20, transcendentals=0),
    )


DMA = pltpu.SemaphoreType.DMA


class Sizes:
    def __init__(self, tokens, seqs, shards, rows):
        self.tokens, self.seqs, self.shards, self.rows = tokens, seqs, shards, rows
        self.depth = shards // 2
        self.slots = tokens // seqs

    def columns(self, count):
        return pltpu.VMEM((count, self.shards, self.rows, WIDE), BF16)

    def by_rows(self):
        return pltpu.VMEM((self.shards, 4, self.rows, WIDE), BF16)

    def unit_grad(self):
        return ((2, 2, 2, self.depth, 2, self.rows, HALF), BF16, ANY)


def run_attention_forward(z, pos, counts, x, unit, side_first, qkv_bias, out_bias, gain, shift):
    t = z.tokens
    return call(
        functools.partial(attention_forward, z.depth, side_first, z.seqs),
        [SMEM, SMEM, VMEM, ANY, ANY, VMEM, VMEM, VMEM, VMEM],
        [
            ((t, WIDE), F32, VMEM),
            ((t, WIDE), F32, VMEM),
            ((t, 128), F32, VMEM),
            ((WIDE, t), BF16, VMEM),
            ((WIDE, t), BF16, VMEM),
            ((WIDE, t), BF16, VMEM),
            ((3 * PAIRS, t, PAIR), BF16, VMEM),
            ((z.seqs, PAIRS, z.slots, 2 * KEYS), BF16, ANY),
        ],
        [
            z.columns(4),
            pltpu.VMEM((PAIRS, t, PAIR), BF16),
            pltpu.VMEM((2, z.slots, 2 * KEYS), BF16),
            DMA,
            DMA((2,)),
        ],
        12 * 10**9,
    )(pos, counts, x, unit[0], unit[1], qkv_bias, out_bias, gain, shift)


def run_mlp_forward(z, pos, first, up, up_side_first, down, down_side_first, up_bias, down_bias, gain, shift):
    t = z.tokens
    return call(
        functools.partial(mlp_forward, z.depth, up_side_first, down_side_first),
        [SMEM, VMEM, ANY, ANY, ANY, ANY, VMEM, VMEM, VMEM, VMEM],
        [
            ((t, WIDE), F32, VMEM),
            ((t, WIDE), F32, VMEM),
            ((t, 128), F32, VMEM),
            ((4, WIDE, t), BF16, ANY),
            ((4, t, WIDE), BF16, ANY),
        ],
        [
            z.columns(4),
            z.by_rows(),
            pltpu.VMEM((t, WIDE), F32),
            pltpu.VMEM((t, WIDE), BF16),
            pltpu.VMEM((2, WIDE, t), BF16),
            pltpu.VMEM((2, t, WIDE), BF16),
            DMA,
            DMA,
            DMA((2,)),
            DMA((2,)),
        ],
        16 * 10**9,
    )(pos, first, up[0], up[1], down[0], down[1], up_bias, down_bias, gain, shift)


def run_down_backward(z, pos, grad, hat, scale, gain, act_t, out_side_first):
    t = z.tokens
    return call(
        functools.partial(down_backward, z.depth, out_side_first),
        [SMEM, VMEM, VMEM, VMEM, VMEM, ANY],
        [
            ((t, WIDE), F32, VMEM),
            ((1, WIDE), F32, VMEM),
            ((1, WIDE), F32, VMEM),
            ((1, WIDE), F32, VMEM),
            z.unit_grad(),
        ],
        [
            pltpu.VMEM((4, WIDE, t), BF16),
            pltpu.VMEM((2, z.shards // 4, 4, z.rows, WIDE), BF16),
            DMA,
            DMA((2,)),
        ],
        8 * 10**9,
    )(pos, grad, hat, scale, gain, act_t)


def run_up_backward(z, pos, second, up, up_side_first, down, down_side_first, slope, first_t, hat, scale, gain, out_side_first):
    t = z.tokens
    return call(
        functools.partial(up_backward, z.depth, up_side_first, down_side_first, out_side_first),
        [SMEM, VMEM, ANY, ANY, ANY, ANY, ANY, VMEM, VMEM, VMEM, VMEM],
        [
            ((t, WIDE), F32, VMEM),
            ((1, WIDE), F32, VMEM),
            ((1, WIDE), F32, VMEM),
            ((1, WIDE), F32, VMEM),
            ((1, 4 * WIDE), F32, VMEM),
            z.unit_grad(),
        ],
        [
            z.columns(4),
            z.by_rows(),
            pltpu.VMEM((4, t, WIDE), BF16),
            pltpu.VMEM((t, WIDE), F32),
            pltpu.VMEM((2, z.shards, z.rows, WIDE), BF16),
            DMA,
            DMA,
            DMA,
            DMA((2,)),
        ],
        20 * 10**9,
    )(pos, second, up[0], up[1], down[0], down[1], slope, first_t, hat, scale, gain)


def run_attention_backward(z, pos, grad, unit, side_first, ctx_t, x_t, qkv, probs, out_side_first):
    t = z.tokens
    return call(
        functools.partial(attention_backward, z.depth, side_first, out_side_first, z.seqs),
        [SMEM, VMEM, ANY, ANY, VMEM, VMEM, VMEM, ANY],
        [
            ((t, WIDE), F32, VMEM),
            ((1, 3 * WIDE), F32, VMEM),
            z.unit_grad(),
        ],
        [
            z.columns(4),
            pltpu.VMEM((z.seqs, PAIRS, z.slots, 2 * KEYS), BF16),
            pltpu.VMEM((PAIRS, t, PAIR), BF16),
            pltpu.VMEM((3 * PAIRS, t, PAIR), BF16),
            pltpu.VMEM((2, z.shards, z.rows, WIDE), BF16),
            DMA,
            DMA,
            DMA((2,)),
        ],
        24 * 10**9,
    )(pos, grad, unit[0], unit[1], ctx_t, x_t, qkv, probs)


class Links:
    def __init__(self, rep_size, fsdp_size):
        self.rep_size, self.fsdp_size = rep_size, fsdp_size
        self.depth = fsdp_size // 2
        rep_at, fsdp_at = lax.axis_index("rep"), lax.axis_index("fsdp")
        self.core, self.side = rep_at % 2, (rep_at // 2) % 2
        self.row, self.level = fsdp_at % 2, fsdp_at // 2

    def permute(self, value, target):
        pairs = []
        for rep_at in range(self.rep_size):
            for fsdp_at in range(self.fsdp_size):
                to_rep, to_fsdp = target(rep_at, fsdp_at)
                pairs.append((rep_at * self.fsdp_size + fsdp_at, to_rep * self.fsdp_size + to_fsdp))
        return lax.ppermute(value, AXES, pairs)

    def other_core(self, value):
        return self.permute(value, lambda r, f: (r ^ 1, f))

    def other_side(self, value):
        return self.permute(value, lambda r, f: (r ^ 2, f))

    def other_row(self, value):
        return self.permute(value, lambda r, f: (r, f ^ 1))

    def level_up(self, value, step):
        return self.permute(value, lambda r, f: (r, ((f // 2 + step) % self.depth) * 2 + f % 2))


def own_quarter(links, columns=None, rows=None):
    if columns is not None:
        blocks = jnp.moveaxis(columns.reshape(columns.shape[0], 4, 2, HALF), 0, 2)
    else:
        blocks = jnp.moveaxis(rows.reshape(4, rows.shape[0] // 4, 2, HALF), 2, 1)
    picked = lax.dynamic_index_in_dim(blocks, links.core, 1, keepdims=False)
    return lax.dynamic_slice_in_dim(picked, links.side * 2, 2, 0)


def gather_unit(links, quarter, side_first):
    column = jnp.stack([quarter] + [links.level_up(quarter, step) for step in range(1, links.depth)])
    hops = (links.other_side, links.other_row) if side_first else (links.other_row, links.other_side)
    part = column
    for hop in hops:
        part = jnp.stack([part, hop(part)])
    return part, links.other_core(part)


def sum_unit(links, grad, side_first):
    hops = (links.other_side, links.other_row) if side_first else (links.other_row, links.other_side)
    total = full(grad[0]) + full(links.other_core(grad[1]))
    for hop in hops:
        total = total[0] + full(hop(low(total[1])))
    share = total[0]
    for step in range(1, links.depth):
        share = share + full(links.level_up(low(total[step]), links.depth - step))
    return low(share)


def sum_copies(links, share):
    if links.rep_size > 4:
        groups = [list(range(first, links.rep_size, 4)) for first in range(4)]
        share = lax.psum(share, "rep", axis_index_groups=groups)
    return share


def pair_up(own, other, at):
    return jnp.where(at == 0, jnp.stack([own, other]), jnp.stack([other, own]))


def join_quarters(links, shares):
    sides = pair_up(shares, links.other_side(shares), links.side)
    return pair_up(sides, links.other_core(sides), links.core)


def gather_small(links, shard):
    column = jnp.zeros((links.depth,) + shard.shape, shard.dtype)
    for step in range(links.depth):
        piece = shard if step == 0 else links.level_up(shard, step)
        at = (links.level - step) % links.depth
        column = lax.dynamic_update_index_in_dim(column, piece, at, 0)
    rows = pair_up(column, links.other_row(column), links.row)
    return jnp.moveaxis(rows, 0, 1).reshape((links.fsdp_size,) + shard.shape)


def sum_small(links, grad):
    total = full(low(grad)) + full(links.other_core(low(grad)))
    total = full(low(total)) + full(links.other_side(low(total)))
    parts = total.reshape((links.depth, 2) + total.shape[1:])
    total = lax.dynamic_index_in_dim(parts, links.row, 1, keepdims=False) + full(
        links.other_row(low(lax.dynamic_index_in_dim(parts, 1 - links.row, 1, keepdims=False)))
    )
    share = lax.dynamic_index_in_dim(total, links.level, 0, keepdims=False)
    for step in range(1, links.depth):
        at = (links.level + step) % links.depth
        piece = lax.dynamic_index_in_dim(total, at, 0, keepdims=False)
        share = share + full(links.level_up(low(piece), step))
    return low(share)


def join_small(bias_up, biases, gains, shard_count):
    return jnp.concatenate(
        [
            bias_up.reshape(shard_count, -1),
            jnp.moveaxis(biases.reshape(6, shard_count, -1), 1, 0).reshape(shard_count, -1),
            jnp.moveaxis(gains.reshape(2, shard_count, -1), 1, 0).reshape(shard_count, -1),
        ],
        axis=1,
    )


def split_small(joined, up_size, width):
    shard_count = joined.shape[0]
    bias_up = joined[:, :up_size].reshape(-1)
    biases = joined[:, up_size : up_size + 6 * width].reshape(shard_count, 6, width)
    gains = joined[:, up_size + 6 * width :].reshape(shard_count, 2, width)
    return (
        bias_up,
        jnp.moveaxis(biases, 0, 1).reshape(6, -1),
        jnp.moveaxis(gains, 0, 1).reshape(2, -1),
    )


SIDE_FIRST = ((False, True, False), (True, False, True))


def shards(
    rep_size, fsdp_size, hidden, region_counts, w_qkv, w_out, w_up, w_down, bias_up, biases, norm_gains, cotangent
):
    links = Links(rep_size, fsdp_size)
    z = Sizes(hidden.shape[0], region_counts.shape[0], fsdp_size, w_qkv.shape[1])
    up_size, width = bias_up.shape[1], biases.shape[2]
    pos = jnp.stack([links.core, links.side, links.row, links.level]).astype(jnp.int32)
    small = jnp.concatenate(
        [join_small(bias_up[l], biases[l], norm_gains[l], 1) for l in range(LAYERS)], axis=1
    )[0]
    small = gather_small(links, small).reshape(fsdp_size, LAYERS, -1)
    units, params = [], []
    for layer in range(LAYERS):
        sides = SIDE_FIRST[layer]
        first_part = jnp.concatenate([w_qkv[layer], w_out[layer]], axis=1)
        units.append(
            (
                gather_unit(links, own_quarter(links, columns=first_part), sides[0]),
                gather_unit(links, own_quarter(links, columns=w_up[layer]), sides[1]),
                gather_unit(links, own_quarter(links, rows=w_down[layer]), sides[2]),
            )
        )
        up_bias, rows, gains = (full(v) for v in split_small(small[:, layer], up_size, width))
        params.append((up_bias[None], rows[:, None], gains[:, None]))
    states = hidden
    kept = []
    for layer in range(LAYERS):
        sides = SIDE_FIRST[layer]
        first_unit, up, down = units[layer]
        up_bias, rows, gains = params[layer]
        qkv_bias = jnp.concatenate([rows[0], jnp.zeros_like(rows[0]), rows[1]], axis=1)
        first, hat_one, scale_one, x_t, ctx_t, first_t, qkv, probs = run_attention_forward(
            z, pos, region_counts, states, first_unit, sides[0], qkv_bias, rows[2], gains[0], rows[3]
        )
        states, hat_two, scale_two, act_t, slope = run_mlp_forward(
            z, pos, first, up, sides[1], down, sides[2], up_bias, rows[4], gains[1], rows[5]
        )
        kept.append((hat_one, scale_one, x_t, ctx_t, first_t, qkv, probs, hat_two, scale_two, act_t, slope))
    output = low(states)
    gradient = cotangent
    weight_grads = [None] * LAYERS
    small_grads = [None] * LAYERS
    for layer in reversed(range(LAYERS)):
        sides = SIDE_FIRST[layer]
        first_unit, up, down = units[layer]
        up_bias, rows, gains = params[layer]
        hat_one, scale_one, x_t, ctx_t, first_t, qkv, probs, hat_two, scale_two, act_t, slope = kept[layer]
        second, gain_two, shift_two, down_bias, down_grad = run_down_backward(
            z, pos, gradient, hat_two, scale_two, gains[1], act_t, sides[2]
        )
        first_in, gain_one, shift_one, out_bias, up_bias_grad, up_grad = run_up_backward(
            z, pos, second, up, sides[1], down, sides[2], slope, first_t, hat_one, scale_one, gains[0], sides[1]
        )
        gradient, qkv_sums, first_grad = run_attention_backward(
            z, pos, first_in, first_unit, sides[0], ctx_t, x_t, qkv, probs, sides[0]
        )
        shares = jnp.stack(
            [
                sum_unit(links, grad, side)
                for grad, side in ((first_grad, sides[0]), (up_grad, sides[1]), (down_grad, sides[2]))
            ]
        )
        weight_grads[layer] = full(join_quarters(links, sum_copies(links, shares)))
        bias_grads = jnp.concatenate(
            [qkv_sums[:, :WIDE], qkv_sums[:, 2 * WIDE :], out_bias, shift_one, down_bias, shift_two]
        )
        gain_grads = jnp.concatenate([gain_one, gain_two])
        small_sum = sum_small(links, join_small(up_bias_grad[0], bias_grads, gain_grads, fsdp_size))
        small_grads[layer] = full(sum_copies(links, small_sum))
    grads = jnp.stack(weight_grads)
    by_columns = jnp.transpose(grads[:, :, :, :2], (0, 3, 5, 2, 4, 1, 6)).reshape(LAYERS, 2, z.rows, 4 * WIDE)
    by_rows = jnp.transpose(grads[:, :, :, 2], (0, 2, 3, 4, 1, 5)).reshape(LAYERS, 4 * z.rows, WIDE)
    small = [split_small(value[None], up_size, width) for value in small_grads]
    return (
        output,
        gradient,
        by_columns[:, 0, :, : 3 * WIDE],
        by_columns[:, 0, :, 3 * WIDE :],
        by_columns[:, 1],
        by_rows,
    ) + tuple(jnp.stack([small[layer][member] for layer in range(LAYERS)]) for member in range(3))


def solution(mesh):
    in_specs = (
        P(("rep", "fsdp"), None),
        P(("rep", "fsdp")),
        P(None, "fsdp", None),
        P(None, "fsdp", None),
        P(None, "fsdp", None),
        P(None, "fsdp", None),
        P(None, "fsdp"),
        P(None, None, "fsdp"),
        P(None, None, "fsdp"),
        P(("rep", "fsdp"), None),
    )
    out_specs = (
        P(("rep", "fsdp"), None),
        P(("rep", "fsdp"), None),
        P(None, "fsdp", None),
        P(None, "fsdp", None),
        P(None, "fsdp", None),
        P(None, "fsdp", None),
        P(None, "fsdp"),
        P(None, None, "fsdp"),
        P(None, None, "fsdp"),
    )
    local = functools.partial(shards, mesh.shape["rep"], mesh.shape["fsdp"])
    return jax.shard_map(local, mesh=mesh, in_specs=in_specs, out_specs=out_specs, check_vma=False)
```

time: 1720 us -> 677 us (0.39)
  waiting for transfers between devices: 1020 us -> 175 us
  matrix products: 232 us -> 0 us
  blocking collectives: 224 us -> 0 us
  Pallas kernels: 0 us -> 194 us
  starting transfers between devices: 0.86 us -> 135 us
  local copies, waits for them, and re-layouts: 157 us -> 83.8 us
  other arithmetic: 59.5 us -> 77.3 us
    reduce_scatter x6 -> x0, waiting for transfers between devices: 527 us -> none  [the longest x2 197 us: reduce_grads(): lax.psum_scatter(local_grads[3].astype(jnp.bfloat16), 'fsdp', scatter_dim...]
    unnamed x27 -> x0, waiting for transfers between devices: 240 us -> none
    dot_general x36 -> x0, matrix products: 232 us -> none  [the longest x8 71.9 us: project(): return jnp.dot(left, right, preferred_element_type=jnp.float32)]
    pallas_call x0 -> x10, Pallas kernels: none -> 194 us  [the longest x2 48.3 us: run_attention_backward(): call(functools.partial(attention_backward, z.depth, side_first, out_side_...]
    all_gather x6 -> x0, blocking collectives: 182 us -> none  [the longest x2 64.4 us: shards(): lax.all_gather(norm_gains[layer_index], 'fsdp', axis=1, tiled=True)]
    all_gather x8 -> x0, waiting for transfers between devices: 177 us -> none  [the longest x2 63.9 us: shards(): lax.all_gather(w_up[layer_index], 'fsdp', axis=0, tiled=True)]
    ppermute x0 -> x92, waiting for transfers between devices: none -> 175 us  [permute(): return lax.ppermute(value, AXES, pairs)]
    ppermute x0 -> x92, starting transfers between devices: none -> 135 us  [permute(): return lax.ppermute(value, AXES, pairs)]
  transfers between devices with their start and end apart: 21 -> 92, of which waited for: 15 -> 34; matrix products, arithmetic and copies ran while one was open for 19% -> 19% of each run, Pallas kernels for 0% -> 24%
where the time goes in v1:
time: 677 us; the launch traced here: 668 us
  Pallas kernels  194 us (29%)
  waiting for transfers between devices  175 us (26%)
  starting transfers between devices  135 us (20%)
  local copies, waits for them, and re-layouts  83.8 us (12%)
  other arithmetic  77.3 us (11%)
    ppermute x92, waiting for transfers between devices, permute(): return lax.ppermute(value, AXES, pairs)  175 us
    ppermute x92, starting transfers between devices, permute(): return lax.ppermute(value, AXES, pairs)  135 us
    pallas_call x2, Pallas kernels, run_attention_backward(): call(functools.partial(attention_backward, z.depth, side_first, out_side_...  48.3 us
    pallas_call x2, Pallas kernels, run_attention_forward(): call(functools.partial(attention_forward, z.depth, side_first, z.seqs), [...  42.1 us
    pallas_call x2, Pallas kernels, run_up_backward(): call(functools.partial(up_backward, z.depth, up_side_first, down_side_fir...  40.6 us
    pallas_call x2, Pallas kernels, run_mlp_forward(): call(functools.partial(mlp_forward, z.depth, up_side_first, down_side_fir...  39.7 us
    another operation x18, other arithmetic, gather_unit(): part = jnp.stack([part, hop(part)])  38.7 us
    pallas_call x2, Pallas kernels, run_down_backward(): call(functools.partial(down_backward, z.depth, out_side_first), [SMEM, VM...  22.8 us
  transfers between devices with their start and end apart: 92, of which 34 were waited for; matrix products, arithmetic and copies ran while one was open for 19% of the time, Pallas kernels for 24%

profile of v1, /device:TPU:0, one launch (start us, length us, event | category | flops | bytes accessed | tf_op | source)
XLA Modules:
  0.0 668.0 jit_solution(977316579752331950)
XLA Ops:
  4.6 5.0 collective-permute-start.2
  24.0 3.9 collective-permute-start.12
  34.0 3.2 collective-permute-start.18
  41.8 4.2 collective-permute-done.11
  46.1 3.8 collective-permute-start.24
  53.4 3.8 collective-permute-done.17
  67.6 3.8 collective-permute-done.23
  71.4 3.8 collective-permute-start.36
  77.4 6.6 collective-permute-done.29
  100.5 6.3 collective-permute-done.13
  114.8 4.7 collective-permute-done.25
  144.8 12.6 %collective-permute-done.20 = bf16[2,4,2,96,384]{4,3,2,1,0:T(8,128)(2,1)} collective-permute-done((bf16[2,4,2,96,384]{4,3,2,1,0:T(8,128)(2,1)}, bf16[2,4,2,96,384]{4,3,2,1,0:T(8,128)(2,1)}, u32[]{:S(2)}, u32[]{:S(2)}) %collective-permute-start.20) | collective-permute-done | bytes 1179680 | tf_op jit(solution)/shard_map/ppermute | solution.py:607
  160.6 4.6 collective-permute-done.26
  180.9 7.5 %collective-permute-done.38 = bf16[2,4,2,96,384]{4,3,2,1,0:T(8,128)(2,1)} collective-permute-done((bf16[2,4,2,96,384]{4,3,2,1,0:T(8,128)(2,1)}, bf16[2,4,2,96,384]{4,3,2,1,0:T(8,128)(2,1)}, u32[]{:S(2)}, u32[]{:S(2)}) %collective-permute-start.38) | collective-permute-done | bytes 1179680 | tf_op jit(solution)/shard_map/ppermute | solution.py:607
  190.5 21.2 %shard_map.169 = (f32[544,768]{1,0:T(8,128)}, f32[544,768]{1,0:T(8,128)}, f32[544,128]{1,0:T(8,128)}, bf16[768,544]{1,0:T(8,128)(2,1)}, bf16[768,544]{1,0:T(8,12...) custom-call(s32[4]{0:T(128)} %pad_add_fusion.pos_ref, ...), custom_call_target="tpu_custom_call" | custom-call | flops 12000000000 | bytes 1048576 | tf_op jit(solution)/shard_map/pallas_call | solution.py:467
  211.8 19.8 %shard_map.170 = (f32[544,768]{1,0:T(8,128)}, f32[544,768]{1,0:T(8,128)}, f32[544,128]{1,0:T(8,128)}, bf16[4,768,544]{2,1,0:T(8,128)(2,1)}, bf16[4,544,768]{2,1,0:T(8,128)(2,1)}) custom-call(s32[4]{0:T(128)} %pad_add_fusion.pos_ref, f32[544,768]{1,0:T(8,128)} %get-tuple-element.63.first_ref, bf16[2,2,4,2,96,384]{5,4,3,2,1,0:T(8,128)(2,1)} %pad_maximum_fusion.1.up_own_ref, ...), custom_call_target="tpu_custom_call" | custom-call | flops 16000000000 | bytes 1048576 | tf_op jit(solution)/shard_map/pallas_call | solution.py:493
  231.6 20.9 %shard_map.171 = (f32[544,768]{1,0:T(8,128)}, f32[544,768]{1,0:T(8,128)}, f32[544,128]{1,0:T(8,128)}, bf16[768,544]{1,0:T(8,128)(2,1)}, bf16[768,544]{1,0:T(8,12...) custom-call(s32[4]{0:T(128)} %pad_add_fusion.pos_ref, ...), custom_call_target="tpu_custom_call" | custom-call | flops 12000000000 | bytes 1048576 | tf_op jit(solution)/shard_map/pallas_call | solution.py:467
  252.6 19.9 %shard_map.172 = (f32[544,768]{1,0:T(8,128)}, f32[544,768]{1,0:T(8,128)}, f32[544,128]{1,0:T(8,128)}, bf16[4,768,544]{2,1,0:T(8,128)(2,1)}, bf16[4,544,768]{2,1,0:T(8,128)(2,1)}) custom-call(s32[4]{0:T(128)} %pad_add_fusion.pos_ref, f32[544,768]{1,0:T(8,128)} %get-tuple-element.65.first_ref, bf16[2,2,4,2,96,384]{5,4,3,2,1,0:T(8,128)(2,1)} %pad_maximum_fusion.4.up_own_ref, ...), custom_call_target="tpu_custom_call" | custom-call | flops 16000000000 | bytes 1048576 | tf_op jit(solution)/shard_map/pallas_call | solution.py:493
  272.5 11.3 %shard_map.173 = (f32[544,768]{1,0:T(8,128)}, f32[1,768]{1,0:T(1,128)}, f32[1,768]{1,0:T(1,128)}, f32[1,768]{1,0:T(1,128)}, bf16[2,2,2,4,2,96,384]{6,5,4,3,2,1,0:T(8,128)(2,1)}) custom-call(s32[4]{0:T(128)} %pad_add_fusion.pos_ref, bf16[544,768]{1,0:T(8,128)(2,1)} %grad_ref.1, f32[544,768]{1,0:T(8,128)} %get-tuple-element.67.hat_ref, ...), custom_call_target="tpu_custom_call" | custom-call | flops 8000000000 | bytes 1048576 | tf_op jit(solution)/shard_map/pallas_call | solution.py:521
  286.3 20.3 %shard_map.174 = (f32[544,768]{1,0:T(8,128)}, f32[1,768]{1,0:T(1,128)}, f32[1,768]{1,0:T(1,128)}, f32[1,768]{1,0:T(1,128)}, f32[1,3072]{1,0:T(1,128)}, /*index=5*/bf16[2,2,2,4,2,96,384]{6,5,4,3,2,1,0:T(8,128)(2,1)}) custom-call(s32[4]{0:T(128)} %pad_add_fusion.pos_ref, f32[544,768]{1,0:T(8,128)} %get-tuple-element.70.second_ref, ...), custom_call_target="tpu_custom_call" | custom-call | flops 20000000000 | bytes 1048576 | tf_op jit(solution)/shard_map/pallas_call | solution.py:543
  306.6 3.3 slice_bitcast_fusion.9
  309.9 24.3 %shard_map.175 = (f32[544,768]{1,0:T(8,128)}, f32[1,2304]{1,0:T(1,128)}, bf16[2,2,2,4,2,96,384]{6,5,4,3,2,1,0:T(8,128)(2,1)}) custom-call(s32[4]{0:T(128)} %pad_add_fusion.pos_ref, f32[544,768]{1,0:T(8,128)} %get-tuple-element.75.grad_ref, bf16[2,2,4,2,96,384]{5,4,3,2,1,0:T(8,128)(2,1)} %pad_maximum_fusion.3.own_ref, ...), custom_call_target="tpu_custom_call" | custom-call | flops 24000000000 | bytes 1048576 | tf_op jit(solution)/shard_map/pallas_call | solution.py:571
  334.2 3.3 slice_bitcast_fusion.10
  338.0 11.5 %shard_map.176 = (f32[544,768]{1,0:T(8,128)}, f32[1,768]{1,0:T(1,128)}, f32[1,768]{1,0:T(1,128)}, f32[1,768]{1,0:T(1,128)}, bf16[2,2,2,4,2,96,384]{6,5,4,3,2,1,0:T(8,128)(2,1)}) custom-call(s32[4]{0:T(128)} %pad_add_fusion.pos_ref, f32[544,768]{1,0:T(8,128)} %get-tuple-element.80.grad_ref, f32[544,768]{1,0:T(8,128)} %get-tuple-element.81.hat_ref, ...), custom_call_target="tpu_custom_call" | custom-call | flops 8000000000 | bytes 1048576 | tf_op jit(solution)/shard_map/pallas_call | solution.py:521
  349.6 3.4 slice_bitcast_fusion.11
  353.0 20.3 %shard_map.177 = (f32[544,768]{1,0:T(8,128)}, f32[1,768]{1,0:T(1,128)}, f32[1,768]{1,0:T(1,128)}, f32[1,768]{1,0:T(1,128)}, f32[1,3072]{1,0:T(1,128)}, /*index=5*/bf16[2,2,2,4,2,96,384]{6,5,4,3,2,1,0:T(8,128)(2,1)}) custom-call(s32[4]{0:T(128)} %pad_add_fusion.pos_ref, f32[544,768]{1,0:T(8,128)} %get-tuple-element.84.second_ref, ...), custom_call_target="tpu_custom_call" | custom-call | flops 20000000000 | bytes 1048576 | tf_op jit(solution)/shard_map/pallas_call | solution.py:543
  373.4 3.4 slice_bitcast_fusion.12
  377.6 24.1 %shard_map.178 = (f32[544,768]{1,0:T(8,128)}, f32[1,2304]{1,0:T(1,128)}, bf16[2,2,2,4,2,96,384]{6,5,4,3,2,1,0:T(8,128)(2,1)}) custom-call(s32[4]{0:T(128)} %pad_add_fusion.pos_ref, f32[544,768]{1,0:T(8,128)} %get-tuple-element.89.grad_ref, bf16[2,2,4,2,96,384]{5,4,3,2,1,0:T(8,128)(2,1)} %pad_maximum_fusion.own_ref, ...), custom_call_target="tpu_custom_call" | custom-call | flops 24000000000 | bytes 1048576 | tf_op jit(solution)/shard_map/pallas_call | solution.py:571
  419.8 3.5 slice_bitcast_fusion.13
  456.4 10.0 %collective-permute-done.73 = bf16[2,4,2,96,384]{4,3,2,1,0:T(8,128)(2,1)} collective-permute-done((bf16[2,4,2,96,384]{4,3,2,1,0:T(8,128)(2,1)S(1)}, bf16[2,4,2,96,384]{4,3,2,1,0:T(8,128)(2,1)}, u32[]{:S(2)}, u32[]{:S(2)}) %collective-permute-start.73) | collective-permute-done | bytes 1179680 | tf_op jit(solution)/shard_map/ppermute | solution.py:607
  473.9 17.7 %collective-permute-done.61 = bf16[2,4,2,96,384]{4,3,2,1,0:T(8,128)(2,1)} collective-permute-done((bf16[2,4,2,96,384]{4,3,2,1,0:T(8,128)(2,1)}, bf16[2,4,2,96,384]{4,3,2,1,0:T(8,128)(2,1)}, u32[]{:S(2)}, u32[]{:S(2)}) %collective-permute-start.61) | collective-permute-done | bytes 1179680 | tf_op jit(solution)/shard_map/ppermute | solution.py:607
  499.2 17.7 %collective-permute-done.47 = bf16[2,4,2,96,384]{4,3,2,1,0:T(8,128)(2,1)} collective-permute-done((bf16[2,4,2,96,384]{4,3,2,1,0:T(8,128)(2,1)}, bf16[2,4,2,96,384]{4,3,2,1,0:T(8,128)(2,1)}, u32[]{:S(2)}, u32[]{:S(2)}) %collective-permute-start.47) | collective-permute-done | bytes 1179680 | tf_op jit(solution)/shard_map/ppermute | solution.py:607
  523.1 11.6 %collective-permute-done.74 = bf16[4,2,96,384]{3,2,1,0:T(8,128)(2,1)S(1)} collective-permute-done((bf16[4,2,96,384]{3,2,1,0:T(8,128)(2,1)S(1)}, bf16[4,2,96,384]{3,2,1,0:T(8,128)(2,1)S(1)}, u32[]{:S(2)}, u32[]{:S(2)}) %collective-permute-start.74) | collective-permute-done | bytes 589856 | tf_op jit(solution)/shard_map/ppermute | solution.py:607
  535.8 11.5 %collective-permute-done.62 = bf16[4,2,96,384]{3,2,1,0:T(8,128)(2,1)S(1)} collective-permute-done((bf16[4,2,96,384]{3,2,1,0:T(8,128)(2,1)S(1)}, bf16[4,2,96,384]{3,2,1,0:T(8,128)(2,1)S(1)}, u32[]{:S(2)}, u32[]{:S(2)}) %collective-permute-start.62) | collective-permute-done | bytes 589856 | tf_op jit(solution)/shard_map/ppermute | solution.py:607
  548.9 9.8 %collective-permute-done.48 = bf16[4,2,96,384]{3,2,1,0:T(8,128)(2,1)S(1)} collective-permute-done((bf16[4,2,96,384]{3,2,1,0:T(8,128)(2,1)S(1)}, bf16[4,2,96,384]{3,2,1,0:T(8,128)(2,1)S(1)}, u32[]{:S(2)}, u32[]{:S(2)}) %collective-permute-start.48) | collective-permute-done | bytes 589856 | tf_op jit(solution)/shard_map/ppermute | solution.py:607
  559.6 3.6 collective-permute-start.69
  568.3 7.7 %collective-permute-done.70 = bf16[2,96,384]{2,1,0:T(8,128)(2,1)S(1)} collective-permute-done((bf16[2,96,384]{2,1,0:T(8,128)(2,1)S(1)}, bf16[2,96,384]{2,1,0:T(8,128)(2,1)S(1)}, u32[]{:S(2)}, u32[]{:S(2)}) %collective-permute-start.70) | collective-permute-done | bytes 147488 | tf_op jit(solution)/shard_map/ppermute | solution.py:607
  576.1 6.1 collective-permute-start.56
  582.3 6.7 %collective-permute-start.55 = (bf16[2,96,384]{2,1,0:T(8,128)(2,1)S(1)}, bf16[2,96,384]{2,1,0:T(8,128)(2,1)S(1)}, u32[]{:S(2)}, u32[]{:S(2)}) collective-permute-start(bf16[2,96,384]{2,1,0:T(8,128)(2,1)S(1)} %get-tuple-element.195), channel_id=1, source_target_pairs={{0,6},{1,7},{2,0},{3,1},{4,2},{5,3},{6,4},{7,5},{8,14},{9,15},{10,... | collective-permute-start | bytes 442376 | tf_op jit(solution)/shard_map/ppermute | solution.py:607
  589.6 5.0 collective-permute-start.50
  594.6 7.0 %collective-permute-start.49 = (bf16[2,96,384]{2,1,0:T(8,128)(2,1)S(1)}, bf16[2,96,384]{2,1,0:T(8,128)(2,1)S(1)}, u32[]{:S(2)}, u32[]{:S(2)}) collective-permute-start(bf16[2,96,384]{2,1,0:T(8,128)(2,1)S(1)} %get-tuple-element.192), channel_id=1, source_target_pairs={{0,6},{1,7},{2,0},{3,1},{4,2},{5,3},{6,4},{7,5},{8,14},{9,15},{10,... | collective-permute-start | bytes 442376 | tf_op jit(solution)/shard_map/ppermute | solution.py:607
  602.2 5.0 collective-permute-start.44
  607.4 7.2 %collective-permute-start.43 = (bf16[2,96,384]{2,1,0:T(8,128)(2,1)S(1)}, bf16[2,96,384]{2,1,0:T(8,128)(2,1)S(1)}, u32[]{:S(2)}, u32[]{:S(2)}) collective-permute-start(bf16[2,96,384]{2,1,0:T(8,128)(2,1)S(1)} %get-tuple-element.189), channel_id=1, source_target_pairs={{0,6},{1,7},{2,0},{3,1},{4,2},{5,3},{6,4},{7,5},{8,14},{9,15},{10,... | collective-permute-start | bytes 442376 | tf_op jit(solution)/shard_map/ppermute | solution.py:607
  615.3 7.0 %collective-permute-done.44 = bf16[2,96,384]{2,1,0:T(8,128)(2,1)S(1)} collective-permute-done((bf16[2,96,384]{2,1,0:T(8,128)(2,1)S(1)}, bf16[2,96,384]{2,1,0:T(8,128)(2,1)S(1)}, u32[]{:S(2)}, u32[]{:S(2)}) %collective-permute-start.44) | collective-permute-done | bytes 147488 | tf_op jit(solution)/shard_map/ppermute | solution.py:607
  626.9 7.6 %collective-permute-done.58 = bf16[3,2,96,384]{3,2,1,0:T(8,128)(2,1)S(1)} collective-permute-done((bf16[3,2,96,384]{3,2,1,0:T(8,128)(2,1)}, bf16[3,2,96,384]{3,2,1,0:T(8,128)(2,1)S(1)}, u32[]{:S(2)}, u32[]{:S(2)}) %collective-permute-start.58) | collective-permute-done | bytes 442400 | tf_op jit(solution)/shard_map/ppermute | solution.py:607
  642.0 5.8 copy.44
  647.8 7.0 %reshape.592 = f32[2,2,96,3072]{3,2,1,0:T(8,128)} reshape(f32[2,2,96,2,2,2,384]{6,5,4,3,2,1,0:T(2,128)} %copy.44) | data formatting | bytes 9437184 | tf_op jit(solution)/shard_map/reshape | solution.py:788
  659.5 3.3 slice_bitcast_fusion.1
  (502 shorter events, 223.3 us)
Async XLA Ops:
  4.6 28.8 %collective-permute-start.2 = (bf16[2,96,384]{2,1,0:T(8,128)(2,1)}, bf16[2,96,384]{2,1,0:T(8,128)(2,1)}, u32[]{:S(2)}, u32[]{:S(2)}) collective-permute-start(bf16[2,96,384]{2,1,0:T(8,128)(2,1)} %bitcast.359.clone.2), channel_id=1, source_target_pairs={{0,6},{1,7},{2,0},{3,1},{4,2},{5,3},{6,4},{7,5},{8,14},{9,15},{10,... | collective-permute-start | bytes 442376 | tf_op jit(solution)/shard_map/ppermute | solution.py:607
  9.6 24.4 %collective-permute-start.1 = (bf16[2,96,384]{2,1,0:T(8,128)(2,1)}, bf16[2,96,384]{2,1,0:T(8,128)(2,1)}, u32[]{:S(2)}, u32[]{:S(2)}) collective-permute-start(bf16[2,96,384]{2,1,0:T(8,128)(2,1)} %bitcast.359.clone.2), channel_id=1, source_target_pairs={{0,4},{1,5},{2,6},{3,7},{4,0},{5,1},{6,2},{7,3},{8,12},{9,13},{10,... | collective-permute-start | bytes 442376 | tf_op jit(solution)/shard_map/ppermute | solution.py:607
  38.4 20.2 %collective-permute-start.3 = (bf16[4,2,96,384]{3,2,1,0:T(8,128)(2,1)S(1)}, bf16[4,2,96,384]{3,2,1,0:T(8,128)(2,1)S(1)}, u32[]{:S(2)}, u32[]{:S(2)}) collective-permute-start(bf16[4,2,96,384]{3,2,1,0:T(8,128)(2,1)S(1)} %get-tuple-element.218), channel_id=1, source_target_pairs={{0,1},{1,0},{2,3},{3,2},{4,5},{5,4},{6,7},{7,6},{8,9},{9,8},{10,11... | collective-permute-start | bytes 1769480 | tf_op jit(solution)/shard_map/ppermute | solution.py:607
  50.5 20.8 %collective-permute-start.23 = (bf16[2,96,384]{2,1,0:T(8,128)(2,1)S(1)}, bf16[2,96,384]{2,1,0:T(8,128)(2,1)S(1)}, u32[]{:S(2)}, u32[]{:S(2)}) collective-permute-start(bf16[2,96,384]{2,1,0:T(8,128)(2,1)S(1)} %bitcast.437), channel_id=1, source_target_pairs={{0,4},{1,5},{2,6},{3,7},{4,0},{5,1},{6,2},{7,3},{8,12},{9,13},{10,... | collective-permute-start | bytes 442376 | tf_op jit(solution)/shard_map/ppermute | solution.py:607
  62.7 21.3 %collective-permute-start.29 = (bf16[2,96,384]{2,1,0:T(8,128)(2,1)S(1)}, bf16[2,96,384]{2,1,0:T(8,128)(2,1)S(1)}, u32[]{:S(2)}, u32[]{:S(2)}) collective-permute-start(bf16[2,96,384]{2,1,0:T(8,128)(2,1)S(1)} %bitcast.433), channel_id=1, source_target_pairs={{0,4},{1,5},{2,6},{3,7},{4,0},{5,1},{6,2},{7,3},{8,12},{9,13},{10,... | collective-permute-start | bytes 442376 | tf_op jit(solution)/shard_map/ppermute | solution.py:607
  65.0 58.3 %collective-permute-start.4 = (bf16[2,4,2,96,384]{4,3,2,1,0:T(8,128)(2,1)}, bf16[2,4,2,96,384]{4,3,2,1,0:T(8,128)(2,1)}, u32[]{:S(2)}, u32[]{:S(2)}) collective-permute-start(bf16[2,4,2,96,384]{4,3,2,1,0:T(8,128)(2,1)} %get-tuple-element.186), channel_id=1, source_target_pairs={{0,16},{1,17},{2,18},{3,19},{4,20},{5,21},{6,22},{7,23},{8,24},{9,... | collective-permute-start | bytes 3538952 | tf_op jit(solution)/shard_map/ppermute | solution.py:607
  84.0 22.9 %collective-permute-start.13 = (bf16[4,2,96,384]{3,2,1,0:T(8,128)(2,1)S(1)}, bf16[4,2,96,384]{3,2,1,0:T(8,128)(2,1)}, u32[]{:S(2)}, u32[]{:S(2)}) collective-permute-start(bf16[4,2,96,384]{3,2,1,0:T(8,128)(2,1)S(1)} %get-tuple-element.216), channel_id=1, source_target_pairs={{0,16},{1,17},{2,18},{3,19},{4,20},{5,21},{6,22},{7,23},{8,24},{9,... | collective-permute-start | bytes 1769480 | tf_op jit(solution)/shard_map/ppermute | solution.py:607
  87.3 23.4 %collective-permute-start.19 = (bf16[4,2,96,384]{3,2,1,0:T(8,128)(2,1)}, bf16[4,2,96,384]{3,2,1,0:T(8,128)(2,1)}, u32[]{:S(2)}, u32[]{:S(2)}) collective-permute-start(bf16[4,2,96,384]{3,2,1,0:T(8,128)(2,1)} %get-tuple-element.214), channel_id=1, source_target_pairs={{0,1},{1,0},{2,3},{3,2},{4,5},{5,4},{6,7},{7,6},{8,9},{9,8},{10,11... | collective-permute-start | bytes 1769480 | tf_op jit(solution)/shard_map/ppermute | solution.py:607
  91.1 28.4 %collective-permute-start.25 = (bf16[4,2,96,384]{3,2,1,0:T(8,128)(2,1)}, bf16[4,2,96,384]{3,2,1,0:T(8,128)(2,1)}, u32[]{:S(2)}, u32[]{:S(2)}) collective-permute-start(bf16[4,2,96,384]{3,2,1,0:T(8,128)(2,1)} %get-tuple-element.212), channel_id=1, source_target_pairs={{0,16},{1,17},{2,18},{3,19},{4,20},{5,21},{6,22},{7,23},{8,24},{9,... | collective-permute-start | bytes 1769480 | tf_op jit(solution)/shard_map/ppermute | solution.py:607
  96.9 30.9 %collective-permute-start.31 = (bf16[4,2,96,384]{3,2,1,0:T(8,128)(2,1)S(1)}, bf16[4,2,96,384]{3,2,1,0:T(8,128)(2,1)}, u32[]{:S(2)}, u32[]{:S(2)}) collective-permute-start(bf16[4,2,96,384]{3,2,1,0:T(8,128)(2,1)S(1)} %get-tuple-element.210), channel_id=1, source_target_pairs={{0,1},{1,0},{2,3},{3,2},{4,5},{5,4},{6,7},{7,6},{8,9},{9,8},{10,11... | collective-permute-start | bytes 1769480 | tf_op jit(solution)/shard_map/ppermute | solution.py:607
  106.9 31.0 %collective-permute-start.37 = (bf16[4,2,96,384]{3,2,1,0:T(8,128)(2,1)}, bf16[4,2,96,384]{3,2,1,0:T(8,128)(2,1)}, u32[]{:S(2)}, u32[]{:S(2)}) collective-permute-start(bf16[4,2,96,384]{3,2,1,0:T(8,128)(2,1)} %get-tuple-element.208), channel_id=1, source_target_pairs={{0,16},{1,17},{2,18},{3,19},{4,20},{5,21},{6,22},{7,23},{8,24},{9,... | collective-permute-start | bytes 1769480 | tf_op jit(solution)/shard_map/ppermute | solution.py:607
  110.6 30.6 %collective-permute-start.14 = (bf16[2,4,2,96,384]{4,3,2,1,0:T(8,128)(2,1)}, bf16[2,4,2,96,384]{4,3,2,1,0:T(8,128)(2,1)}, u32[]{:S(2)}, u32[]{:S(2)}) collective-permute-start(bf16[2,4,2,96,384]{4,3,2,1,0:T(8,128)(2,1)} %get-tuple-element.184), channel_id=1, source_target_pairs={{0,1},{1,0},{2,3},{3,2},{4,5},{5,4},{6,7},{7,6},{8,9},{9,8},{10,11... | collective-permute-start | bytes 3538952 | tf_op jit(solution)/shard_map/ppermute | solution.py:607
  119.5 37.9 %collective-permute-start.20 = (bf16[2,4,2,96,384]{4,3,2,1,0:T(8,128)(2,1)}, bf16[2,4,2,96,384]{4,3,2,1,0:T(8,128)(2,1)}, u32[]{:S(2)}, u32[]{:S(2)}) collective-permute-start(bf16[2,4,2,96,384]{4,3,2,1,0:T(8,128)(2,1)} %get-tuple-element.182), channel_id=1, source_target_pairs={{0,16},{1,17},{2,18},{3,19},{4,20},{5,21},{6,22},{7,23},{8,24},{9,... | collective-permute-start | bytes 3538952 | tf_op jit(solution)/shard_map/ppermute | solution.py:607
  123.3 41.9 %collective-permute-start.26 = (bf16[2,4,2,96,384]{4,3,2,1,0:T(8,128)(2,1)}, bf16[2,4,2,96,384]{4,3,2,1,0:T(8,128)(2,1)}, u32[]{:S(2)}, u32[]{:S(2)}) collective-permute-start(bf16[2,4,2,96,384]{4,3,2,1,0:T(8,128)(2,1)} %get-tuple-element.180), channel_id=1, source_target_pairs={{0,1},{1,0},{2,3},{3,2},{4,5},{5,4},{6,7},{7,6},{8,9},{9,8},{10,11... | collective-permute-start | bytes 3538952 | tf_op jit(solution)/shard_map/ppermute | solution.py:607
  127.8 62.2 %collective-permute-start.5 = (bf16[2,2,4,2,96,384]{5,4,3,2,1,0:T(8,128)(2,1)}, bf16[2,2,4,2,96,384]{5,4,3,2,1,0:T(8,128)(2,1)}, u32[]{:S(2)}, u32[]{:S(2)}) collective-permute-start(bf16[2,2,4,2,96,384]{5,4,3,2,1,0:T(8,128)(2,1)} %pad_maximum_fusion.own_ref), channel_id=1, source_target_pairs={{0,8},{1,9},{2,10},{3,11},{4,12},{5,13},{6,14},{7,15},{8,0},{9,1},... | collective-permute-start | bytes 7077896 | tf_op jit(solution)/shard_map/ppermute | solution.py:607
  137.9 39.6 %collective-permute-start.32 = (bf16[2,4,2,96,384]{4,3,2,1,0:T(8,128)(2,1)}, bf16[2,4,2,96,384]{4,3,2,1,0:T(8,128)(2,1)}, u32[]{:S(2)}, u32[]{:S(2)}) collective-permute-start(bf16[2,4,2,96,384]{4,3,2,1,0:T(8,128)(2,1)} %get-tuple-element.176), channel_id=1, source_target_pairs={{0,16},{1,17},{2,18},{3,19},{4,20},{5,21},{6,22},{7,23},{8,24},{9,... | collective-permute-start | bytes 3538952 | tf_op jit(solution)/shard_map/ppermute | solution.py:607
  141.3 47.1 %collective-permute-start.38 = (bf16[2,4,2,96,384]{4,3,2,1,0:T(8,128)(2,1)}, bf16[2,4,2,96,384]{4,3,2,1,0:T(8,128)(2,1)}, u32[]{:S(2)}, u32[]{:S(2)}) collective-permute-start(bf16[2,4,2,96,384]{4,3,2,1,0:T(8,128)(2,1)} %get-tuple-element.172), channel_id=1, source_target_pairs={{0,1},{1,0},{2,3},{3,2},{4,5},{5,4},{6,7},{7,6},{8,9},{9,8},{10,11... | collective-permute-start | bytes 3538952 | tf_op jit(solution)/shard_map/ppermute | solution.py:607
  157.4 54.4 %collective-permute-start.15 = (bf16[2,2,4,2,96,384]{5,4,3,2,1,0:T(8,128)(2,1)}, bf16[2,2,4,2,96,384]{5,4,3,2,1,0:T(8,128)(2,1)}, u32[]{:S(2)}, u32[]{:S(2)}) collective-permute-start(bf16[2,2,4,2,96,384]{5,4,3,2,1,0:T(8,128)(2,1)} %pad_maximum_fusion.1.up_own_ref), channel_id=1, source_target_pairs={{0,8},{1,9},{2,10},{3,11},{4,12},{5,13},{6,14},{7,15},{8,0},{9,1},... | collective-permute-start | bytes 7077896 | tf_op jit(solution)/shard_map/ppermute | solution.py:607
  165.1 46.6 %collective-permute-start.21 = (bf16[2,2,4,2,96,384]{5,4,3,2,1,0:T(8,128)(2,1)}, bf16[2,2,4,2,96,384]{5,4,3,2,1,0:T(8,128)(2,1)}, u32[]{:S(2)}, u32[]{:S(2)}) collective-permute-start(bf16[2,2,4,2,96,384]{5,4,3,2,1,0:T(8,128)(2,1)} %pad_maximum_fusion.2.down_own_ref), channel_id=1, source_target_pairs={{0,8},{1,9},{2,10},{3,11},{4,12},{5,13},{6,14},{7,15},{8,0},{9,1},... | collective-permute-start | bytes 7077896 | tf_op jit(solution)/shard_map/ppermute | solution.py:607
  177.5 54.1 %collective-permute-start.27 = (bf16[2,2,4,2,96,384]{5,4,3,2,1,0:T(8,128)(2,1)}, bf16[2,2,4,2,96,384]{5,4,3,2,1,0:T(8,128)(2,1)}, u32[]{:S(2)}, u32[]{:S(2)}) collective-permute-start(bf16[2,2,4,2,96,384]{5,4,3,2,1,0:T(8,128)(2,1)} %pad_maximum_fusion.3.own_ref), channel_id=1, source_target_pairs={{0,8},{1,9},{2,10},{3,11},{4,12},{5,13},{6,14},{7,15},{8,0},{9,1},... | collective-permute-start | bytes 7077896 | tf_op jit(solution)/shard_map/ppermute | solution.py:607
  188.4 64.2 %collective-permute-start.33 = (bf16[2,2,4,2,96,384]{5,4,3,2,1,0:T(8,128)(2,1)}, bf16[2,2,4,2,96,384]{5,4,3,2,1,0:T(8,128)(2,1)}, u32[]{:S(2)}, u32[]{:S(2)}) collective-permute-start(bf16[2,2,4,2,96,384]{5,4,3,2,1,0:T(8,128)(2,1)} %pad_maximum_fusion.4.up_own_ref), channel_id=1, source_target_pairs={{0,8},{1,9},{2,10},{3,11},{4,12},{5,13},{6,14},{7,15},{8,0},{9,1},... | collective-permute-start | bytes 7077896 | tf_op jit(solution)/shard_map/ppermute | solution.py:607
  190.0 62.6 %collective-permute-start.39 = (bf16[2,2,4,2,96,384]{5,4,3,2,1,0:T(8,128)(2,1)S(1)}, bf16[2,2,4,2,96,384]{5,4,3,2,1,0:T(8,128)(2,1)}, u32[]{:S(2)}, u32[]{:S(2)}) collective-permute-start(bf16[2,2,4,2,96,384]{5,4,3,2,1,0:T(8,128)(2,1)S(1)} %pad_maximum_fusion.5.down_own_ref), channel_id=1, source_target_pairs={{0,8},{1,9},{2,10},{3,11},{4,12},{5,13},{6,14},{7,15},{8,0},{9,1},... | collective-permute-start | bytes 7077896 | tf_op jit(solution)/shard_map/ppermute | solution.py:607
  285.7 147.7 %collective-permute-start.72 = (bf16[2,2,4,2,96,384]{5,4,3,2,1,0:T(8,128)(2,1)S(1)}, bf16[2,2,4,2,96,384]{5,4,3,2,1,0:T(8,128)(2,1)}, u32[]{:S(2)}, u32[]{:S(2)}) collective-permute-start(bf16[2,2,4,2,96,384]{5,4,3,2,1,0:T(8,128)(2,1)S(1)} %slice_bitcast_fusion.8), channel_id=1, source_target_pairs={{0,8},{1,9},{2,10},{3,11},{4,12},{5,13},{6,14},{7,15},{8,0},{9,1},... | collective-permute-start | bytes 7077896 | tf_op jit(solution)/shard_map/ppermute | solution.py:607
  309.9 127.5 %collective-permute-start.66 = (bf16[2,2,4,2,96,384]{5,4,3,2,1,0:T(8,128)(2,1)}, bf16[2,2,4,2,96,384]{5,4,3,2,1,0:T(8,128)(2,1)}, u32[]{:S(2)}, u32[]{:S(2)}) collective-permute-start(bf16[2,2,4,2,96,384]{5,4,3,2,1,0:T(8,128)(2,1)} %slice_bitcast_fusion.9), channel_id=1, source_target_pairs={{0,8},{1,9},{2,10},{3,11},{4,12},{5,13},{6,14},{7,15},{8,0},{9,1},... | collective-permute-start | bytes 7077896 | tf_op jit(solution)/shard_map/ppermute | solution.py:607
  337.5 104.9 %collective-permute-start.60 = (bf16[2,2,4,2,96,384]{5,4,3,2,1,0:T(8,128)(2,1)}, bf16[2,2,4,2,96,384]{5,4,3,2,1,0:T(8,128)(2,1)}, u32[]{:S(2)}, u32[]{:S(2)}) collective-permute-start(bf16[2,2,4,2,96,384]{5,4,3,2,1,0:T(8,128)(2,1)} %slice_bitcast_fusion.10), channel_id=1, source_target_pairs={{0,8},{1,9},{2,10},{3,11},{4,12},{5,13},{6,14},{7,15},{8,0},{9,1},... | collective-permute-start | bytes 7077896 | tf_op jit(solution)/shard_map/ppermute | solution.py:607
  377.5 26.1 %collective-permute-start.86 = (bf16[8,1152]{1,0:T(8,128)(2,1)S(1)}, bf16[8,1152]{1,0:T(8,128)(2,1)S(1)}, u32[]{:S(2)}, u32[]{:S(2)}) collective-permute-start(bf16[8,1152]{1,0:T(8,128)(2,1)S(1)} %concatenate.141), channel_id=1, source_target_pairs={{0,8},{1,9},{2,10},{3,11},{4,12},{5,13},{6,14},{7,15},{8,0},{9,1},... | collective-permute-start | bytes 55304 | tf_op jit(solution)/shard_map/ppermute | solution.py:607
  433.4 20.7 %collective-permute-start.40 = (bf16[2,2,4,2,96,384]{5,4,3,2,1,0:T(8,128)(2,1)}, bf16[2,2,4,2,96,384]{5,4,3,2,1,0:T(8,128)(2,1)S(1)}, u32[]{:S(2)}, u32[]{:S(2)}) collective-permute-start(bf16[2,2,4,2,96,384]{5,4,3,2,1,0:T(8,128)(2,1)} %slice_bitcast_fusion.13), channel_id=1, source_target_pairs={{0,8},{1,9},{2,10},{3,11},{4,12},{5,13},{6,14},{7,15},{8,0},{9,1},... | collective-permute-start | bytes 7077896 | tf_op jit(solution)/shard_map/ppermute | solution.py:607
  437.4 29.0 %collective-permute-start.73 = (bf16[2,4,2,96,384]{4,3,2,1,0:T(8,128)(2,1)S(1)}, bf16[2,4,2,96,384]{4,3,2,1,0:T(8,128)(2,1)}, u32[]{:S(2)}, u32[]{:S(2)}) collective-permute-start(bf16[2,4,2,96,384]{4,3,2,1,0:T(8,128)(2,1)S(1)} %fusion.11), channel_id=1, source_target_pairs={{0,16},{1,17},{2,18},{3,19},{4,20},{5,21},{6,22},{7,23},{8,24},{9,... | collective-permute-start | bytes 3538952 | tf_op jit(solution)/shard_map/ppermute | solution.py:607
  442.5 29.2 %collective-permute-start.67 = (bf16[2,4,2,96,384]{4,3,2,1,0:T(8,128)(2,1)}, bf16[2,4,2,96,384]{4,3,2,1,0:T(8,128)(2,1)}, u32[]{:S(2)}, u32[]{:S(2)}) collective-permute-start(bf16[2,4,2,96,384]{4,3,2,1,0:T(8,128)(2,1)} %fusion.10), channel_id=1, source_target_pairs={{0,1},{1,0},{2,3},{3,2},{4,5},{5,4},{6,7},{7,6},{8,9},{9,8},{10,11... | collective-permute-start | bytes 3538952 | tf_op jit(solution)/shard_map/ppermute | solution.py:607
  446.7 44.9 %collective-permute-start.61 = (bf16[2,4,2,96,384]{4,3,2,1,0:T(8,128)(2,1)}, bf16[2,4,2,96,384]{4,3,2,1,0:T(8,128)(2,1)}, u32[]{:S(2)}, u32[]{:S(2)}) collective-permute-start(bf16[2,4,2,96,384]{4,3,2,1,0:T(8,128)(2,1)} %fusion.9), channel_id=1, source_target_pairs={{0,16},{1,17},{2,18},{3,19},{4,20},{5,21},{6,22},{7,23},{8,24},{9,... | collective-permute-start | bytes 3538952 | tf_op jit(solution)/shard_map/ppermute | solution.py:607
  449.9 47.0 %collective-permute-start.53 = (bf16[2,4,2,96,384]{4,3,2,1,0:T(8,128)(2,1)}, bf16[2,4,2,96,384]{4,3,2,1,0:T(8,128)(2,1)}, u32[]{:S(2)}, u32[]{:S(2)}) collective-permute-start(bf16[2,4,2,96,384]{4,3,2,1,0:T(8,128)(2,1)} %fusion.8), channel_id=1, source_target_pairs={{0,1},{1,0},{2,3},{3,2},{4,5},{5,4},{6,7},{7,6},{8,9},{9,8},{10,11... | collective-permute-start | bytes 3538952 | tf_op jit(solution)/shard_map/ppermute | solution.py:607
  454.1 62.8 %collective-permute-start.47 = (bf16[2,4,2,96,384]{4,3,2,1,0:T(8,128)(2,1)}, bf16[2,4,2,96,384]{4,3,2,1,0:T(8,128)(2,1)}, u32[]{:S(2)}, u32[]{:S(2)}) collective-permute-start(bf16[2,4,2,96,384]{4,3,2,1,0:T(8,128)(2,1)} %fusion.7), channel_id=1, source_target_pairs={{0,16},{1,17},{2,18},{3,19},{4,20},{5,21},{6,22},{7,23},{8,24},{9,... | collective-permute-start | bytes 3538952 | tf_op jit(solution)/shard_map/ppermute | solution.py:607
  466.4 55.7 %collective-permute-start.41 = (bf16[2,4,2,96,384]{4,3,2,1,0:T(8,128)(2,1)S(1)}, bf16[2,4,2,96,384]{4,3,2,1,0:T(8,128)(2,1)S(1)}, u32[]{:S(2)}, u32[]{:S(2)}) collective-permute-start(bf16[2,4,2,96,384]{4,3,2,1,0:T(8,128)(2,1)S(1)} %fusion.6), channel_id=1, source_target_pairs={{0,1},{1,0},{2,3},{3,2},{4,5},{5,4},{6,7},{7,6},{8,9},{9,8},{10,11... | collective-permute-start | bytes 3538952 | tf_op jit(solution)/shard_map/ppermute | solution.py:607
  471.7 63.1 %collective-permute-start.74 = (bf16[4,2,96,384]{3,2,1,0:T(8,128)(2,1)S(1)}, bf16[4,2,96,384]{3,2,1,0:T(8,128)(2,1)S(1)}, u32[]{:S(2)}, u32[]{:S(2)}) collective-permute-start(bf16[4,2,96,384]{3,2,1,0:T(8,128)(2,1)S(1)} %fusion.25), channel_id=1, source_target_pairs={{0,1},{1,0},{2,3},{3,2},{4,5},{5,4},{6,7},{7,6},{8,9},{9,8},{10,11... | collective-permute-start | bytes 1769480 | tf_op jit(solution)/shard_map/ppermute | solution.py:607
  491.7 43.9 %collective-permute-start.68 = (bf16[4,2,96,384]{3,2,1,0:T(8,128)(2,1)S(1)}, bf16[4,2,96,384]{3,2,1,0:T(8,128)(2,1)S(1)}, u32[]{:S(2)}, u32[]{:S(2)}) collective-permute-start(bf16[4,2,96,384]{3,2,1,0:T(8,128)(2,1)S(1)} %fusion.24), channel_id=1, source_target_pairs={{0,16},{1,17},{2,18},{3,19},{4,20},{5,21},{6,22},{7,23},{8,24},{9,... | collective-permute-start | bytes 1769480 | tf_op jit(solution)/shard_map/ppermute | solution.py:607
  496.9 50.5 %collective-permute-start.62 = (bf16[4,2,96,384]{3,2,1,0:T(8,128)(2,1)S(1)}, bf16[4,2,96,384]{3,2,1,0:T(8,128)(2,1)S(1)}, u32[]{:S(2)}, u32[]{:S(2)}) collective-permute-start(bf16[4,2,96,384]{3,2,1,0:T(8,128)(2,1)S(1)} %fusion.23), channel_id=1, source_target_pairs={{0,1},{1,0},{2,3},{3,2},{4,5},{5,4},{6,7},{7,6},{8,9},{9,8},{10,11... | collective-permute-start | bytes 1769480 | tf_op jit(solution)/shard_map/ppermute | solution.py:607
  517.0 30.7 %collective-permute-start.54 = (bf16[4,2,96,384]{3,2,1,0:T(8,128)(2,1)S(1)}, bf16[4,2,96,384]{3,2,1,0:T(8,128)(2,1)S(1)}, u32[]{:S(2)}, u32[]{:S(2)}) collective-permute-start(bf16[4,2,96,384]{3,2,1,0:T(8,128)(2,1)S(1)} %fusion.22), channel_id=1, source_target_pairs={{0,16},{1,17},{2,18},{3,19},{4,20},{5,21},{6,22},{7,23},{8,24},{9,... | collective-permute-start | bytes 1769480 | tf_op jit(solution)/shard_map/ppermute | solution.py:607
  522.1 36.7 %collective-permute-start.48 = (bf16[4,2,96,384]{3,2,1,0:T(8,128)(2,1)S(1)}, bf16[4,2,96,384]{3,2,1,0:T(8,128)(2,1)S(1)}, u32[]{:S(2)}, u32[]{:S(2)}) collective-permute-start(bf16[4,2,96,384]{3,2,1,0:T(8,128)(2,1)S(1)} %fusion.21), channel_id=1, source_target_pairs={{0,1},{1,0},{2,3},{3,2},{4,5},{5,4},{6,7},{7,6},{8,9},{9,8},{10,11... | collective-permute-start | bytes 1769480 | tf_op jit(solution)/shard_map/ppermute | solution.py:607
  534.7 24.3 %collective-permute-start.42 = (bf16[4,2,96,384]{3,2,1,0:T(8,128)(2,1)S(1)}, bf16[4,2,96,384]{3,2,1,0:T(8,128)(2,1)S(1)}, u32[]{:S(2)}, u32[]{:S(2)}) collective-permute-start(bf16[4,2,96,384]{3,2,1,0:T(8,128)(2,1)S(1)} %fusion.20), channel_id=1, source_target_pairs={{0,16},{1,17},{2,18},{3,19},{4,20},{5,21},{6,22},{7,23},{8,24},{9,... | collective-permute-start | bytes 1769480 | tf_op jit(solution)/shard_map/ppermute | solution.py:607
  535.6 24.1 %collective-permute-start.77 = (bf16[2,96,384]{2,1,0:T(8,128)(2,1)S(1)}, bf16[2,96,384]{2,1,0:T(8,128)(2,1)S(1)}, u32[]{:S(2)}, u32[]{:S(2)}) collective-permute-start(bf16[2,96,384]{2,1,0:T(8,128)(2,1)S(1)} %get-tuple-element.205), channel_id=1, source_target_pairs={{0,2},{1,3},{2,4},{3,5},{4,6},{5,7},{6,0},{7,1},{8,10},{9,11},{10,... | collective-permute-start | bytes 442376 | tf_op jit(solution)/shard_map/ppermute | solution.py:607
  563.2 19.0 %collective-permute-start.65 = (bf16[2,96,384]{2,1,0:T(8,128)(2,1)S(1)}, bf16[2,96,384]{2,1,0:T(8,128)(2,1)S(1)}, u32[]{:S(2)}, u32[]{:S(2)}) collective-permute-start(bf16[2,96,384]{2,1,0:T(8,128)(2,1)S(1)} %get-tuple-element.199), channel_id=1, source_target_pairs={{0,2},{1,3},{2,4},{3,5},{4,6},{5,7},{6,0},{7,1},{8,10},{9,11},{10,... | collective-permute-start | bytes 442376 | tf_op jit(solution)/shard_map/ppermute | solution.py:607
  563.9 25.2 %collective-permute-start.64 = (bf16[2,96,384]{2,1,0:T(8,128)(2,1)S(1)}, bf16[2,96,384]{2,1,0:T(8,128)(2,1)S(1)}, u32[]{:S(2)}, u32[]{:S(2)}) collective-permute-start(bf16[2,96,384]{2,1,0:T(8,128)(2,1)S(1)} %get-tuple-element.200), channel_id=1, source_target_pairs={{0,4},{1,5},{2,6},{3,7},{4,0},{5,1},{6,2},{7,3},{8,12},{9,13},{10,... | collective-permute-start | bytes 442376 | tf_op jit(solution)/shard_map/ppermute | solution.py:607
  567.4 22.2 %collective-permute-start.63 = (bf16[2,96,384]{2,1,0:T(8,128)(2,1)S(1)}, bf16[2,96,384]{2,1,0:T(8,128)(2,1)S(1)}, u32[]{:S(2)}, u32[]{:S(2)}) collective-permute-start(bf16[2,96,384]{2,1,0:T(8,128)(2,1)S(1)} %get-tuple-element.198), channel_id=1, source_target_pairs={{0,6},{1,7},{2,0},{3,1},{4,2},{5,3},{6,4},{7,5},{8,14},{9,15},{10,... | collective-permute-start | bytes 442376 | tf_op jit(solution)/shard_map/ppermute | solution.py:607
  576.1 25.7 %collective-permute-start.56 = (bf16[2,96,384]{2,1,0:T(8,128)(2,1)S(1)}, bf16[2,96,384]{2,1,0:T(8,128)(2,1)S(1)}, u32[]{:S(2)}, u32[]{:S(2)}) collective-permute-start(bf16[2,96,384]{2,1,0:T(8,128)(2,1)S(1)} %get-tuple-element.197), channel_id=1, source_target_pairs={{0,4},{1,5},{2,6},{3,7},{4,0},{5,1},{6,2},{7,3},{8,12},{9,13},{10,... | collective-permute-start | bytes 442376 | tf_op jit(solution)/shard_map/ppermute | solution.py:607
  582.3 20.0 %collective-permute-start.55 = (bf16[2,96,384]{2,1,0:T(8,128)(2,1)S(1)}, bf16[2,96,384]{2,1,0:T(8,128)(2,1)S(1)}, u32[]{:S(2)}, u32[]{:S(2)}) collective-permute-start(bf16[2,96,384]{2,1,0:T(8,128)(2,1)S(1)} %get-tuple-element.195), channel_id=1, source_target_pairs={{0,6},{1,7},{2,0},{3,1},{4,2},{5,3},{6,4},{7,5},{8,14},{9,15},{10,... | collective-permute-start | bytes 442376 | tf_op jit(solution)/shard_map/ppermute | solution.py:607
  589.6 25.1 %collective-permute-start.50 = (bf16[2,96,384]{2,1,0:T(8,128)(2,1)S(1)}, bf16[2,96,384]{2,1,0:T(8,128)(2,1)S(1)}, u32[]{:S(2)}, u32[]{:S(2)}) collective-permute-start(bf16[2,96,384]{2,1,0:T(8,128)(2,1)S(1)} %get-tuple-element.194), channel_id=1, source_target_pairs={{0,4},{1,5},{2,6},{3,7},{4,0},{5,1},{6,2},{7,3},{8,12},{9,13},{10,... | collective-permute-start | bytes 442376 | tf_op jit(solution)/shard_map/ppermute | solution.py:607
  594.6 20.6 %collective-permute-start.49 = (bf16[2,96,384]{2,1,0:T(8,128)(2,1)S(1)}, bf16[2,96,384]{2,1,0:T(8,128)(2,1)S(1)}, u32[]{:S(2)}, u32[]{:S(2)}) collective-permute-start(bf16[2,96,384]{2,1,0:T(8,128)(2,1)S(1)} %get-tuple-element.192), channel_id=1, source_target_pairs={{0,6},{1,7},{2,0},{3,1},{4,2},{5,3},{6,4},{7,5},{8,14},{9,15},{10,... | collective-permute-start | bytes 442376 | tf_op jit(solution)/shard_map/ppermute | solution.py:607
  602.2 20.1 %collective-permute-start.44 = (bf16[2,96,384]{2,1,0:T(8,128)(2,1)S(1)}, bf16[2,96,384]{2,1,0:T(8,128)(2,1)S(1)}, u32[]{:S(2)}, u32[]{:S(2)}) collective-permute-start(bf16[2,96,384]{2,1,0:T(8,128)(2,1)S(1)} %get-tuple-element.191), channel_id=1, source_target_pairs={{0,4},{1,5},{2,6},{3,7},{4,0},{5,1},{6,2},{7,3},{8,12},{9,13},{10,... | collective-permute-start | bytes 442376 | tf_op jit(solution)/shard_map/ppermute | solution.py:607
  (101 other events, 1172.0 us)

commit v2 on v1

v2 whole, which is shorter than its diff:
```python
import functools

import jax
import jax.numpy as jnp
from jax import lax
from jax.experimental import pallas as pl
from jax.experimental.pallas import tpu as pltpu
from jax.sharding import PartitionSpec as P

HEADS = 12
HEAD_DIM = 64
LAYERS = 2
TEXT = 128
KEYS = 256
WIDE = 768
HALF = WIDE // 2
PAIR = 2 * HEAD_DIM
PAIRS = HEADS // 2
EPSILON = 1e-12
MASKED = -1000000000.0
AXES = ("rep", "fsdp")
COST = 1.15e9
SMALL = 16
VMEM_LIMIT = 63 * 1024 * 1024
SMALL_LIMIT = 14 * 1024 * 1024


def low(value):
    return value.astype(jnp.bfloat16)


def full(value):
    return value.astype(jnp.float32)


def mm(left, right):
    return jnp.dot(left, right, preferred_element_type=jnp.float32)


def mm_t(left, right):
    return lax.dot_general(
        left, right, (((1,), (1,)), ((), ())), preferred_element_type=jnp.float32
    )


def t_mm(left, right):
    return lax.dot_general(
        left, right, (((0,), (0,)), ((), ())), preferred_element_type=jnp.float32
    )


def flip(at, by):
    return 1 - at if by else at


class Place:
    def __init__(self, pos_ref):
        self.core, self.side = pos_ref[0], pos_ref[1]
        self.row, self.level = pos_ref[2], pos_ref[3]

    def shard(self, level, far_row):
        return level * 2 + flip(self.row, far_row)


def half_lanes(at):
    return pl.ds(pl.multiple_of(at * HALF, HALF), HALF)


def part_of(arrays, path, far_core, far_side, far_row):
    last, first = (far_side, far_row) if path == 0 else (far_row, far_side)
    return arrays[path * 4 + far_core * 2 + last], first


def load_unit(place, depth, arrays, unit, whole, sem, by_rows):
    rows = pl.ds(0, whole.shape[2])
    for path in range(2):
        for far_core in range(2):
            lanes = half_lanes(flip(place.core, far_core))
            for far_side in range(2):
                block = flip(place.side, far_side) * 2 + path
                for far_row in range(2):
                    array, first = part_of(arrays, path, far_core, far_side, far_row)
                    for level in range(depth):
                        shard = place.shard(level, far_row)
                        at = (shard, block) if by_rows else (block, shard)
                        target = whole.at[at[0], at[1], :, lanes]
                        pltpu.make_async_copy(array.at[first, level, unit, rows], target, sem).start()


def load_block(place, depth, block, arrays, whole, sem):
    path = block % 2
    rows = pl.ds(0, whole.shape[1])
    needed_side = place.side if block // 2 == 0 else 1 - place.side
    for far_core in range(2):
        lanes = half_lanes(flip(place.core, far_core))
        for far_row in range(2):
            for far_side in range(2):

                @pl.when(needed_side == far_side)
                def _():
                    array, first = part_of(arrays, path, far_core, far_side, far_row)
                    for level in range(depth):
                        target = whole.at[place.shard(level, far_row), :, lanes]
                        pltpu.make_async_copy(array.at[first, level, 0, rows], target, sem).start()


def wait_all(ref, sem):
    pltpu.make_async_copy(ref, ref, sem).wait()


def sum_place(out, block, far_row, far_side, level):
    if block % 2:
        return out.at[1, far_side, far_row, level]
    return out.at[0, far_row, far_side, level]


def store_columns(place, block, held, outs, sem):
    rows = pl.ds(0, held.shape[1])
    far_side = place.side if block // 2 == 0 else 1 - place.side
    for far_core, out in enumerate(outs):
        core = flip(place.core, far_core)
        for far_row in range(2):
            for level in range(held.shape[0] // 2):
                source = held.at[place.shard(level, far_row), :, half_lanes(core)]
                target = sum_place(out, block, far_row, far_side, level).at[rows]
                pltpu.make_async_copy(source, target, sem).start()


def store_rows(place, tile, held, outs, sem):
    count = held.shape[0]
    for inner in range(count):
        shard = tile * count + inner
        far_row = place.row if shard % 2 == 0 else 1 - place.row
        for block in range(4):
            far_side = place.side if block // 2 == 0 else 1 - place.side
            for far_core, out in enumerate(outs):
                source = held.at[inner, block, :, half_lanes(flip(place.core, far_core))]
                target = sum_place(out, block, far_row, far_side, shard // 2)
                pltpu.make_async_copy(source, target, sem).start()


def chunks(rows):
    size = rows // 4 if rows % 64 == 0 or (rows // 4) % 8 == 0 else rows
    return [(start, size) for start in range(0, rows, size)]


def normalize(value):
    centered = value - jnp.mean(value, axis=-1, keepdims=True)
    scale = lax.rsqrt(jnp.mean(centered * centered, axis=-1, keepdims=True) + EPSILON)
    return centered * scale, scale


def norm_backward(grad, hat, scale, gain):
    direct = grad * gain
    return (
        direct
        - jnp.mean(direct, axis=-1, keepdims=True)
        - hat * jnp.mean(direct * hat, axis=-1, keepdims=True)
    ) * scale


def gelu_and_slope(value):
    size = jnp.abs(value) * 0.7071067811865476
    t = 1.0 / (1.0 + 0.3275911 * size)
    series = t * (
        0.127414796
        + t * (-0.142248368 + t * (0.7107068705 + t * (-0.7265760135 + t * 0.5307027145)))
    )
    bell = jnp.exp(-0.5 * value * value)
    tail = series * bell
    below = jnp.where(value >= 0, 1.0 - tail, tail)
    return value * below, below + value * bell * 0.3989422804014327


def attention_forward(
    depth, seqs, extra, pos_ref, counts_ref, x_ref, params_ref,
    *refs,
):
    parts, refs = refs[:8], refs[8 + extra :]
    first_ref, hat_ref, scale_ref, x_t_ref, ctx_t_ref, first_t_ref, qkv_ref, probs_ref = refs[:8]
    weight, ctx, held, weight_sem, held_sem = refs[8:]
    place = Place(pos_ref)
    load_unit(place, depth, parts, 0, weight, weight_sem, False)
    tokens = x_ref.shape[0]
    slots = tokens // seqs
    x_low = low(x_ref[...])
    x_t_ref[...] = x_low.T
    wait_all(weight, weight_sem)
    for block in range(3):
        out = mm(x_low, weight[block].reshape(WIDE, WIDE))
        if block != 1:
            out = out + params_ref[1 + block // 2 : 2 + block // 2, :WIDE]
        out = low(out)
        for pair in range(PAIRS):
            qkv_ref[block * PAIRS + pair] = out[:, pair * PAIR : (pair + 1) * PAIR]
    lane = lax.broadcasted_iota(jnp.int32, (KEYS, PAIR), 1)
    key = lax.broadcasted_iota(jnp.int32, (slots, KEYS), 1)
    for seq in range(seqs):
        valid = key < TEXT + counts_ref[seq]

        def pair_step(pair, carry, seq=seq, valid=valid):
            start = seq * slots
            slot = lax.rem(pair, 2)
            q = qkv_ref[pair, start : start + slots, :] * jnp.bfloat16(HEAD_DIM**-0.5)
            k = qkv_ref[PAIRS + pair, start : start + KEYS, :]
            v = qkv_ref[2 * PAIRS + pair, start : start + KEYS, :]
            none = jnp.zeros_like(k)
            k_both = jnp.concatenate(
                [jnp.where(lane < HEAD_DIM, k, none), jnp.where(lane < HEAD_DIM, none, k)], 0
            )
            v_both = jnp.concatenate(
                [jnp.where(lane < HEAD_DIM, v, none), jnp.where(lane < HEAD_DIM, none, v)], 0
            )
            scores = mm_t(q, k_both)
            halves = []
            for half in range(2):
                part = jnp.where(valid, scores[:, half * KEYS : (half + 1) * KEYS], MASKED)
                part = jnp.exp(part - jnp.max(part, axis=-1, keepdims=True))
                halves.append(low(part / jnp.sum(part, axis=-1, keepdims=True)))
            probs = jnp.concatenate(halves, 1)

            @pl.when(pair >= 2)
            def _():
                wait_all(held.at[slot], held_sem.at[slot])

            held[slot] = probs
            pltpu.make_async_copy(
                held.at[slot], probs_ref.at[seq, pair], held_sem.at[slot]
            ).start()
            ctx[pair, start : start + slots, :] = low(mm(probs, v_both))
            return carry

        lax.fori_loop(0, PAIRS, pair_step, 0)
        for slot in range(2):
            wait_all(held.at[slot], held_sem.at[slot])
    context = jnp.concatenate([ctx[pair] for pair in range(PAIRS)], 1)
    ctx_t_ref[...] = context.T
    first_ref[...] = mm(context, weight[3].reshape(WIDE, WIDE))
    for start, size in chunks(tokens):
        rows = pl.ds(start, size)
        hat, scale = normalize(full(x_ref[rows, :]) + (first_ref[rows, :] + params_ref[3:4, :WIDE]))
        hat_ref[rows, :] = hat
        scale_ref[rows, :] = jnp.broadcast_to(scale, (size, 128))
        first_ref[rows, :] = hat * params_ref[7:8, :WIDE] + params_ref[4:5, :WIDE]
    first_t_ref[...] = low(first_ref[...]).T


def mlp_forward(
    depth, extra, pos_ref, first_ref, params_ref,
    *refs,
):
    parts, refs = refs[:8], refs[8 + extra :]
    out_ref, hat_ref, scale_ref, act_t_ref, slope_ref = refs[:5]
    up, down, pre, act, act_t, slope, up_sem, down_sem, act_sem, slope_sem = refs[5:]
    place = Place(pos_ref)
    load_unit(place, depth, parts, 0, up, up_sem, False)
    load_unit(place, depth, parts, 1, down, down_sem, True)
    tokens = first_ref.shape[0]
    first_low = low(first_ref[...])
    shards = down.shape[0] // 4
    wait_all(up, up_sem)
    total = None
    for tile in range(4):
        slot = tile % 2
        pre[...] = mm(first_low, up[tile].reshape(WIDE, WIDE))
        if tile >= 2:
            wait_all(slope.at[slot], slope_sem.at[slot])
            wait_all(act_t.at[slot], act_sem.at[slot])

        def row_step(step, carry, tile=tile, slot=slot):
            rows = pl.ds(pl.multiple_of(step * 32, 32), 32)
            value = pre[rows, :] + params_ref[0:1, tile * WIDE : (tile + 1) * WIDE]
            gelu, rise = gelu_and_slope(value)
            act[rows, :] = low(gelu)
            slope[slot, rows, :] = low(rise)
            return carry

        lax.fori_loop(0, tokens // 32, row_step, 0)
        pltpu.make_async_copy(slope.at[slot], slope_ref.at[tile], slope_sem.at[slot]).start()
        act_t[slot] = act[...].T
        pltpu.make_async_copy(act_t.at[slot], act_t_ref.at[tile], act_sem.at[slot]).start()
        if tile == 0:
            wait_all(down, down_sem)
        part = mm(act[...], down[tile * shards : (tile + 1) * shards].reshape(WIDE, WIDE))
        if tile == 0:
            out_ref[...] = part
        else:
            out_ref[...] += part
    for start, size in chunks(tokens):
        rows = pl.ds(start, size)
        hat, scale = normalize(first_ref[rows, :] + out_ref[rows, :] + params_ref[5:6, :WIDE])
        hat_ref[rows, :] = hat
        scale_ref[rows, :] = jnp.broadcast_to(scale, (size, 128))
        out_ref[rows, :] = hat * params_ref[8:9, :WIDE] + params_ref[6:7, :WIDE]
    for slot in range(2):
        wait_all(slope.at[slot], slope_sem.at[slot])
        wait_all(act_t.at[slot], act_sem.at[slot])


def norm_step(grad_ref, hat_ref, scale_ref, gain, out_ref, sums_ref):
    sums = [0.0, 0.0, 0.0]
    for start, size in chunks(grad_ref.shape[0]):
        rows = pl.ds(start, size)
        grad, hat = full(grad_ref[rows, :]), hat_ref[rows, :]
        grad_in = norm_backward(grad, hat, scale_ref[rows, :][:, :1], gain)
        out_ref[rows, :] = grad_in
        for at, value in enumerate((grad * hat, grad, full(low(grad_in)))):
            sums[at] += jnp.sum(value, axis=0, keepdims=True)
    sums_ref[...] = jnp.zeros_like(sums_ref)
    for at in range(3):
        sums_ref[at : at + 1, :] = sums[at]


def down_backward(
    depth, extra, pos_ref, grad_ref, hat_ref, scale_ref, params_ref, act_t_ref, *refs,
):
    second_ref, sums_ref, near_ref, far_ref = refs[extra : extra + 4]
    act_t, held, act_sem, held_sem = refs[extra + 4 :]
    place = Place(pos_ref)
    pltpu.make_async_copy(act_t_ref, act_t, act_sem).start()
    norm_step(grad_ref, hat_ref, scale_ref, params_ref[8:9, :WIDE], second_ref, sums_ref)
    grad_low = low(second_ref[...])
    wait_all(act_t, act_sem)
    for tile in range(4):
        slot = tile % 2
        if tile >= 2:
            wait_all(held.at[slot], held_sem.at[slot])
        held[slot] = low(mm(act_t[tile], grad_low)).reshape(held.shape[1:])
        store_rows(place, tile, held.at[slot], (near_ref, far_ref), held_sem.at[slot])
    for slot in range(2):
        wait_all(held.at[slot], held_sem.at[slot])


def up_backward(
    depth, extra, pos_ref, second_ref, slope_ref, first_t_ref, hat_ref, scale_ref, params_ref, *refs,
):
    parts, refs = refs[:8], refs[8 + extra :]
    first_in_ref, sums_ref, up_grad_ref, near_ref, far_ref = refs[:5]
    up, down, slope, total, held, up_sem, down_sem, slope_sem, held_sem = refs[5:]
    place = Place(pos_ref)
    load_unit(place, depth, parts, 1, down, down_sem, True)
    load_unit(place, depth, parts, 0, up, up_sem, False)
    pltpu.make_async_copy(slope_ref, slope, slope_sem).start()
    shards = down.shape[0] // 4
    grad_low = low(second_ref[...])
    first_t = first_t_ref[...]
    total[...] = second_ref[...]
    wait_all(down, down_sem)
    wait_all(slope, slope_sem)
    wait_all(up, up_sem)
    for tile in range(4):
        slot = tile % 2
        grad = mm_t(grad_low, down[tile * shards : (tile + 1) * shards].reshape(WIDE, WIDE))
        grad = low(grad * full(slope[tile]))
        up_grad_ref[:, tile * WIDE : (tile + 1) * WIDE] = jnp.sum(
            full(grad), axis=0, keepdims=True
        )
        if tile >= 2:
            wait_all(held.at[slot], held_sem.at[slot])
        held[slot] = low(mm(first_t, grad)).reshape(held.shape[1:])
        store_columns(place, tile, held.at[slot], (near_ref, far_ref), held_sem.at[slot])
        total[...] += mm_t(grad, up[tile].reshape(WIDE, WIDE))
    norm_step(total, hat_ref, scale_ref, params_ref[7:8, :WIDE], first_in_ref, sums_ref)
    for slot in range(2):
        wait_all(held.at[slot], held_sem.at[slot])


def attention_backward(
    depth, seqs, extra, pos_ref, grad_ref, qkv_ref, probs_ref, *refs,
):
    parts, refs = refs[:8], refs[8 + extra :]
    grads_ref = refs[0]
    weight, probs, ctx_grad, weight_sem, probs_sem = refs[1:]
    place = Place(pos_ref)
    load_block(place, depth, 3, parts, weight, weight_sem)
    pltpu.make_async_copy(probs_ref, probs, probs_sem).start()
    tokens = grad_ref.shape[0]
    slots = tokens // seqs
    grad_low = low(grad_ref[...])
    wait_all(weight, weight_sem)
    from_out = low(mm_t(grad_low, weight[...].reshape(WIDE, WIDE)))
    for pair in range(PAIRS):
        ctx_grad[pair] = from_out[:, pair * PAIR : (pair + 1) * PAIR]
    wait_all(probs, probs_sem)
    lane = lax.broadcasted_iota(jnp.int32, (KEYS, PAIR), 1)
    for seq in range(seqs):

        def pair_step(pair, carry, seq=seq):
            start = seq * slots
            q = qkv_ref[pair, start : start + slots, :]
            k = qkv_ref[PAIRS + pair, start : start + KEYS, :]
            v = qkv_ref[2 * PAIRS + pair, start : start + KEYS, :]
            out_grad = ctx_grad[pair, start : start + slots, :]
            none = jnp.zeros_like(k)
            k_both = jnp.concatenate(
                [jnp.where(lane < HEAD_DIM, k, none), jnp.where(lane < HEAD_DIM, none, k)], 0
            )
            v_both = jnp.concatenate(
                [jnp.where(lane < HEAD_DIM, v, none), jnp.where(lane < HEAD_DIM, none, v)], 0
            )
            weights = probs[seq, pair]
            probs_grad = mm_t(out_grad, v_both)
            halves = []
            for half in range(2):
                lanes = slice(half * KEYS, (half + 1) * KEYS)
                weight_part, grad_part = full(weights[:, lanes]), probs_grad[:, lanes]
                dot = jnp.sum(weight_part * grad_part, axis=-1, keepdims=True)
                halves.append(low(weight_part * (grad_part - dot)))
            scores_grad = jnp.concatenate(halves, 1)
            q_grad = mm(scores_grad, k_both) * HEAD_DIM**-0.5
            grads_ref[pair, start : start + slots, :] = low(q_grad)
            k_grad = t_mm(q, scores_grad) * HEAD_DIM**-0.5
            v_grad = t_mm(out_grad, weights)
            for at, value in ((PAIRS, k_grad), (2 * PAIRS, v_grad)):
                value = jnp.concatenate(
                    [value[:HEAD_DIM, :KEYS], value[HEAD_DIM:, KEYS:]], 0
                )
                grads_ref[at + pair, start : start + KEYS, :] = low(value.T)
                grads_ref[at + pair, start + KEYS : start + slots, :] = jnp.zeros(
                    (slots - KEYS, PAIR), jnp.bfloat16
                )
            return carry

        lax.fori_loop(0, PAIRS, pair_step, 0)


def qkv_weights(
    depth, up_size, width, extra, pos_ref, grad_ref, grads_ref, ctx_t_ref, x_t_ref, down_sums_ref, up_sums_ref, up_bias_ref, *refs,
):
    near_ref, far_ref = refs[extra : extra + 2]
    held, sums, block_rows, small, held_sem, small_sem = refs[extra + 2 :]
    place = Place(pos_ref)
    outs = (near_ref, far_ref)
    x_t = x_t_ref[...]
    for block in range(3):
        slot = block % 2
        grad = jnp.concatenate([grads_ref[block * PAIRS + pair] for pair in range(PAIRS)], 1)
        if block != 1:
            sums[1 + block // 2 : 2 + block // 2, :] = jnp.sum(full(grad), axis=0, keepdims=True)
        if block >= 2:
            wait_all(held.at[slot], held_sem.at[slot])
        held[slot] = low(mm(x_t, grad)).reshape(held.shape[1:])
        store_columns(place, block, held.at[slot], outs, held_sem.at[slot])
    sums[3:4, :], sums[4:5, :], sums[7:8, :] = up_sums_ref[2:3, :], up_sums_ref[1:2, :], up_sums_ref[0:1, :]
    sums[5:6, :], sums[6:7, :], sums[8:9, :] = down_sums_ref[2:3, :], down_sums_ref[1:2, :], down_sums_ref[0:1, :]
    block_rows[...] = jnp.zeros_like(block_rows)
    for shard in range(2 * depth):
        block_rows[0:1, :up_size] = up_bias_ref[:, shard * up_size : (shard + 1) * up_size]
        block_rows[1:9, :width] = sums[1:9, shard * width : (shard + 1) * width]
        small[shard] = low(block_rows[...])
    rows = held.shape[2]
    for out in outs:
        for far_row in range(2):
            for far_side in range(2):
                for level in range(depth):
                    source = small.at[place.shard(level, far_row)]
                    for path in range(2):
                        target = sum_place(out, path, far_row, far_side, level).at[pl.ds(rows, SMALL)]
                        pltpu.make_async_copy(source, target, small_sem).start()
    wait_all(held.at[1], held_sem.at[1])
    held[1] = low(mm(ctx_t_ref[...], low(grad_ref[...]))).reshape(held.shape[1:])
    store_columns(place, 3, held.at[1], outs, held_sem.at[1])
    for slot in range(2):
        wait_all(held.at[slot], held_sem.at[slot])
    for _ in range(8):
        wait_all(small, small_sem)


def qkv_backward(depth, extra, pos_ref, grad_ref, grads_ref, *refs):
    parts, refs = refs[:8], refs[8 + extra :]
    x_grad_ref, weight, weight_sem = refs
    place = Place(pos_ref)
    for block in range(3):
        load_block(place, depth, block, parts, weight.at[block], weight_sem.at[block])
    x_grad_ref[...] = grad_ref[...]
    for block in range(3):
        grad = jnp.concatenate([grads_ref[block * PAIRS + pair] for pair in range(PAIRS)], 1)
        wait_all(weight.at[block], weight_sem.at[block])
        x_grad_ref[...] += mm_t(grad, weight[block].reshape(WIDE, WIDE))


def finish_first(pos_ref, *refs):
    core, side = pos_ref[0], pos_ref[1]
    quarters, (qkv_ref, out_ref, up_bias_ref, biases_ref, gains_ref) = refs[: 4 * LAYERS], refs[4 * LAYERS :]
    rows = qkv_ref.shape[1]
    for layer in range(LAYERS):
        small = full(quarters[4 * layer][0, rows : rows + SMALL, :])
        up_bias_ref[layer : layer + 1, :] = small[0:1, : up_bias_ref.shape[1]]
        biases_ref[layer] = small[1:7, : biases_ref.shape[2]]
        gains_ref[layer] = small[7:9, : gains_ref.shape[2]]
        for far in range(4):
            part = quarters[4 * layer + far]
            at_core, at_side = flip(core, far // 2), flip(side, far % 2)
            half = at_core * HALF
            lanes = pl.ds(pl.multiple_of(at_side * (2 * WIDE) + half, HALF), HALF)
            qkv_ref[layer, :, lanes] = full(part[0, :rows, :])
            last = full(part[1, :rows, :])

            @pl.when(at_side == 0)
            def _():
                qkv_ref[layer, :, pl.ds(pl.multiple_of(WIDE + half, HALF), HALF)] = last

            @pl.when(at_side == 1)
            def _():
                out_ref[layer, :, half_lanes(at_core)] = last


def finish_second(extra, pos_ref, *refs):
    core, side = pos_ref[0], pos_ref[1]
    quarters, (up_ref, down_ref) = refs[: 4 * LAYERS], refs[4 * LAYERS + extra :]
    rows = up_ref.shape[1]
    for layer in range(LAYERS):
        for far in range(4):
            part = quarters[4 * layer + far]
            at_core, at_side = flip(core, far // 2), flip(side, far % 2)
            for block in range(2):
                lanes = pl.ds(
                    pl.multiple_of(at_side * (2 * WIDE) + block * WIDE + at_core * HALF, HALF), HALF
                )
                up_ref[layer, :, lanes] = full(part[block])
                down_rows = pl.ds(pl.multiple_of((at_side * 2 + block) * rows, rows), rows)
                down_ref[layer, down_rows, half_lanes(at_core)] = full(part[2 + block])


def prepare(
    pos_ref, qkv_ref, out_ref, up_ref, down_ref, up_bias_ref, biases_ref, gains_ref,
    first_group, second_group, third_group, rows_of, sem,
):
    core, side = pos_ref[0], pos_ref[1]
    rows = out_ref.shape[1]
    up_size, width = up_bias_ref.shape[1], biases_ref.shape[2]
    for layer in range(LAYERS):
        for block in range(2):
            at = side * 2 + block
            lanes = pl.ds(pl.multiple_of(at * WIDE + core * HALF, HALF), HALF)
            if layer == 0:
                target = first_group.at[block, 0, pl.ds(0, rows)]
                up, down = second_group.at[block, 0], second_group.at[block, 1]
            else:
                target, up, down = (third_group.at[block, unit] for unit in range(3))
            if block == 0:
                pltpu.make_async_copy(qkv_ref.at[layer, :, lanes], target, sem.at[layer, 0, 0]).start()
            else:

                @pl.when(side == 0)
                def _():
                    lanes = pl.ds(pl.multiple_of(WIDE + core * HALF, HALF), HALF)
                    pltpu.make_async_copy(qkv_ref.at[layer, :, lanes], target, sem.at[layer, 0, 1]).start()

                @pl.when(side == 1)
                def _():
                    pltpu.make_async_copy(
                        out_ref.at[layer, :, half_lanes(core)], target, sem.at[layer, 0, 1]
                    ).start()

            pltpu.make_async_copy(up_ref.at[layer, :, lanes], up, sem.at[layer, 1, block]).start()
            down_rows = pl.ds(pl.multiple_of(at * rows, rows), rows)
            pltpu.make_async_copy(
                down_ref.at[layer, down_rows, half_lanes(core)], down, sem.at[layer, 2, block]
            ).start()
    for layer in range(LAYERS):
        rows_of[...] = jnp.zeros_like(rows_of)
        rows_of[0:1, :up_size] = full(up_bias_ref[layer : layer + 1, :])
        rows_of[1:7, :width] = full(biases_ref[layer])
        rows_of[7:9, :width] = full(gains_ref[layer])
        first_group[layer, 0, rows : rows + SMALL, :] = low(rows_of[...])
    for layer in range(LAYERS):
        for block in range(2):
            for unit in range(3):
                if layer:
                    part = third_group.at[block, unit]
                elif unit:
                    part = second_group.at[block, unit - 1]
                else:
                    part = first_group.at[block, 0, pl.ds(0, rows)]
                wait_all(part, sem.at[layer, unit, block])


def columns_of(depth, pos_ref, *refs):
    level = pos_ref[3]
    for path, out in enumerate(refs[-2:]):
        for far_level, piece in enumerate(refs[:depth]):
            out[lax.rem(level + depth - far_level, depth)] = piece[path]


def split_paths(sizes, column_ref, *refs):
    start = 0
    for at, size in enumerate(sizes):
        for path in range(2):
            refs[-2 * len(sizes) + 2 * at + path][...] = column_ref[:, path, start : start + size]
        start += size


def join(*refs):
    for path, out in enumerate(refs[-2:]):
        out[0] = refs[2 * path][...]
        out[1] = refs[2 * path + 1][...]


def add_up(counts, stacked, *refs):
    start = 0
    for at, count in enumerate(counts):
        total = full(refs[start][...])
        for ref in refs[start + 1 : start + count]:
            total = total + full(ref[...])
        if stacked:
            refs[-1][:, at] = low(total)
        else:
            refs[at - len(counts)][...] = low(total)
        start += count


def add_up_far(depth, count, pos_ref, *refs):
    inputs, outs = refs[: 2 * count], refs[2 * count :]
    step = pl.program_id(0)
    for path in range(2):
        total = full(inputs[path * count][...])
        for ref in inputs[path * count + 1 : (path + 1) * count]:
            total = total + full(ref[...])
        for at in range(depth):

            @pl.when(step == at)
            def _():
                outs[at][path] = total[0].astype(outs[at].dtype)


def add_all(*refs):
    total = full(refs[0][...])
    for ref in refs[1:-1]:
        total = total + full(ref[...])
    refs[-1][...] = low(total)


def spread(depth, up_size, width, near_at, far_at, pos_ref, near_ref, far_ref, params_ref, small, sem):
    place = Place(pos_ref)
    rows = near_ref.shape[3] - SMALL
    for far_row, part in enumerate((near_ref.at[near_at], far_ref.at[far_at])):
        for level in range(depth):
            pltpu.make_async_copy(
                part.at[level, 0, pl.ds(rows, SMALL)], small.at[far_row, level], sem
            ).start()
    wait_all(small, sem)
    ups, others = 0.0, 0.0
    for far_row in range(2):
        for level in range(depth):
            shard = place.shard(level, far_row)
            block = full(small[far_row, level])
            up = jnp.concatenate([block, jnp.zeros((SMALL, 4 * WIDE - HALF), F32)], 1)
            ups += pltpu.roll(up, shard * up_size, 1)
            other = jnp.concatenate([block[:, :128], jnp.zeros((SMALL, WIDE - 128), F32)], 1)
            others += pltpu.roll(other, shard * width, 1)
    params_ref[...] = ups
    params_ref[1:9, :WIDE] = others[1:9]


VMEM = pltpu.MemorySpace.VMEM
SMEM = pltpu.MemorySpace.SMEM
ANY = pl.ANY
F32 = jnp.float32
BF16 = jnp.bfloat16


def call(kernel, spaces, outs, scratch, cost, after=(), limit=VMEM_LIMIT):
    run = pl.pallas_call(
        kernel,
        in_specs=[pl.BlockSpec(memory_space=space) for space in spaces + [ANY] * len(after)],
        out_specs=[pl.BlockSpec(memory_space=space) for _, _, space in outs],
        out_shape=[jax.ShapeDtypeStruct(shape, dtype) for shape, dtype, _ in outs],
        scratch_shapes=scratch,
        compiler_params=pltpu.CompilerParams(vmem_limit_bytes=limit),
        cost_estimate=pl.CostEstimate(flops=int(cost * COST), bytes_accessed=0, transcendentals=0),
    )
    return lambda *args: run(*args, *after)


def pass_through(*refs):
    pass


def tie(values, after):
    count = len(values)
    return pl.pallas_call(
        pass_through,
        in_specs=[pl.BlockSpec(memory_space=ANY)] * (count + len(after)),
        out_specs=[pl.BlockSpec(memory_space=ANY)] * count,
        out_shape=[jax.ShapeDtypeStruct(value.shape, value.dtype) for value in values],
        input_output_aliases={at: at for at in range(count)},
    )(*values, *after)


DMA = pltpu.SemaphoreType.DMA


class Sizes:
    def __init__(self, tokens, seqs, shards, rows, up_size, width):
        self.tokens, self.seqs, self.shards, self.rows = tokens, seqs, shards, rows
        self.up_size, self.width = up_size, width
        self.depth = shards // 2
        self.slots = tokens // seqs

    def columns(self, count):
        return pltpu.VMEM((count, self.shards, self.rows, WIDE), BF16)

    def by_rows(self):
        return pltpu.VMEM((self.shards, 4, self.rows, WIDE), BF16)

    def unit_grad(self, more=0):
        return [((2, 2, 2, self.depth, self.rows + more, HALF), BF16, ANY)] * 2


def run_attention_forward(z, pos, counts, x, unit, params, after=()):
    t = z.tokens
    return call(
        functools.partial(attention_forward, z.depth, z.seqs, len(after)),
        [SMEM, SMEM] + [VMEM] * 2 + [ANY] * 8,
        [
            ((t, WIDE), F32, VMEM),
            ((t, WIDE), F32, VMEM),
            ((t, 128), F32, VMEM),
            ((WIDE, t), BF16, VMEM),
            ((WIDE, t), BF16, VMEM),
            ((WIDE, t), BF16, VMEM),
            ((3 * PAIRS, t, PAIR), BF16, VMEM),
            ((z.seqs, PAIRS, z.slots, 2 * KEYS), BF16, ANY),
        ],
        [
            z.columns(4),
            pltpu.VMEM((PAIRS, t, PAIR), BF16),
            pltpu.VMEM((2, z.slots, 2 * KEYS), BF16),
            DMA,
            DMA((2,)),
        ],
        21,
        after,
    )(pos, counts, x, params, *unit)


def run_mlp_forward(z, pos, first, group, params, after=()):
    t = z.tokens
    return call(
        functools.partial(mlp_forward, z.depth, len(after)),
        [SMEM] + [VMEM] * 2 + [ANY] * 8,
        [
            ((t, WIDE), F32, VMEM),
            ((t, WIDE), F32, VMEM),
            ((t, 128), F32, VMEM),
            ((4, WIDE, t), BF16, ANY),
            ((4, t, WIDE), BF16, ANY),
        ],
        [
            z.columns(4),
            z.by_rows(),
            pltpu.VMEM((t, WIDE), F32),
            pltpu.VMEM((t, WIDE), BF16),
            pltpu.VMEM((2, WIDE, t), BF16),
            pltpu.VMEM((2, t, WIDE), BF16),
            DMA,
            DMA,
            DMA((2,)),
            DMA((2,)),
        ],
        20,
        after,
    )(pos, first, params, *group)


def run_down_backward(z, pos, grad, hat, scale, params, act_t, after=()):
    t = z.tokens
    return call(
        functools.partial(down_backward, z.depth, len(after)),
        [SMEM, VMEM, VMEM, VMEM, VMEM, ANY],
        [
            ((t, WIDE), F32, VMEM),
            ((8, WIDE), F32, VMEM),
            *z.unit_grad(),
        ],
        [
            pltpu.VMEM((4, WIDE, t), BF16),
            pltpu.VMEM((2, z.shards // 4, 4, z.rows, WIDE), BF16),
            DMA,
            DMA((2,)),
        ],
        11.3,
        after,
    )(pos, grad, hat, scale, params, act_t)


def run_up_backward(z, pos, second, group, slope, first_t, hat, scale, params, after=()):
    t = z.tokens
    return call(
        functools.partial(up_backward, z.depth, len(after)),
        [SMEM, VMEM, ANY] + [VMEM] * 4 + [ANY] * 8,
        [
            ((t, WIDE), F32, VMEM),
            ((8, WIDE), F32, VMEM),
            ((1, 4 * WIDE), F32, VMEM),
            *z.unit_grad(),
        ],
        [
            z.columns(4),
            z.by_rows(),
            pltpu.VMEM((4, t, WIDE), BF16),
            pltpu.VMEM((t, WIDE), F32),
            pltpu.VMEM((2, z.shards, z.rows, WIDE), BF16),
            DMA,
            DMA,
            DMA,
            DMA((2,)),
        ],
        20,
        after,
    )(pos, second, slope, first_t, hat, scale, params, *group)


def run_attention_backward(z, pos, grad, unit, qkv, probs, after=()):
    t = z.tokens
    return call(
        functools.partial(attention_backward, z.depth, z.seqs, len(after)),
        [SMEM] + [VMEM] * 2 + [ANY] * 9,
        [((3 * PAIRS, t, PAIR), BF16, VMEM)],
        [
            pltpu.VMEM((z.shards, z.rows, WIDE), BF16),
            pltpu.VMEM((z.seqs, PAIRS, z.slots, 2 * KEYS), BF16),
            pltpu.VMEM((PAIRS, t, PAIR), BF16),
            DMA,
            DMA,
        ],
        15.4,
        after,
    )(pos, grad, qkv, probs, *unit)[0]


def run_qkv_weights(z, pos, grad, grads, ctx_t, x_t, down_sums, up_sums, up_bias, after=()):
    return call(
        functools.partial(qkv_weights, z.depth, z.up_size, z.width, len(after)),
        [SMEM] + [VMEM] * 7,
        z.unit_grad(SMALL),
        [
            pltpu.VMEM((2, z.shards, z.rows, WIDE), BF16),
            pltpu.VMEM((SMALL, WIDE), F32),
            pltpu.VMEM((SMALL, HALF), F32),
            pltpu.VMEM((z.shards, SMALL, HALF), BF16),
            DMA((2,)),
            DMA,
        ],
        8,
        after,
    )(pos, grad, grads, ctx_t, x_t, down_sums, up_sums, up_bias)


def run_qkv_backward(z, pos, grad, grads, unit, after=()):
    return call(
        functools.partial(qkv_backward, z.depth, len(after)),
        [SMEM] + [VMEM] * 2 + [ANY] * 8,
        [((z.tokens, WIDE), F32, VMEM)],
        [
            z.columns(3),
            DMA((3,)),
        ],
        7,
        after,
    )(pos, grad, grads, *unit)[0]


def run_finish_first(z, pos, quarters):
    r = z.rows
    return call(
        finish_first,
        [SMEM] + [VMEM] * (4 * LAYERS),
        [
            ((LAYERS, r, 3 * WIDE), F32, VMEM),
            ((LAYERS, r, WIDE), F32, VMEM),
            ((LAYERS, z.up_size), F32, VMEM),
            ((LAYERS, 6, z.width), F32, VMEM),
            ((LAYERS, 2, z.width), F32, VMEM),
        ],
        [],
        3,
        limit=SMALL_LIMIT,
    )(pos, *quarters)


def run_finish_second(z, pos, quarters, after=()):
    r = z.rows
    return call(
        functools.partial(finish_second, len(after)),
        [SMEM] + [VMEM] * (4 * LAYERS),
        [
            ((LAYERS, r, 4 * WIDE), F32, VMEM),
            ((LAYERS, 4 * r, WIDE), F32, VMEM),
        ],
        [],
        5,
        after,
        limit=SMALL_LIMIT,
    )(pos, *quarters)


def run_prepare(z, pos, *arrays):
    r = z.rows
    return call(
        prepare,
        [SMEM] + [ANY] * 4 + [VMEM] * 3,
        [
            ((2, 1, r + SMALL, HALF), BF16, VMEM),
            ((2, 2, r, HALF), BF16, VMEM),
            ((2, 3, r, HALF), BF16, VMEM),
        ],
        [
            pltpu.VMEM((SMALL, HALF), F32),
            DMA((LAYERS, 3, 2)),
        ],
        1,
        limit=SMALL_LIMIT,
    )(pos, *arrays)


def run_columns_of(pos, pieces):
    depth = len(pieces)
    return call(
        functools.partial(columns_of, depth),
        [SMEM] + [VMEM] * depth,
        [((depth,) + pieces[0].shape[1:], BF16, VMEM)] * 2,
        [],
        2,
        limit=SMALL_LIMIT,
    )(pos, *pieces)


def run_split_paths(column, sizes):
    outs = []
    for size in sizes:
        outs += [(column.shape[:1] + (size,) + column.shape[3:], BF16, VMEM)] * 2
    return call(functools.partial(split_paths, sizes), [VMEM], outs, [], 2, limit=SMALL_LIMIT)(column)


def run_join(pairs):
    return call(
        join, [VMEM] * 4, [((2,) + near.shape, BF16, VMEM) for near, _ in pairs], [], 2,
        limit=SMALL_LIMIT,
    )(*[part for pair in pairs for part in pair])


def add_specs(sums, size, place):
    specs = []
    for parts in sums:
        for array, lead in parts:
            rest = array.shape[len(lead) + 1 :]
            specs.append(
                pl.BlockSpec(
                    (None,) * len(lead) + (size,) + rest,
                    lambda *at, lead=lead, rest=len(rest): lead + (place(*at),) + (0,) * rest,
                )
            )
    return specs


def run_add_up(sums, stacked=False):
    array, lead = sums[0][0]
    shape = array.shape[len(lead) :]
    size = shape[0] // 2
    if stacked:
        outs = [(shape[0], len(sums)) + shape[1:]]
    else:
        outs = [shape] * len(sums)
    return pl.pallas_call(
        functools.partial(add_up, [len(parts) for parts in sums], stacked),
        grid=(2,),
        in_specs=add_specs(sums, size, lambda step: step),
        out_specs=[
            pl.BlockSpec((size,) + out[1:], lambda step, rest=len(out) - 1: (step,) + (0,) * rest) for out in outs
        ],
        out_shape=[jax.ShapeDtypeStruct(out, BF16) for out in outs],
        compiler_params=pltpu.CompilerParams(vmem_limit_bytes=SMALL_LIMIT),
        cost_estimate=pl.CostEstimate(flops=int(3 * COST), bytes_accessed=0, transcendentals=0),
    )(*[array for parts in sums for array, _ in parts])


def run_add_up_far(pos, sums):
    array, lead = sums[0][0]
    depth, *rest = array.shape[len(lead) :]
    outs = [jax.ShapeDtypeStruct((2, *rest), F32 if at == 0 else BF16) for at in range(depth)]
    return pl.pallas_call(
        functools.partial(add_up_far, depth, len(sums[0])),
        grid_spec=pltpu.PrefetchScalarGridSpec(
            num_scalar_prefetch=1,
            grid=(depth,),
            in_specs=add_specs(sums, 1, lambda step, pos_ref: lax.rem(pos_ref[3] + step, depth)),
            out_specs=[pl.BlockSpec(out.shape, lambda step, pos_ref: (0, 0, 0)) for out in outs],
        ),
        out_shape=outs,
        compiler_params=pltpu.CompilerParams(vmem_limit_bytes=SMALL_LIMIT),
        cost_estimate=pl.CostEstimate(flops=int(3 * COST), bytes_accessed=0, transcendentals=0),
    )(pos, *[array for parts in sums for array, _ in parts])


def run_add_all(arrays):
    return call(add_all, [VMEM] * len(arrays), [(arrays[0].shape, BF16, VMEM)], [], 1, limit=SMALL_LIMIT)(*arrays)[0]


def run_spread(z, pos, near, near_at, far, far_at):
    return call(
        functools.partial(spread, z.depth, z.up_size, z.width, near_at, far_at),
        [SMEM, ANY, ANY],
        [((SMALL, 4 * WIDE), F32, VMEM)],
        [pltpu.VMEM((2, z.depth, SMALL, HALF), BF16), DMA],
        2,
        limit=SMALL_LIMIT,
    )(pos, near, far)[0]


class Links:
    def __init__(self, rep_size, fsdp_size):
        self.rep_size, self.fsdp_size = rep_size, fsdp_size
        self.depth = fsdp_size // 2
        rep_at, fsdp_at = lax.axis_index("rep"), lax.axis_index("fsdp")
        self.core, self.side = rep_at % 2, (rep_at // 2) % 2
        self.row, self.level = fsdp_at % 2, fsdp_at // 2

    def permute(self, value, target):
        pairs = []
        for rep_at in range(self.rep_size):
            for fsdp_at in range(self.fsdp_size):
                to_rep, to_fsdp = target(rep_at, fsdp_at)
                pairs.append((rep_at * self.fsdp_size + fsdp_at, to_rep * self.fsdp_size + to_fsdp))
        return lax.ppermute(value, AXES, pairs)

    def other_core(self, value):
        return self.permute(value, lambda r, f: (r ^ 1, f))

    def other_side(self, value):
        return self.permute(value, lambda r, f: (r ^ 2, f))

    def other_row(self, value):
        return self.permute(value, lambda r, f: (r, f ^ 1))

    def level_up(self, value, step):
        return self.permute(value, lambda r, f: (r, ((f // 2 + step) % self.depth) * 2 + f % 2))

    def levels(self):
        return [list(range(row, self.fsdp_size, 2)) for row in range(2)]


class Gather:
    def __init__(self, name, links, columns):
        self.name, self.links, self.live, self.moving = name, links, list(columns), []

    def scope(self, stage):
        return jax.named_scope("gather_" + self.name + "_" + stage)

    def first(self):
        with self.scope("first"):
            self.moving = [self.links.other_row(self.live[0]), self.links.other_side(self.live[1])]

    def join(self):
        with self.scope("join"):
            self.live, self.moving = list(run_join(list(zip(self.live, self.moving)))), []

    def second(self, cores=2):
        with self.scope("second"):
            self.moving = [self.links.other_side(self.live[0]), self.links.other_row(self.live[1])]
        with self.scope("cores"):
            self.moving += [self.links.other_core(part) for part in self.live[:cores]]

    def last(self):
        self.live += self.moving
        near, gone = self.live[:4], len(self.live) - 4
        with self.scope("last"):
            self.moving = [self.links.other_core(part) for part in near[gone:]]

    def arrays(self):
        near, far = self.live[:4], self.live[4:] + self.moving
        return [part for path in range(2) for part in (near[path], near[2 + path], far[path], far[2 + path])]


class Sum:
    def __init__(self, name, links, near, far):
        self.name, self.links, self.near, self.sends = name, links, near, [far]
        self.hops = ((links.other_row, links.other_side), (links.other_side, links.other_row))

    def scope(self, stage):
        return jax.named_scope("sum_" + self.name + "_" + stage)

    def cores(self):
        with self.scope("cores"):
            self.moving = [self.links.other_core(self.sends[0])]

    def after_cores(self):
        self.parts = [[(self.near, (path,)), (self.moving[0], (path,))] for path in range(2)]
        with self.scope("first"):
            self.sends = list(run_add_up(self.at(1)))

    def at(self, far):
        return [[(array, lead + (far,)) for array, lead in parts] for parts in self.parts]

    def first(self):
        with self.scope("first"):
            self.moving = [self.hops[path][0](self.sends[path]) for path in range(2)]

    def after_first(self):
        self.parts = [parts + [(moved, ())] for parts, moved in zip(self.at(0), self.moving)]
        with self.scope("second"):
            self.sends = list(run_add_up(self.at(1)))

    def second(self):
        with self.scope("second"):
            self.moving = [self.hops[path][1](self.sends[path]) for path in range(2)]

    def after_second(self):
        self.parts = [parts + [(moved, ())] for parts, moved in zip(self.at(0), self.moving)]


class Share:
    def __init__(self, name, links, pos, sums, offload):
        self.name, self.links, self.offload = name, links, offload
        with self.scope():
            parts = [part for one in sums for part in one.parts]
            if offload:
                total = run_add_up(parts, stacked=True)[0]
                self.sends = [
                    lax.psum_scatter(total, "fsdp", scatter_dimension=0, axis_index_groups=links.levels())
                ]
            else:
                self.kept, *self.sends = run_add_up_far(pos, parts)

    def scope(self):
        return jax.named_scope("share_" + self.name)

    def levels(self):
        with self.scope():
            self.moving = [self.links.level_up(send, at + 1) for at, send in enumerate(self.sends)]

    def after_levels(self):
        with self.scope():
            self.sends = [run_add_all([self.kept] + self.moving)]

    def copies(self):
        if self.links.rep_size > 4:
            groups = [list(range(first, self.links.rep_size, 4)) for first in range(4)]
            self.sends = [lax.psum(self.sends[0], "rep", axis_index_groups=groups)]

    def sides(self):
        with self.scope():
            self.sends += [self.links.other_side(self.sends[0])]

    def last(self):
        with self.scope():
            self.moving = [self.links.other_core(send) for send in self.sends]

    def quarters(self):
        return self.sends + self.moving


def order(steps, after=()):
    names = ("live", "moving", "sends")
    held = [(step, name) for step in steps for name in (names[:2] if hasattr(step, "live") else names[2:])]
    values = [value for step, name in held for value in getattr(step, name)]
    values = list(tie(values, list(after)))
    token = min(values, key=lambda value: value.size)
    for step, name in held:
        size = len(getattr(step, name))
        setattr(step, name, values[:size])
        values = values[size:]
    return [token]


def shards(
    rep_size, fsdp_size, hidden, region_counts, w_qkv, w_out, w_up, w_down, bias_up, biases, norm_gains, cotangent
):
    links = Links(rep_size, fsdp_size)
    z = Sizes(
        hidden.shape[0], region_counts.shape[0], fsdp_size, w_qkv.shape[1], bias_up.shape[1], biases.shape[2]
    )
    pos = jnp.stack([links.core, links.side, links.row, links.level]).astype(jnp.int32)
    quarters = run_prepare(z, pos, w_qkv, w_out, w_up, w_down, bias_up, biases, norm_gains)
    kept, groups, params = [], [None] * 4, [None] * 2

    def run_first(layer, states, after):
        return run_attention_forward(z, pos, region_counts, states, groups[2 * layer], params[layer], after)

    def run_second(layer, first, after):
        return run_mlp_forward(z, pos, first, groups[2 * layer + 1], params[layer], after)

    def columns(name, quarter, after=()):
        with jax.named_scope("columns_" + name):
            if after:
                quarter = tie([quarter], list(after))[0]
            pieces = [quarter] + [links.level_up(quarter, step) for step in range(1, links.depth)]
            return run_columns_of(pos, pieces)

    first_0 = Gather("first0", links, columns("first0", quarters[0]))
    first_0.first()
    second_0 = Gather("second0", links, columns("second0", quarters[1], first_0.live))

    first_0.join()
    first_0.second()

    order([first_0, second_0])
    first_0.last()
    second_0.first()
    with jax.named_scope("columns_third"):
        third = tie([quarters[2]], second_0.live)[0]
        third = lax.all_gather(third, "fsdp", axis_index_groups=links.levels())
    params[0] = run_spread(z, pos, first_0.live[0], 0, first_0.live[0], 1)
    params[1] = run_spread(z, pos, first_0.live[1], 0, first_0.live[3], 0)
    groups[0] = first_0.arrays()

    second_0.join()
    token = order([second_0], first_0.moving)
    second_0.second()
    one = run_first(0, hidden, token)

    with jax.named_scope("columns_third"):
        third = run_split_paths(third, (1, 2))
    first_1, second_1 = Gather("first1", links, third[:2]), Gather("second1", links, third[2:])
    order([second_0, first_1], one[2:3])
    second_0.last()
    first_1.first()
    groups[1] = second_0.arrays()

    first_1.join()
    token = order([first_1, second_1], second_0.moving)
    first_1.second(cores=1)
    second_1.first()
    two = run_second(0, one[0], token)
    kept.append((one, two))

    second_1.join()
    order([first_1, second_1], two[2:3])
    first_1.last()
    groups[2] = first_1.arrays()

    token = order([second_1], first_1.moving)
    second_1.second()
    one = run_first(1, two[0], token)

    order([second_1], one[2:3])
    second_1.last()
    groups[3] = second_1.arrays()
    two = run_second(1, one[0], ())
    kept.append((one, two))
    output = low(two[0])

    def run_down(layer, gradient, after):
        hat, scale, act_t = kept[layer][1][1:4]
        return run_down_backward(z, pos, gradient, hat, scale, params[layer], act_t, after)

    def run_up(layer, second, after):
        hat, scale, first_t = kept[layer][0][1], kept[layer][0][2], kept[layer][0][5]
        return run_up_backward(
            z, pos, second, groups[2 * layer + 1], kept[layer][1][4], first_t, hat, scale, params[layer], after
        )

    def run_attention(layer, first_in, after):
        qkv, probs = kept[layer][0][6:8]
        return run_attention_backward(z, pos, first_in, groups[2 * layer], qkv, probs, after)

    def run_weights(layer, first_in, grads, small, after):
        x_t, ctx_t = kept[layer][0][3:5]
        return run_qkv_weights(z, pos, first_in, grads, ctx_t, x_t, *small, after)

    def run_states(layer, first_in, grads, after):
        return run_qkv_backward(z, pos, first_in, grads, groups[2 * layer], after)

    second, down_sums, near, far = run_down(1, cotangent, ())
    sum_down_1 = Sum("down1", links, near, far)

    token = order([sum_down_1])
    sum_down_1.cores()
    first_in, up_sums, up_bias, near, far = run_up(1, second, token)
    sum_up_1 = Sum("up1", links, near, far)

    sum_down_1.after_cores()
    token = order([sum_down_1, sum_up_1])
    sum_down_1.first()
    sum_up_1.cores()
    grads = run_attention(1, first_in, token)

    sum_down_1.after_first()
    sum_up_1.after_cores()
    token = order([sum_down_1, sum_up_1], [grads])
    sum_up_1.first()
    sum_down_1.second()
    near, far = run_weights(1, first_in, grads, (down_sums, up_sums, up_bias), token)
    sum_first_1 = Sum("first1", links, near, far)
    gradient = run_states(1, first_in, grads, sum_first_1.sends)

    sum_up_1.after_first()
    sum_down_1.after_second()
    token = order([sum_up_1, sum_first_1], sum_down_1.moving + [gradient])
    sum_up_1.second()
    sum_first_1.cores()
    second, down_sums, near, far = run_down(0, gradient, token)
    sum_down_0 = Sum("down0", links, near, far)

    sum_up_1.after_second()
    sum_first_1.after_cores()
    token = order([sum_first_1, sum_down_0], sum_up_1.moving)
    sum_first_1.first()
    sum_down_0.cores()
    share_second_1 = Share("second1", links, pos, [sum_up_1, sum_down_1], True)
    first_in, up_sums, up_bias, near, far = run_up(0, second, token)
    sum_up_0 = Sum("up0", links, near, far)

    sum_first_1.after_first()
    sum_down_0.after_cores()
    token = order([sum_first_1, sum_down_0, sum_up_0])
    sum_first_1.second()
    sum_down_0.first()
    sum_up_0.cores()
    grads = run_attention(0, first_in, token)

    sum_first_1.after_second()
    sum_down_0.after_first()
    sum_up_0.after_cores()
    share_second_1.copies()
    share_first_1 = Share("first1", links, pos, [sum_first_1], True)
    token = order([sum_down_0, sum_up_0, share_second_1], [grads] + sum_first_1.moving)
    sum_up_0.first()
    sum_down_0.second()
    share_second_1.sides()
    near, far = run_weights(0, first_in, grads, (down_sums, up_sums, up_bias), token)
    sum_first_0 = Sum("first0", links, near, far)

    sum_up_0.after_first()
    sum_down_0.after_second()
    token = order([sum_up_0, sum_first_0, share_second_1], sum_down_0.moving)
    sum_first_0.cores()
    sum_up_0.second()
    share_second_1.last()
    gradient = run_states(0, first_in, grads, token)

    sum_first_0.after_cores()
    sum_up_0.after_second()
    share_first_1.copies()
    order([sum_first_0, share_first_1], sum_up_0.moving + [gradient])
    sum_first_0.first()
    share_second_0 = Share("second0", links, pos, [sum_up_0, sum_down_0], True)
    share_first_1.sides()

    sum_first_0.after_first()
    order([sum_first_0, share_first_1])
    sum_first_0.second()
    share_first_1.last()

    sum_first_0.after_second()
    share_first_0 = Share("first0", links, pos, [sum_first_0], False)
    share_second_0.copies()
    order([share_first_0, share_second_0], share_first_1.moving)
    share_first_0.levels()
    share_second_0.sides()

    share_first_0.after_levels()
    share_first_0.copies()
    order([share_first_0, share_second_0])
    share_first_0.sides()
    share_second_0.last()

    order([share_first_0], share_second_0.moving)
    share_first_0.last()
    up_grad, down_grad = run_finish_second(z, pos, share_second_0.quarters() + share_second_1.quarters())
    qkv_grad, out_grad, *small = run_finish_first(z, pos, share_first_0.quarters() + share_first_1.quarters())
    return (output, gradient, qkv_grad, out_grad, up_grad, down_grad) + tuple(small)


def solution(mesh):
    in_specs = (
        P(("rep", "fsdp"), None),
        P(("rep", "fsdp")),
        P(None, "fsdp", None),
        P(None, "fsdp", None),
        P(None, "fsdp", None),
        P(None, "fsdp", None),
        P(None, "fsdp"),
        P(None, None, "fsdp"),
        P(None, None, "fsdp"),
        P(("rep", "fsdp"), None),
    )
    out_specs = (
        P(("rep", "fsdp"), None),
        P(("rep", "fsdp"), None),
        P(None, "fsdp", None),
        P(None, "fsdp", None),
        P(None, "fsdp", None),
        P(None, "fsdp", None),
        P(None, "fsdp"),
        P(None, None, "fsdp"),
        P(None, None, "fsdp"),
    )
    local = functools.partial(shards, mesh.shape["rep"], mesh.shape["fsdp"])
    return jax.shard_map(local, mesh=mesh, in_specs=in_specs, out_specs=out_specs, check_vma=False)
```

time: 677 us -> 557 us (0.82)
  other arithmetic: 77.3 us -> 2.56 us
  starting transfers between devices: 135 us -> 66.9 us
  Pallas kernels: 194 us -> 254 us
  waiting for transfers between devices: 175 us -> 128 us
  between operations: 2.77 us -> 15.3 us
    unnamed x127 -> x278, local copies, waits for them, and re-layouts: 3.86 us -> 85.9 us
    ppermute x92 -> x83, starting transfers between devices: 135 us -> 66.3 us  [permute(): return lax.ppermute(value, AXES, pairs)]
    pallas_call x10 -> x65, Pallas kernels: 194 us -> 254 us  [the longest x27 225 us: call(): return lambda *args: run(*args, *after)]
    ppermute x92 -> x83, waiting for transfers between devices: 175 us -> 125 us  [permute(): return lax.ppermute(value, AXES, pairs)]
    another operation x54 -> x0, other arithmetic: 44.8 us -> none  [the longest x18 38.7 us: gather_unit(): part = jnp.stack([part, hop(part)])]
    squeeze x11 -> x0, local copies, waits for them, and re-layouts: 29.1 us -> none  [the longest x6 18.9 us: sum_unit(): total = full(grad[0]) + full(links.other_core(grad[1]))]
    add x16 -> x0, other arithmetic: 19.5 us -> none  [the longest x6 11.6 us: sum_unit(): total = full(grad[0]) + full(links.other_core(grad[1]))]
    slice x32 -> x0, local copies, waits for them, and re-layouts: 13.7 us -> none  [the longest x4 2.69 us: shards(): rows[5]]
  transfers between devices with their start and end apart: 92 -> 87, of which waited for: 34 -> 34; matrix products, arithmetic and copies ran while one was open for 19% -> 0% of each run, Pallas kernels for 24% -> 39%
where the time goes in v2:
time: 557 us; the launch traced here: 553 us
  Pallas kernels  254 us (46%)
  waiting for transfers between devices  128 us (23%)
  local copies, waits for them, and re-layouts  85.9 us (15%)
  starting transfers between devices  66.9 us (12%)
  between operations  15.3 us (3%)
    pallas_call x27, Pallas kernels, call(): return lambda *args: run(*args, *after)  225 us
    ppermute x83, waiting for transfers between devices, permute(): return lax.ppermute(value, AXES, pairs)  125 us
    unnamed x278, local copies, waits for them, and re-layouts  85.9 us
    ppermute x83, starting transfers between devices, permute(): return lax.ppermute(value, AXES, pairs)  66.3 us
    pallas_call x15, Pallas kernels, run_add_up(): pl.pallas_call(functools.partial(add_up, [len(parts) for parts in sums],...  26.2 us
  transfers between devices with their start and end apart: 87, of which 34 were waited for; matrix products, arithmetic and copies ran while one was open for 0% of the time, Pallas kernels for 39%

profile of v2, /device:TPU:0, one launch (start us, length us, event | category | flops | bytes accessed | tf_op | source)
XLA Modules:
  0.0 552.8 jit_solution(16075863693412560417)
XLA Ops:
  14.9 5.1 collective-permute-start.2
  21.1 3.8 collective-permute-done.2.refs_3_
  24.9 9.8 %collective-permute-done.1.refs_2_ = bf16[2,1,112,384]{3,2,1,0:T(8,128)(2,1)S(1)} collective-permute-done((bf16[2,1,112,384]{3,2,1,0:T(8,128)(2,1)S(1)}, bf16[2,1,112,384]{3,2,1,0:T(8,128)(2,1)S(1)}, u32[]{:S(2)}, u32[]{:S(2)}) %collective-permute-start.1) | collective-permute-done | bytes 172064 | tf_op jit(solution)/shard_map/columns_first0/ppermute | solution.py:1026
  39.3 2.0 collective-permute-start.10
  41.2 3.8 collective-permute-done.3.refs_1_
  50.7 9.2 %collective-permute-done.10.refs_2_ = bf16[2,2,96,384]{3,2,1,0:T(8,128)(2,1)S(1)} collective-permute-done((bf16[2,2,96,384]{3,2,1,0:T(8,128)(2,1)}, bf16[2,2,96,384]{3,2,1,0:T(8,128)(2,1)S(1)}, u32[]{:S(2)}, u32[]{:S(2)}) %collective-permute-start.10) | collective-permute-done | bytes 294944 | tf_op jit(solution)/shard_map/columns_second0/ppermute | solution.py:1026
  59.9 8.7 %collective-permute-done.9.refs_1_ = bf16[2,2,96,384]{3,2,1,0:T(8,128)(2,1)S(1)} collective-permute-done((bf16[2,2,96,384]{3,2,1,0:T(8,128)(2,1)S(1)}, bf16[2,2,96,384]{3,2,1,0:T(8,128)(2,1)S(1)}, u32[]{:S(2)}, u32[]{:S(2)}) %collective-permute-start.9) | collective-permute-done | bytes 294944 | tf_op jit(solution)/shard_map/columns_second0/ppermute | solution.py:1026
  76.2 8.8 %collective-permute-done.14.refs_1_ = bf16[4,2,96,384]{3,2,1,0:T(8,128)(2,1)S(1)} collective-permute-done((bf16[4,2,96,384]{3,2,1,0:T(8,128)(2,1)}, bf16[4,2,96,384]{3,2,1,0:T(8,128)(2,1)S(1)}, u32[]{:S(2)}, u32[]{:S(2)}) %collective-permute-start.14) | collective-permute-done | bytes 589856 | tf_op jit(solution)/shard_map/gather_second0_first/ppermute | solution.py:1026
  90.7 20.7 %shard_map.173 = (f32[544,768]{1,0:T(8,128)}, f32[544,768]{1,0:T(8,128)}, f32[544,128]{1,0:T(8,128)}, bf16[768,544]{1,0:T(8,128)(2,1)}, bf16[768,544]{1,0:T(8,12...) custom-call(s32[4]{0:T(128)} %copy-done.116, s32[2]{0:T(128)} %counts_ref.3, ...), custom_call_target="tpu_custom_call" | custom-call | flops 24149999616 | tf_op jit(solution)/shard_map/pallas_call | solution.py:673
  111.4 2.5 all-gather.3.cloned.1.call-done
  122.1 6.3 %collective-permute-done.22.refs_1_ = bf16[4,1,96,384]{3,2,1,0:T(8,128)(2,1)S(1)} collective-permute-done((bf16[4,1,96,384]{3,2,1,0:T(8,128)(2,1)}, bf16[4,1,96,384]{3,2,1,0:T(8,128)(2,1)S(1)}, u32[]{:S(2)}, u32[]{:S(2)}) %collective-permute-start.22) | collective-permute-done | bytes 294944 | tf_op jit(solution)/shard_map/gather_first1_first/ppermute | solution.py:1026
  138.7 21.4 %shard_map.176 = (f32[544,768]{1,0:T(8,128)}, f32[544,768]{1,0:T(8,128)}, f32[544,128]{1,0:T(8,128)}, bf16[4,768,544]{2,1,0:T(8,128)(2,1)}, bf16[4,544,768]{2,1,0:T(8,128)(2,1)}) custom-call(s32[4]{0:T(128)} %copy-done.116, f32[544,768]{1,0:T(8,128)} %get-tuple-element.211.first_ref, f32[16,3072]{1,0:T(8,128)} %copy-done.128, ...), custom_call_target="tpu_custom_call" | custom-call | flops 23000000512 | tf_op jit(solution)/shard_map/pallas_call | solution.py:673
  160.2 4.4 collective-permute-done.27.refs_1_
  175.4 21.0 %shard_map.180 = (f32[544,768]{1,0:T(8,128)}, f32[544,768]{1,0:T(8,128)}, f32[544,128]{1,0:T(8,128)}, bf16[768,544]{1,0:T(8,128)(2,1)}, bf16[768,544]{1,0:T(8,12...) custom-call(s32[4]{0:T(128)} %copy-done.116, s32[2]{0:T(128)} %counts_ref.3, ...), custom_call_target="tpu_custom_call" | custom-call | flops 24149999616 | tf_op jit(solution)/shard_map/pallas_call | solution.py:673
  196.4 6.3 %collective-permute-done.33.refs_3_ = bf16[2,4,2,96,384]{4,3,2,1,0:T(8,128)(2,1)} collective-permute-done((bf16[2,4,2,96,384]{4,3,2,1,0:T(8,128)(2,1)}, bf16[2,4,2,96,384]{4,3,2,1,0:T(8,128)(2,1)}, u32[]{:S(2)}, u32[]{:S(2)}) %collective-permute-start.33) | collective-permute-done | bytes 1179680 | tf_op jit(solution)/shard_map/gather_second1_second/ppermute | solution.py:1026
  204.0 2.7 collective-permute-done.36.refs_3_
  208.3 21.6 %shard_map.182 = (f32[544,768]{1,0:T(8,128)}, f32[544,768]{1,0:T(8,128)}, f32[544,128]{1,0:T(8,128)}, bf16[4,768,544]{2,1,0:T(8,128)(2,1)}, bf16[4,544,768]{2,1,0:T(8,128)(2,1)}) custom-call(s32[4]{0:T(128)} %copy-done.116, f32[544,768]{1,0:T(8,128)} %get-tuple-element.245.first_ref, f32[16,3072]{1,0:T(8,128)} %copy-done.129, ...), custom_call_target="tpu_custom_call" | custom-call | flops 23000000512 | tf_op jit(solution)/shard_map/pallas_call | solution.py:673
  229.9 11.3 %shard_map.183 = (f32[544,768]{1,0:T(8,128)}, f32[8,768]{1,0:T(8,128)}, bf16[2,2,2,4,96,384]{5,4,3,2,1,0:T(8,128)(2,1)}, bf16[2,2,2,4,96,384]{5,4,3,2,1,0:T(8,128)(2,1)}) custom-call(s32[4]{0:T(128)} %copy-done.116, bf16[544,768]{1,0:T(8,128)(2,1)} %grad_ref.1, f32[544,768]{1,0:T(8,128)} %get-tuple-element.255.hat_ref, ...), custom_call_target="tpu_custom_call" | custom-call | flops 12995000320 | tf_op jit(solution)/shard_map/pallas_call | solution.py:673
  241.4 20.0 %shard_map.185 = (f32[544,768]{1,0:T(8,128)}, f32[8,768]{1,0:T(8,128)}, f32[1,3072]{1,0:T(1,128)}, bf16[2,2,2,4,96,384]{5,4,3,2,1,0:T(8,128)(2,1)}, bf16[2,2,2,4,96,384]{5,4,3,2,1,0:T(8,128)(2,1)}) custom-call(s32[4]{0:T(128)} %copy-done.116, f32[544,768]{1,0:T(8,128)} %get-tuple-element.258.second_ref, bf16[4,544,768]{2,1,0:T(8,128)(2,1)} %get-tuple-element.259.slope_ref, ...), custom_call_target="tpu_custom_call" | custom-call | flops 23000000512 | tf_op jit(solution)/shard_map/pallas_call | solution.py:673
  268.5 15.3 %shard_map.187.refs_4_.grads_ref = bf16[18,544,128]{2,1,0:T(8,128)(2,1)} custom-call(s32[4]{0:T(128)} %copy-done.116, f32[544,768]{1,0:T(8,128)} %get-tuple-element.263.grad_ref, bf16[18,544,128]{2,1,0:T(8,128)(2,1)} %get-tuple-element.264.qkv_ref, bf16[2,6,272,512]{3,2,1,0:T(8,128)(2,1)} %get-tuple-element.265.probs_ref, ...), custom_call_target="tpu_custom_call" | custom-call | flops 17710000128 | tf_op jit(solution)/shard_map/pallas_call | solution.py:673
  283.9 1.9 copy-done.11
  294.9 9.1 %shard_map.189 = (bf16[2,2,2,4,112,384]{5,4,3,2,1,0:T(8,128)(2,1)}, bf16[2,2,2,4,112,384]{5,4,3,2,1,0:T(8,128)(2,1)}) custom-call(s32[4]{0:T(128)} %copy-done.116, f32[544,768]{1,0:T(8,128)} %get-tuple-element.263.grad_ref, bf16[18,544,128]{2,1,0:T(8,128)(2,1)} %shard_map.187.refs_4_.grads_ref, bf16[768,544]{1,0:T(8,128)(2,1)} %get-tuple-element.271.ctx_t_ref, ...), custom_call_target="tpu_custom_call" | custom-call | flops 9200000000 | tf_op jit(solution)/shard_map/pallas_call | solution.py:673
  304.0 8.2 %shard_map.190.refs_5_.grad_ref = f32[544,768]{1,0:T(8,128)} custom-call(s32[4]{0:T(128)} %copy-done.116, f32[544,768]{1,0:T(8,128)} %get-tuple-element.263.grad_ref, bf16[18,544,128]{2,1,0:T(8,128)(2,1)} %shard_map.187.refs_4_.grads_ref, bf16[2,4,1,96,384]{4,3,2,1,0:T(8,128)(2,1)} %get-tuple-element.237.refs_0_, ...), custom_call_target="tpu_custom_call" | custom-call | flops 8049999872 | tf_op jit(solution)/shard_map/pallas_call | solution.py:673
  320.9 11.5 %shard_map.192 = (f32[544,768]{1,0:T(8,128)}, f32[8,768]{1,0:T(8,128)}, bf16[2,2,2,4,96,384]{5,4,3,2,1,0:T(8,128)(2,1)}, bf16[2,2,2,4,96,384]{5,4,3,2,1,0:T(8,128)(2,1)}) custom-call(s32[4]{0:T(128)} %copy-done.116, f32[544,768]{1,0:T(8,128)} %shard_map.190.refs_5_.grad_ref, f32[544,768]{1,0:T(8,128)} %get-tuple-element.285.hat_ref, ...), custom_call_target="tpu_custom_call" | custom-call | flops 12995000320 | tf_op jit(solution)/shard_map/pallas_call | solution.py:673
  334.2 1.9 sum_first1_first.1
  339.8 19.9 %shard_map.194 = (f32[544,768]{1,0:T(8,128)}, f32[8,768]{1,0:T(8,128)}, f32[1,3072]{1,0:T(1,128)}, bf16[2,2,2,4,96,384]{5,4,3,2,1,0:T(8,128)(2,1)}, bf16[2,2,2,4,96,384]{5,4,3,2,1,0:T(8,128)(2,1)}) custom-call(s32[4]{0:T(128)} %copy-done.116, f32[544,768]{1,0:T(8,128)} %get-tuple-element.293.second_ref, bf16[4,544,768]{2,1,0:T(8,128)(2,1)} %get-tuple-element.294.slope_ref, ...), custom_call_target="tpu_custom_call" | custom-call | flops 23000000512 | tf_op jit(solution)/shard_map/pallas_call | solution.py:673
  359.7 2.0 copy-done.3
  371.5 2.7 share_second1.1
  378.5 15.7 %shard_map.196.refs_5_.grads_ref = bf16[18,544,128]{2,1,0:T(8,128)(2,1)} custom-call(s32[4]{0:T(128)} %copy-done.116, f32[544,768]{1,0:T(8,128)} %get-tuple-element.304.grad_ref, bf16[18,544,128]{2,1,0:T(8,128)(2,1)} %get-tuple-element.305.qkv_ref, bf16[2,6,272,512]{3,2,1,0:T(8,128)(2,1)} %get-tuple-element.306.probs_ref, ...), custom_call_target="tpu_custom_call" | custom-call | flops 17710000128 | tf_op jit(solution)/shard_map/pallas_call | solution.py:673
  394.2 3.7 collective-permute-done.53.refs_2_.refs_10_
  413.2 9.2 %shard_map.198 = (bf16[2,2,2,4,112,384]{5,4,3,2,1,0:T(8,128)(2,1)}, bf16[2,2,2,4,112,384]{5,4,3,2,1,0:T(8,128)(2,1)}) custom-call(s32[4]{0:T(128)} %copy-done.116, f32[544,768]{1,0:T(8,128)} %get-tuple-element.304.grad_ref, bf16[18,544,128]{2,1,0:T(8,128)(2,1)} %shard_map.196.refs_5_.grads_ref, bf16[768,544]{1,0:T(8,128)(2,1)} %get-tuple-element.329.ctx_t_ref, ...), custom_call_target="tpu_custom_call" | custom-call | flops 9200000000 | tf_op jit(solution)/shard_map/pallas_call | solution.py:673
  422.4 6.5 %collective-permute-done.57.refs_2_ = bf16[2,4,96,384]{3,2,1,0:T(8,128)(2,1)} collective-permute-done((bf16[2,4,96,384]{3,2,1,0:T(8,128)(2,1)}, bf16[2,4,96,384]{3,2,1,0:T(8,128)(2,1)}, u32[]{:S(2)}, u32[]{:S(2)}) %collective-permute-start.57) | collective-permute-done | bytes 589856 | tf_op jit(solution)/shard_map/sum_up0_first/ppermute | solution.py:1026
  428.9 6.7 %collective-permute-done.58.refs_5_.refs_6_ = bf16[2,4,96,384]{3,2,1,0:T(8,128)(2,1)} collective-permute-done((bf16[2,4,96,384]{3,2,1,0:T(8,128)(2,1)}, bf16[2,4,96,384]{3,2,1,0:T(8,128)(2,1)}, u32[]{:S(2)}, u32[]{:S(2)}) %collective-permute-start.58) | collective-permute-done | bytes 589856 | tf_op jit(solution)/shard_map/sum_up0_first/ppermute | solution.py:1026
  444.2 2.3 share_first1.1
  449.4 4.9 collective-permute-done.64.refs_4_.refs_7_
  460.7 2.9 share_second0.1
  463.7 8.3 %shard_map.200.refs_5_ = f32[544,768]{1,0:T(8,128)} custom-call(s32[4]{0:T(128)} %copy-done.116, f32[544,768]{1,0:T(8,128)} %get-tuple-element.304.grad_ref, bf16[18,544,128]{2,1,0:T(8,128)(2,1)} %shard_map.196.refs_5_.grads_ref, bf16[2,4,1,112,384]{4,3,2,1,0:T(8,128)(2,1)} %get-tuple-element.200.near_ref.far_ref.refs_0_, ...), custom_call_target="tpu_custom_call" | custom-call | flops 8049999872 | tf_op jit(solution)/shard_map/pallas_call | solution.py:673
  479.6 12.3 %collective-permute-done.65.refs_2_ = bf16[2,4,112,384]{3,2,1,0:T(8,128)(2,1)S(1)} collective-permute-done((bf16[2,4,112,384]{3,2,1,0:T(8,128)(2,1)}, bf16[2,4,112,384]{3,2,1,0:T(8,128)(2,1)S(1)}, u32[]{:S(2)}, u32[]{:S(2)}) %collective-permute-start.65) | collective-permute-done | bytes 688160 | tf_op jit(solution)/shard_map/sum_first0_first/ppermute | solution.py:1026
  491.9 2.3 collective-permute-done.66.refs_5_.refs_6_
  501.3 4.2 collective-permute-done.68.refs_3_
  508.0 2.9 share_first0.2
  514.7 3.7 collective-permute-start.73
  518.9 2.9 collective-permute-done.72.refs_1_
  521.8 3.8 collective-permute-done.73.refs_2_
  530.2 2.5 convert_element_type.3
  532.7 3.2 collective-permute-done.76.refs_1_
  539.8 3.0 shard_map.207
  542.9 2.6 shard_map.206
  (475 shorter events, 172.2 us)
Async XLA Ops:
  7.2 106.7 %all-gather.3.cloned.1.call-start = ((), (), s32[]{:S(2)}) async-start(), calls=%async_computation.6 | async-start | bytes 2211840 | tf_op jit(solution)/shard_map/columns_third/all_gather | solution.py:1203
  39.3 20.6 %collective-permute-start.10 = (bf16[2,2,96,384]{3,2,1,0:T(8,128)(2,1)}, bf16[2,2,96,384]{3,2,1,0:T(8,128)(2,1)S(1)}, u32[]{:S(2)}, u32[]{:S(2)}) collective-permute-start(bf16[2,2,96,384]{3,2,1,0:T(8,128)(2,1)} %columns_second0.2.refs_0_), channel_id=1, source_target_pairs={{0,4},{1,5},{2,6},{3,7},{4,0},{5,1},{6,2},{7,3},{8,12},{9,13},{10,... | collective-permute-start | bytes 884744 | tf_op jit(solution)/shard_map/columns_second0/ppermute | solution.py:1026
  48.4 22.6 %collective-permute-start.7 = (bf16[2,4,1,112,384]{4,3,2,1,0:T(8,128)(2,1)S(1)}, bf16[2,4,1,112,384]{4,3,2,1,0:T(8,128)(2,1)S(1)}, u32[]{:S(2)}, u32[]{:S(2)}) collective-permute-start(bf16[2,4,1,112,384]{4,3,2,1,0:T(8,128)(2,1)S(1)} %get-tuple-element.195.refs_0_), channel_id=1, source_target_pairs={{0,8},{1,9},{2,10},{3,11},{4,12},{5,13},{6,14},{7,15},{8,0},{9,1},... | collective-permute-start | bytes 2064392 | tf_op jit(solution)/shard_map/gather_first0_cores/ppermute | solution.py:1026
  48.4 22.5 %collective-permute-start.5 = (bf16[2,4,1,112,384]{4,3,2,1,0:T(8,128)(2,1)S(1)}, bf16[2,4,1,112,384]{4,3,2,1,0:T(8,128)(2,1)S(1)}, u32[]{:S(2)}, u32[]{:S(2)}) collective-permute-start(bf16[2,4,1,112,384]{4,3,2,1,0:T(8,128)(2,1)S(1)} %get-tuple-element.195.refs_0_), channel_id=1, source_target_pairs={{0,16},{1,17},{2,18},{3,19},{4,20},{5,21},{6,22},{7,23},{8,24},{9,... | collective-permute-start | bytes 2064392 | tf_op jit(solution)/shard_map/gather_first0_second/ppermute | solution.py:1026
  50.0 20.9 %collective-permute-start.8 = (bf16[2,4,1,112,384]{4,3,2,1,0:T(8,128)(2,1)S(1)}, bf16[2,4,1,112,384]{4,3,2,1,0:T(8,128)(2,1)S(1)}, u32[]{:S(2)}, u32[]{:S(2)}) collective-permute-start(bf16[2,4,1,112,384]{4,3,2,1,0:T(8,128)(2,1)S(1)} %get-tuple-element.196.refs_1_), channel_id=1, source_target_pairs={{0,8},{1,9},{2,10},{3,11},{4,12},{5,13},{6,14},{7,15},{8,0},{9,1},... | collective-permute-start | bytes 2064392 | tf_op jit(solution)/shard_map/gather_first0_cores/ppermute | solution.py:1026
  50.2 20.8 %collective-permute-start.6 = (bf16[2,4,1,112,384]{4,3,2,1,0:T(8,128)(2,1)S(1)}, bf16[2,4,1,112,384]{4,3,2,1,0:T(8,128)(2,1)S(1)}, u32[]{:S(2)}, u32[]{:S(2)}) collective-permute-start(bf16[2,4,1,112,384]{4,3,2,1,0:T(8,128)(2,1)S(1)} %get-tuple-element.196.refs_1_), channel_id=1, source_target_pairs={{0,1},{1,0},{2,3},{3,2},{4,5},{5,4},{6,7},{7,6},{8,9},{9,8},{10,11... | collective-permute-start | bytes 2064392 | tf_op jit(solution)/shard_map/gather_first0_second/ppermute | solution.py:1026
  74.6 332.2 %reduce-scatter.4.cloned.1.call-start = ((), (), s32[]{:S(2)}) async-start(), calls=%async_computation.3 | async-start | bytes 1474560 | tf_op jit(solution)/shard_map/share_second1/reduce_scatter | solution.py:1121
  88.4 30.2 %collective-permute-start.19 = (bf16[2,4,2,96,384]{4,3,2,1,0:T(8,128)(2,1)}, bf16[2,4,2,96,384]{4,3,2,1,0:T(8,128)(2,1)}, u32[]{:S(2)}, u32[]{:S(2)}) collective-permute-start(bf16[2,4,2,96,384]{4,3,2,1,0:T(8,128)(2,1)} %get-tuple-element.212.refs_1_), channel_id=1, source_target_pairs={{0,8},{1,9},{2,10},{3,11},{4,12},{5,13},{6,14},{7,15},{8,0},{9,1},... | collective-permute-start | bytes 3538952 | tf_op jit(solution)/shard_map/gather_second0_cores/ppermute | solution.py:1026
  88.4 30.2 %collective-permute-start.17 = (bf16[2,4,2,96,384]{4,3,2,1,0:T(8,128)(2,1)}, bf16[2,4,2,96,384]{4,3,2,1,0:T(8,128)(2,1)}, u32[]{:S(2)}, u32[]{:S(2)}) collective-permute-start(bf16[2,4,2,96,384]{4,3,2,1,0:T(8,128)(2,1)} %get-tuple-element.212.refs_1_), channel_id=1, source_target_pairs={{0,1},{1,0},{2,3},{3,2},{4,5},{5,4},{6,7},{7,6},{8,9},{9,8},{10,11... | collective-permute-start | bytes 3538952 | tf_op jit(solution)/shard_map/gather_second0_second/ppermute | solution.py:1026
  89.9 28.6 %collective-permute-start.18 = (bf16[2,4,2,96,384]{4,3,2,1,0:T(8,128)(2,1)}, bf16[2,4,2,96,384]{4,3,2,1,0:T(8,128)(2,1)}, u32[]{:S(2)}, u32[]{:S(2)}) collective-permute-start(bf16[2,4,2,96,384]{4,3,2,1,0:T(8,128)(2,1)} %get-tuple-element.210.refs_8_.refs_0_), channel_id=1, source_target_pairs={{0,8},{1,9},{2,10},{3,11},{4,12},{5,13},{6,14},{7,15},{8,0},{9,1},... | collective-permute-start | bytes 3538952 | tf_op jit(solution)/shard_map/gather_second0_cores/ppermute | solution.py:1026
  90.2 28.5 %collective-permute-start.16 = (bf16[2,4,2,96,384]{4,3,2,1,0:T(8,128)(2,1)}, bf16[2,4,2,96,384]{4,3,2,1,0:T(8,128)(2,1)}, u32[]{:S(2)}, u32[]{:S(2)}) collective-permute-start(bf16[2,4,2,96,384]{4,3,2,1,0:T(8,128)(2,1)} %get-tuple-element.210.refs_8_.refs_0_), channel_id=1, source_target_pairs={{0,16},{1,17},{2,18},{3,19},{4,20},{5,21},{6,22},{7,23},{8,24},{9,... | collective-permute-start | bytes 3538952 | tf_op jit(solution)/shard_map/gather_second0_second/ppermute | solution.py:1026
  134.7 34.5 %collective-permute-start.26 = (bf16[2,4,1,96,384]{4,3,2,1,0:T(8,128)(2,1)}, bf16[2,4,1,96,384]{4,3,2,1,0:T(8,128)(2,1)}, u32[]{:S(2)}, u32[]{:S(2)}) collective-permute-start(bf16[2,4,1,96,384]{4,3,2,1,0:T(8,128)(2,1)} %get-tuple-element.229.refs_8_.refs_0_), channel_id=1, source_target_pairs={{0,8},{1,9},{2,10},{3,11},{4,12},{5,13},{6,14},{7,15},{8,0},{9,1},... | collective-permute-start | bytes 1769480 | tf_op jit(solution)/shard_map/gather_first1_cores/ppermute | solution.py:1026
  134.7 34.5 %collective-permute-start.24 = (bf16[2,4,1,96,384]{4,3,2,1,0:T(8,128)(2,1)}, bf16[2,4,1,96,384]{4,3,2,1,0:T(8,128)(2,1)}, u32[]{:S(2)}, u32[]{:S(2)}) collective-permute-start(bf16[2,4,1,96,384]{4,3,2,1,0:T(8,128)(2,1)} %get-tuple-element.229.refs_8_.refs_0_), channel_id=1, source_target_pairs={{0,16},{1,17},{2,18},{3,19},{4,20},{5,21},{6,22},{7,23},{8,24},{9,... | collective-permute-start | bytes 1769480 | tf_op jit(solution)/shard_map/gather_first1_second/ppermute | solution.py:1026
  136.1 33.0 %collective-permute-start.25 = (bf16[2,4,1,96,384]{4,3,2,1,0:T(8,128)(2,1)}, bf16[2,4,1,96,384]{4,3,2,1,0:T(8,128)(2,1)}, u32[]{:S(2)}, u32[]{:S(2)}) collective-permute-start(bf16[2,4,1,96,384]{4,3,2,1,0:T(8,128)(2,1)} %get-tuple-element.231.refs_1_), channel_id=1, source_target_pairs={{0,1},{1,0},{2,3},{3,2},{4,5},{5,4},{6,7},{7,6},{8,9},{9,8},{10,11... | collective-permute-start | bytes 1769480 | tf_op jit(solution)/shard_map/gather_first1_second/ppermute | solution.py:1026
  136.7 27.9 %collective-permute-start.27 = (bf16[4,2,96,384]{3,2,1,0:T(8,128)(2,1)}, bf16[4,2,96,384]{3,2,1,0:T(8,128)(2,1)}, u32[]{:S(2)}, u32[]{:S(2)}) collective-permute-start(bf16[4,2,96,384]{3,2,1,0:T(8,128)(2,1)} %get-tuple-element.232.refs_0_), channel_id=1, source_target_pairs={{0,1},{1,0},{2,3},{3,2},{4,5},{5,4},{6,7},{7,6},{8,9},{9,8},{10,11... | collective-permute-start | bytes 1769480 | tf_op jit(solution)/shard_map/gather_second1_first/ppermute | solution.py:1026
  138.2 26.4 %collective-permute-start.28 = (bf16[4,2,96,384]{3,2,1,0:T(8,128)(2,1)}, bf16[4,2,96,384]{3,2,1,0:T(8,128)(2,1)}, u32[]{:S(2)}, u32[]{:S(2)}) collective-permute-start(bf16[4,2,96,384]{3,2,1,0:T(8,128)(2,1)} %get-tuple-element.233.refs_2_), channel_id=1, source_target_pairs={{0,16},{1,17},{2,18},{3,19},{4,20},{5,21},{6,22},{7,23},{8,24},{9,... | collective-permute-start | bytes 1769480 | tf_op jit(solution)/shard_map/gather_second1_first/ppermute | solution.py:1026
  174.0 22.4 %collective-permute-start.35 = (bf16[2,4,2,96,384]{4,3,2,1,0:T(8,128)(2,1)}, bf16[2,4,2,96,384]{4,3,2,1,0:T(8,128)(2,1)}, u32[]{:S(2)}, u32[]{:S(2)}) collective-permute-start(bf16[2,4,2,96,384]{4,3,2,1,0:T(8,128)(2,1)} %get-tuple-element.246.refs_1_), channel_id=1, source_target_pairs={{0,8},{1,9},{2,10},{3,11},{4,12},{5,13},{6,14},{7,15},{8,0},{9,1},... | collective-permute-start | bytes 3538952 | tf_op jit(solution)/shard_map/gather_second1_cores/ppermute | solution.py:1026
  174.2 28.6 %collective-permute-start.33 = (bf16[2,4,2,96,384]{4,3,2,1,0:T(8,128)(2,1)}, bf16[2,4,2,96,384]{4,3,2,1,0:T(8,128)(2,1)}, u32[]{:S(2)}, u32[]{:S(2)}) collective-permute-start(bf16[2,4,2,96,384]{4,3,2,1,0:T(8,128)(2,1)} %get-tuple-element.246.refs_1_), channel_id=1, source_target_pairs={{0,1},{1,0},{2,3},{3,2},{4,5},{5,4},{6,7},{7,6},{8,9},{9,8},{10,11... | collective-permute-start | bytes 3538952 | tf_op jit(solution)/shard_map/gather_second1_second/ppermute | solution.py:1026
  174.7 28.0 %collective-permute-start.34 = (bf16[2,4,2,96,384]{4,3,2,1,0:T(8,128)(2,1)}, bf16[2,4,2,96,384]{4,3,2,1,0:T(8,128)(2,1)}, u32[]{:S(2)}, u32[]{:S(2)}) collective-permute-start(bf16[2,4,2,96,384]{4,3,2,1,0:T(8,128)(2,1)} %get-tuple-element.244.refs_8_.refs_0_), channel_id=1, source_target_pairs={{0,8},{1,9},{2,10},{3,11},{4,12},{5,13},{6,14},{7,15},{8,0},{9,1},... | collective-permute-start | bytes 3538952 | tf_op jit(solution)/shard_map/gather_second1_cores/ppermute | solution.py:1026
  174.8 28.6 %collective-permute-start.32 = (bf16[2,4,2,96,384]{4,3,2,1,0:T(8,128)(2,1)}, bf16[2,4,2,96,384]{4,3,2,1,0:T(8,128)(2,1)}, u32[]{:S(2)}, u32[]{:S(2)}) collective-permute-start(bf16[2,4,2,96,384]{4,3,2,1,0:T(8,128)(2,1)} %get-tuple-element.244.refs_8_.refs_0_), channel_id=1, source_target_pairs={{0,16},{1,17},{2,18},{3,19},{4,20},{5,21},{6,22},{7,23},{8,24},{9,... | collective-permute-start | bytes 3538952 | tf_op jit(solution)/shard_map/gather_second1_second/ppermute | solution.py:1026
  241.2 20.2 %collective-permute-start.38 = (bf16[2,2,2,4,96,384]{5,4,3,2,1,0:T(8,128)(2,1)}, bf16[2,2,2,4,96,384]{5,4,3,2,1,0:T(8,128)(2,1)}, u32[]{:S(2)}, u32[]{:S(2)}) collective-permute-start(bf16[2,2,2,4,96,384]{5,4,3,2,1,0:T(8,128)(2,1)} %shard_map.184.refs_8_), channel_id=1, source_target_pairs={{0,8},{1,9},{2,10},{3,11},{4,12},{5,13},{6,14},{7,15},{8,0},{9,1},... | collective-permute-start | bytes 7077896 | tf_op jit(solution)/shard_map/sum_down1_cores/ppermute | solution.py:1026
  266.1 21.2 %collective-permute-start.41 = (bf16[2,2,2,4,96,384]{5,4,3,2,1,0:T(8,128)(2,1)}, bf16[2,2,2,4,96,384]{5,4,3,2,1,0:T(8,128)(2,1)}, u32[]{:S(2)}, u32[]{:S(2)}) collective-permute-start(bf16[2,2,2,4,96,384]{5,4,3,2,1,0:T(8,128)(2,1)} %get-tuple-element.280), channel_id=1, source_target_pairs={{0,8},{1,9},{2,10},{3,11},{4,12},{5,13},{6,14},{7,15},{8,0},{9,1},... | collective-permute-start | bytes 7077896 | tf_op jit(solution)/shard_map/sum_up1_cores/ppermute | solution.py:1026
  266.5 17.3 %collective-permute-start.40 = (bf16[2,4,96,384]{3,2,1,0:T(8,128)(2,1)}, bf16[2,4,96,384]{3,2,1,0:T(8,128)(2,1)S(1)}, u32[]{:S(2)}, u32[]{:S(2)}) collective-permute-start(bf16[2,4,96,384]{3,2,1,0:T(8,128)(2,1)} %get-tuple-element.276), channel_id=1, source_target_pairs={{0,16},{1,17},{2,18},{3,19},{4,20},{5,21},{6,22},{7,23},{8,24},{9,... | collective-permute-start | bytes 1769480 | tf_op jit(solution)/shard_map/sum_down1_first/ppermute | solution.py:1026
  267.1 16.8 %collective-permute-start.39 = (bf16[2,4,96,384]{3,2,1,0:T(8,128)(2,1)}, bf16[2,4,96,384]{3,2,1,0:T(8,128)(2,1)}, u32[]{:S(2)}, u32[]{:S(2)}) collective-permute-start(bf16[2,4,96,384]{3,2,1,0:T(8,128)(2,1)} %get-tuple-element.270.refs_8_), channel_id=1, source_target_pairs={{0,1},{1,0},{2,3},{3,2},{4,5},{5,4},{6,7},{7,6},{8,9},{9,8},{10,11... | collective-permute-start | bytes 1769480 | tf_op jit(solution)/shard_map/sum_down1_first/ppermute | solution.py:1026
  290.8 26.3 %collective-permute-start.45 = (bf16[4,96,384]{2,1,0:T(8,128)(2,1)}, bf16[4,96,384]{2,1,0:T(8,128)(2,1)S(1)}, u32[]{:S(2)}, u32[]{:S(2)}) collective-permute-start(bf16[4,96,384]{2,1,0:T(8,128)(2,1)} %get-tuple-element.291), channel_id=1, source_target_pairs={{0,1},{1,0},{2,3},{3,2},{4,5},{5,4},{6,7},{7,6},{8,9},{9,8},{10,11... | collective-permute-start | bytes 884744 | tf_op jit(solution)/shard_map/sum_down1_second/ppermute | solution.py:1026
  291.4 25.8 %collective-permute-start.44 = (bf16[4,96,384]{2,1,0:T(8,128)(2,1)}, bf16[4,96,384]{2,1,0:T(8,128)(2,1)S(1)}, u32[]{:S(2)}, u32[]{:S(2)}) collective-permute-start(bf16[4,96,384]{2,1,0:T(8,128)(2,1)} %get-tuple-element.283.refs_0_), channel_id=1, source_target_pairs={{0,16},{1,17},{2,18},{3,19},{4,20},{5,21},{6,22},{7,23},{8,24},{9,... | collective-permute-start | bytes 884744 | tf_op jit(solution)/shard_map/sum_down1_second/ppermute | solution.py:1026
  292.9 19.4 %collective-permute-start.42 = (bf16[2,4,96,384]{3,2,1,0:T(8,128)(2,1)}, bf16[2,4,96,384]{3,2,1,0:T(8,128)(2,1)}, u32[]{:S(2)}, u32[]{:S(2)}) collective-permute-start(bf16[2,4,96,384]{3,2,1,0:T(8,128)(2,1)} %get-tuple-element.287), channel_id=1, source_target_pairs={{0,1},{1,0},{2,3},{3,2},{4,5},{5,4},{6,7},{7,6},{8,9},{9,8},{10,11... | collective-permute-start | bytes 1769480 | tf_op jit(solution)/shard_map/sum_up1_first/ppermute | solution.py:1026
  294.3 18.2 %collective-permute-start.43 = (bf16[2,4,96,384]{3,2,1,0:T(8,128)(2,1)}, bf16[2,4,96,384]{3,2,1,0:T(8,128)(2,1)}, u32[]{:S(2)}, u32[]{:S(2)}) collective-permute-start(bf16[2,4,96,384]{3,2,1,0:T(8,128)(2,1)} %get-tuple-element.288), channel_id=1, source_target_pairs={{0,16},{1,17},{2,18},{3,19},{4,20},{5,21},{6,22},{7,23},{8,24},{9,... | collective-permute-start | bytes 1769480 | tf_op jit(solution)/shard_map/sum_up1_first/ppermute | solution.py:1026
  318.0 19.8 %collective-permute-start.48 = (bf16[4,96,384]{2,1,0:T(8,128)(2,1)}, bf16[4,96,384]{2,1,0:T(8,128)(2,1)S(1)}, u32[]{:S(2)}, u32[]{:S(2)}) collective-permute-start(bf16[4,96,384]{2,1,0:T(8,128)(2,1)} %get-tuple-element.302), channel_id=1, source_target_pairs={{0,1},{1,0},{2,3},{3,2},{4,5},{5,4},{6,7},{7,6},{8,9},{9,8},{10,11... | collective-permute-start | bytes 884744 | tf_op jit(solution)/shard_map/sum_up1_second/ppermute | solution.py:1026
  319.5 18.4 %collective-permute-start.47 = (bf16[4,96,384]{2,1,0:T(8,128)(2,1)}, bf16[4,96,384]{2,1,0:T(8,128)(2,1)S(1)}, u32[]{:S(2)}, u32[]{:S(2)}) collective-permute-start(bf16[4,96,384]{2,1,0:T(8,128)(2,1)} %get-tuple-element.292.refs_0_), channel_id=1, source_target_pairs={{0,16},{1,17},{2,18},{3,19},{4,20},{5,21},{6,22},{7,23},{8,24},{9,... | collective-permute-start | bytes 884744 | tf_op jit(solution)/shard_map/sum_up1_second/ppermute | solution.py:1026
  338.6 21.0 %collective-permute-start.50 = (bf16[2,4,112,384]{3,2,1,0:T(8,128)(2,1)}, bf16[2,4,112,384]{3,2,1,0:T(8,128)(2,1)S(1)}, u32[]{:S(2)}, u32[]{:S(2)}) collective-permute-start(bf16[2,4,112,384]{3,2,1,0:T(8,128)(2,1)} %get-tuple-element.307), channel_id=1, source_target_pairs={{0,16},{1,17},{2,18},{3,19},{4,20},{5,21},{6,22},{7,23},{8,24},{9,... | collective-permute-start | bytes 2064392 | tf_op jit(solution)/shard_map/sum_first1_first/ppermute | solution.py:1026
  339.2 20.5 %collective-permute-start.49 = (bf16[2,4,112,384]{3,2,1,0:T(8,128)(2,1)}, bf16[2,4,112,384]{3,2,1,0:T(8,128)(2,1)}, u32[]{:S(2)}, u32[]{:S(2)}) collective-permute-start(bf16[2,4,112,384]{3,2,1,0:T(8,128)(2,1)} %get-tuple-element.303.refs_8_), channel_id=1, source_target_pairs={{0,1},{1,0},{2,3},{3,2},{4,5},{5,4},{6,7},{7,6},{8,9},{9,8},{10,11... | collective-permute-start | bytes 2064392 | tf_op jit(solution)/shard_map/sum_first1_first/ppermute | solution.py:1026
  339.8 23.6 %collective-permute-start.51 = (bf16[2,2,2,4,96,384]{5,4,3,2,1,0:T(8,128)(2,1)}, bf16[2,2,2,4,96,384]{5,4,3,2,1,0:T(8,128)(2,1)}, u32[]{:S(2)}, u32[]{:S(2)}) collective-permute-start(bf16[2,2,2,4,96,384]{5,4,3,2,1,0:T(8,128)(2,1)} %get-tuple-element.311), channel_id=1, source_target_pairs={{0,8},{1,9},{2,10},{3,11},{4,12},{5,13},{6,14},{7,15},{8,0},{9,1},... | collective-permute-start | bytes 7077896 | tf_op jit(solution)/shard_map/sum_down0_cores/ppermute | solution.py:1026
  366.9 36.9 %collective-permute-start.52 = (bf16[2,2,2,4,96,384]{5,4,3,2,1,0:T(8,128)(2,1)}, bf16[2,2,2,4,96,384]{5,4,3,2,1,0:T(8,128)(2,1)}, u32[]{:S(2)}, u32[]{:S(2)}) collective-permute-start(bf16[2,2,2,4,96,384]{5,4,3,2,1,0:T(8,128)(2,1)} %get-tuple-element.317), channel_id=1, source_target_pairs={{0,8},{1,9},{2,10},{3,11},{4,12},{5,13},{6,14},{7,15},{8,0},{9,1},... | collective-permute-start | bytes 7077896 | tf_op jit(solution)/shard_map/sum_up0_cores/ppermute | solution.py:1026
  374.3 102.6 %reduce-scatter.6.cloned.1.call-start = ((), (), s32[]{:S(2)}) async-start(), calls=%async_computation.4 | async-start | bytes 860160 | tf_op jit(solution)/shard_map/share_first1/reduce_scatter | solution.py:1121
  374.3 32.5 %collective-permute-start.56 = (bf16[4,112,384]{2,1,0:T(8,128)(2,1)}, bf16[4,112,384]{2,1,0:T(8,128)(2,1)S(1)}, u32[]{:S(2)}, u32[]{:S(2)}) collective-permute-start(bf16[4,112,384]{2,1,0:T(8,128)(2,1)} %get-tuple-element.324), channel_id=1, source_target_pairs={{0,1},{1,0},{2,3},{3,2},{4,5},{5,4},{6,7},{7,6},{8,9},{9,8},{10,11... | collective-permute-start | bytes 1032200 | tf_op jit(solution)/shard_map/sum_first1_second/ppermute | solution.py:1026
  375.9 31.0 %collective-permute-start.55 = (bf16[4,112,384]{2,1,0:T(8,128)(2,1)}, bf16[4,112,384]{2,1,0:T(8,128)(2,1)S(1)}, u32[]{:S(2)}, u32[]{:S(2)}) collective-permute-start(bf16[4,112,384]{2,1,0:T(8,128)(2,1)} %get-tuple-element.315.refs_8_), channel_id=1, source_target_pairs={{0,16},{1,17},{2,18},{3,19},{4,20},{5,21},{6,22},{7,23},{8,24},{9,... | collective-permute-start | bytes 1032200 | tf_op jit(solution)/shard_map/sum_first1_second/ppermute | solution.py:1026
  377.3 20.5 %collective-permute-start.53 = (bf16[2,4,96,384]{3,2,1,0:T(8,128)(2,1)}, bf16[2,4,96,384]{3,2,1,0:T(8,128)(2,1)}, u32[]{:S(2)}, u32[]{:S(2)}) collective-permute-start(bf16[2,4,96,384]{3,2,1,0:T(8,128)(2,1)} %get-tuple-element.318), channel_id=1, source_target_pairs={{0,1},{1,0},{2,3},{3,2},{4,5},{5,4},{6,7},{7,6},{8,9},{9,8},{10,11... | collective-permute-start | bytes 1769480 | tf_op jit(solution)/shard_map/sum_down0_first/ppermute | solution.py:1026
  377.9 21.1 %collective-permute-start.54 = (bf16[2,4,96,384]{3,2,1,0:T(8,128)(2,1)}, bf16[2,4,96,384]{3,2,1,0:T(8,128)(2,1)}, u32[]{:S(2)}, u32[]{:S(2)}) collective-permute-start(bf16[2,4,96,384]{3,2,1,0:T(8,128)(2,1)} %get-tuple-element.319), channel_id=1, source_target_pairs={{0,16},{1,17},{2,18},{3,19},{4,20},{5,21},{6,22},{7,23},{8,24},{9,... | collective-permute-start | bytes 1769480 | tf_op jit(solution)/shard_map/sum_down0_first/ppermute | solution.py:1026
  407.7 32.5 %collective-permute-start.61 = (bf16[4,96,384]{2,1,0:T(8,128)(2,1)}, bf16[4,96,384]{2,1,0:T(8,128)(2,1)S(1)}, u32[]{:S(2)}, u32[]{:S(2)}) collective-permute-start(bf16[4,96,384]{2,1,0:T(8,128)(2,1)} %get-tuple-element.337), channel_id=1, source_target_pairs={{0,1},{1,0},{2,3},{3,2},{4,5},{5,4},{6,7},{7,6},{8,9},{9,8},{10,11... | collective-permute-start | bytes 884744 | tf_op jit(solution)/shard_map/sum_down0_second/ppermute | solution.py:1026
  408.3 32.0 %collective-permute-start.60 = (bf16[4,96,384]{2,1,0:T(8,128)(2,1)}, bf16[4,96,384]{2,1,0:T(8,128)(2,1)S(1)}, u32[]{:S(2)}, u32[]{:S(2)}) collective-permute-start(bf16[4,96,384]{2,1,0:T(8,128)(2,1)} %get-tuple-element.334.refs_0_), channel_id=1, source_target_pairs={{0,16},{1,17},{2,18},{3,19},{4,20},{5,21},{6,22},{7,23},{8,24},{9,... | collective-permute-start | bytes 884744 | tf_op jit(solution)/shard_map/sum_down0_second/ppermute | solution.py:1026
  409.7 30.5 %collective-permute-start.59 = (bf16[4,96,384]{2,1,0:T(8,128)(2,1)}, bf16[4,96,384]{2,1,0:T(8,128)(2,1)S(1)}, u32[]{:S(2)}, u32[]{:S(2)}) collective-permute-start(bf16[4,96,384]{2,1,0:T(8,128)(2,1)} %get-tuple-element.336.refs_3_), channel_id=1, source_target_pairs={{0,16},{1,17},{2,18},{3,19},{4,20},{5,21},{6,22},{7,23},{8,24},{9,... | collective-permute-start | bytes 884744 | tf_op jit(solution)/shard_map/share_second1/ppermute | solution.py:1026
  410.3 18.6 %collective-permute-start.57 = (bf16[2,4,96,384]{3,2,1,0:T(8,128)(2,1)}, bf16[2,4,96,384]{3,2,1,0:T(8,128)(2,1)}, u32[]{:S(2)}, u32[]{:S(2)}) collective-permute-start(bf16[2,4,96,384]{3,2,1,0:T(8,128)(2,1)} %get-tuple-element.325), channel_id=1, source_target_pairs={{0,1},{1,0},{2,3},{3,2},{4,5},{5,4},{6,7},{7,6},{8,9},{9,8},{10,11... | collective-permute-start | bytes 1769480 | tf_op jit(solution)/shard_map/sum_up0_first/ppermute | solution.py:1026
  411.7 23.9 %collective-permute-start.58 = (bf16[2,4,96,384]{3,2,1,0:T(8,128)(2,1)}, bf16[2,4,96,384]{3,2,1,0:T(8,128)(2,1)}, u32[]{:S(2)}, u32[]{:S(2)}) collective-permute-start(bf16[2,4,96,384]{3,2,1,0:T(8,128)(2,1)} %get-tuple-element.326), channel_id=1, source_target_pairs={{0,16},{1,17},{2,18},{3,19},{4,20},{5,21},{6,22},{7,23},{8,24},{9,... | collective-permute-start | bytes 1769480 | tf_op jit(solution)/shard_map/sum_up0_first/ppermute | solution.py:1026
  441.2 30.8 %collective-permute-start.62 = (bf16[2,2,2,4,112,384]{5,4,3,2,1,0:T(8,128)(2,1)}, bf16[2,2,2,4,112,384]{5,4,3,2,1,0:T(8,128)(2,1)}, u32[]{:S(2)}, u32[]{:S(2)}) collective-permute-start(bf16[2,2,2,4,112,384]{5,4,3,2,1,0:T(8,128)(2,1)} %get-tuple-element.340), channel_id=1, source_target_pairs={{0,8},{1,9},{2,10},{3,11},{4,12},{5,13},{6,14},{7,15},{8,0},{9,1},... | collective-permute-start | bytes 8257544 | tf_op jit(solution)/shard_map/sum_first0_cores/ppermute | solution.py:1026
  446.4 67.3 %reduce-scatter.8.cloned.1.call-start = ((), (), s32[]{:S(2)}) async-start(), calls=%async_computation.5 | async-start | bytes 1474560 | tf_op jit(solution)/shard_map/share_second0/reduce_scatter | solution.py:1121
  477.6 16.7 %collective-permute-start.66 = (bf16[2,4,112,384]{3,2,1,0:T(8,128)(2,1)}, bf16[2,4,112,384]{3,2,1,0:T(8,128)(2,1)S(1)}, u32[]{:S(2)}, u32[]{:S(2)}) collective-permute-start(bf16[2,4,112,384]{3,2,1,0:T(8,128)(2,1)} %get-tuple-element.345), channel_id=1, source_target_pairs={{0,16},{1,17},{2,18},{3,19},{4,20},{5,21},{6,22},{7,23},{8,24},{9,... | collective-permute-start | bytes 2064392 | tf_op jit(solution)/shard_map/sum_first0_first/ppermute | solution.py:1026
  479.1 18.2 %collective-permute-start.67 = (bf16[2,112,384]{2,1,0:T(8,128)(2,1)}, bf16[2,112,384]{2,1,0:T(8,128)(2,1)S(1)}, u32[]{:S(2)}, u32[]{:S(2)}) collective-permute-start(bf16[2,112,384]{2,1,0:T(8,128)(2,1)} %get-tuple-element.348.refs_2_), channel_id=1, source_target_pairs={{0,16},{1,17},{2,18},{3,19},{4,20},{5,21},{6,22},{7,23},{8,24},{9,... | collective-permute-start | bytes 516104 | tf_op jit(solution)/shard_map/share_first1/ppermute | solution.py:1026
  (177 other events, 819.7 us)
Sparse Core Ops, SparseCore 0:
  74.7 39.1 all-gather.2
  374.4 28.9 reduce-scatter.3
  446.6 22.0 reduce-scatter.5
  471.5 28.0 reduce-scatter.7

commit v3 on v2

v3 whole, which is shorter than its diff:
```python
import functools

import jax
import jax.numpy as jnp
from jax import lax
from jax.experimental import pallas as pl
from jax.experimental.pallas import tpu as pltpu
from jax.sharding import PartitionSpec as P

HEADS = 12
HEAD_DIM = 64
LAYERS = 2
TEXT = 128
KEYS = 256
WIDE = 768
HALF = WIDE // 2
PAIR = 2 * HEAD_DIM
PAIRS = HEADS // 2
EPSILON = 1e-12
MASKED = -1000000000.0
AXES = ("rep", "fsdp")
COST = 1.15e9
SMALL = 16
VMEM_LIMIT = 64 * 1024 * 1024
SMALL_LIMIT = VMEM_LIMIT


def low(value):
    return value.astype(jnp.bfloat16)


def full(value):
    return value.astype(jnp.float32)


def mm(left, right):
    return jnp.dot(left, right, preferred_element_type=jnp.float32)


def mm_t(left, right):
    return lax.dot_general(
        left, right, (((1,), (1,)), ((), ())), preferred_element_type=jnp.float32
    )


def t_mm(left, right):
    return lax.dot_general(
        left, right, (((0,), (0,)), ((), ())), preferred_element_type=jnp.float32
    )


def flip(at, by):
    return 1 - at if by else at


class Place:
    def __init__(self, pos_ref):
        self.core, self.side = pos_ref[0], pos_ref[1]
        self.row, self.level = pos_ref[2], pos_ref[3]

    def shard(self, level, far_row):
        return level * 2 + flip(self.row, far_row)


def half_lanes(at):
    return pl.ds(pl.multiple_of(at * HALF, HALF), HALF)


def part_of(arrays, path, far_core, far_side, far_row):
    arrays = arrays[5 * far_core : 5 * far_core + 5]
    if far_side and far_row:
        return arrays[3 + path]
    return arrays[2 * far_side + far_row].at[path]


def load_unit(place, depth, arrays, unit, whole, sems, by_rows):
    rows = pl.ds(0, whole.shape[2])
    for far_side in range(2):
        for path in range(2):
            block = flip(place.side, far_side) * 2 + path
            for far_core in range(2):
                lanes = half_lanes(flip(place.core, far_core))
                for far_row in range(2):
                    part = part_of(arrays, path, far_core, far_side, far_row)
                    for level in range(depth):
                        shard = place.shard(level, far_row)
                        at = (shard, block) if by_rows else (block, shard)
                        sem = sems.at[level * 4 // depth if by_rows else block]
                        target = whole.at[at[0], at[1], :, lanes]
                        pltpu.make_async_copy(part.at[level, unit, rows], target, sem).start()


def load_block(place, depth, block, arrays, whole, sem):
    path = block % 2
    rows = pl.ds(0, whole.shape[1])
    needed_side = place.side if block // 2 == 0 else 1 - place.side
    for far_side in range(2):

        @pl.when(needed_side == far_side)
        def _():
            for far_core in range(2):
                lanes = half_lanes(flip(place.core, far_core))
                for far_row in range(2):
                    part = part_of(arrays, path, far_core, far_side, far_row)
                    for level in range(depth):
                        target = whole.at[place.shard(level, far_row), :, lanes]
                        pltpu.make_async_copy(part.at[level, 0, rows], target, sem).start()


def wait_all(ref, sem):
    pltpu.make_async_copy(ref, ref, sem).wait()


def either(choice, one, other):
    return other + choice * (one - other)


def sum_place(out, block, far_row, far_side, level):
    path = block % 2
    return out.at[path, either(path, far_side, far_row), either(path, far_row, far_side), level]


def side_distance(place, block):
    return either(place.side, 1 - block // 2, block // 2)


def store_columns(place, block, held, outs, sem):
    rows = pl.ds(0, held.shape[1])
    far_side = side_distance(place, block)
    for far_core, out in enumerate(outs):
        core = flip(place.core, far_core)
        for far_row in range(2):
            for level in range(held.shape[0] // 2):
                source = held.at[place.shard(level, far_row), :, half_lanes(core)]
                target = sum_place(out, block, far_row, far_side, level).at[rows]
                pltpu.make_async_copy(source, target, sem).start()


def store_rows(place, tile, held, outs, sem):
    count = held.shape[0]
    for inner in range(count):
        far_row = either(place.row, 1 - inner % 2, inner % 2)
        level = (tile * count + inner) // 2
        for block in range(4):
            far_side = side_distance(place, block)
            for far_core, out in enumerate(outs):
                source = held.at[inner, block, :, half_lanes(flip(place.core, far_core))]
                target = sum_place(out, block, far_row, far_side, level)
                pltpu.make_async_copy(source, target, sem).start()


def copy(source, target, sem):
    pltpu.make_async_copy(source, target, sem).start()


def chunks(rows):
    edges = [rows // 16 * at // 4 * 16 for at in range(4)] + [rows]
    return [(start, end - start) for start, end in zip(edges, edges[1:])]


def normalize(value):
    centered = value - jnp.mean(value, axis=-1, keepdims=True)
    scale = lax.rsqrt(jnp.mean(centered * centered, axis=-1, keepdims=True) + EPSILON)
    return centered * scale, scale


def norm_backward(grad, hat, scale, gain):
    direct = grad * gain
    return (
        direct
        - jnp.mean(direct, axis=-1, keepdims=True)
        - hat * jnp.mean(direct * hat, axis=-1, keepdims=True)
    ) * scale


def gelu_and_slope(value):
    size = jnp.abs(value) * 0.7071067811865476
    t = 1.0 / (1.0 + 0.3275911 * size)
    series = t * (
        0.127414796
        + t * (-0.142248368 + t * (0.7107068705 + t * (-0.7265760135 + t * 0.5307027145)))
    )
    bell = jnp.exp(-0.5 * value * value)
    tail = series * bell
    below = jnp.where(value >= 0, 1.0 - tail, tail)
    return value * below, below + value * bell * 0.3989422804014327


def head_masks(value, lane):
    none = jnp.zeros_like(value)
    return jnp.concatenate(
        [jnp.where(lane < HEAD_DIM, value, none), jnp.where(lane < HEAD_DIM, none, value)], 0
    )


def side_by_side(ref, block):
    return jnp.concatenate([ref[block * PAIRS + pair] for pair in range(PAIRS)], 1)


def attention_forward(depth, seqs, extra, pos_ref, counts_ref, x_ref, params_ref, *refs):
    parts, refs = refs[:10], refs[10 + extra :]
    first_ref, first_low_ref, hat_ref, scale_ref, ctx_ref, qkv_ref, probs_ref = refs[:7]
    weight, held, weight_sem, held_sem = refs[7:]
    place = Place(pos_ref)
    load_unit(place, depth, parts, 0, weight, weight_sem, False)
    tokens = x_ref.shape[0]
    slots = tokens // seqs
    x_low = low(x_ref[...])

    for block in range(3):
        wait_all(weight.at[block], weight_sem.at[block])

    def project(block, carry):
        out = mm(x_low, weight[block].reshape(WIDE, WIDE))
        bias = params_ref[pl.ds(1 + block // 2, 1), :WIDE]
        out = low(out + jnp.where(block == 1, jnp.zeros_like(bias), bias))
        for pair in range(PAIRS):
            qkv_ref[block * PAIRS + pair] = out[:, pair * PAIR : (pair + 1) * PAIR]
        return carry

    lax.fori_loop(0, 3, project, 0)
    lane = lax.broadcasted_iota(jnp.int32, (KEYS, PAIR), 1)
    key = lax.broadcasted_iota(jnp.int32, (slots, KEYS), 1)

    def pair_step(step, carry):
        seq, pair = step // PAIRS, lax.rem(step, PAIRS)
        rows = pl.ds(pl.multiple_of(seq * slots, 16), slots)
        key_rows = pl.ds(pl.multiple_of(seq * slots, 16), KEYS)
        valid = key < TEXT + counts_ref[seq]
        q = qkv_ref[pair, rows, :] * jnp.bfloat16(HEAD_DIM**-0.5)
        scores = mm_t(q, head_masks(qkv_ref[PAIRS + pair, key_rows, :], lane))
        halves = []
        for half in range(2):
            part = jnp.where(valid, scores[:, half * KEYS : (half + 1) * KEYS], MASKED)
            part = jnp.exp(part - jnp.max(part, axis=-1, keepdims=True))
            halves.append(low(part * (1.0 / jnp.sum(part, axis=-1, keepdims=True))))
        probs = jnp.concatenate(halves, 1)
        held[seq, pair] = probs
        copy(held.at[seq, pair], probs_ref.at[seq, pair], held_sem)
        ctx_ref[pair, rows, :] = low(mm(probs, head_masks(qkv_ref[2 * PAIRS + pair, key_rows, :], lane)))
        return carry

    lax.fori_loop(0, seqs * PAIRS, pair_step, 0, unroll=2)
    wait_all(weight.at[3], weight_sem.at[3])
    first_ref[...] = mm(side_by_side(ctx_ref, 0), weight[3].reshape(WIDE, WIDE))
    for start, size in chunks(tokens):
        rows = pl.ds(start, size)
        hat, scale = normalize(full(x_ref[rows, :]) + (first_ref[rows, :] + params_ref[3:4, :WIDE]))
        hat_ref[rows, :] = hat
        scale_ref[rows, :] = jnp.broadcast_to(scale, (size, 128))
        first = hat * params_ref[7:8, :WIDE] + params_ref[4:5, :WIDE]
        first_ref[rows, :] = first
        first_low_ref[rows, :] = low(first)
    wait_all(held, held_sem)


def mlp_forward(depth, extra, pos_ref, first_ref, params_ref, *refs):
    parts, refs = refs[:10], refs[10 + extra :]
    out_ref, out_low_ref, hat_ref, scale_ref, act_ref, slope_ref = refs[:6]
    up, down, pre, first_low, act, slope, up_sem, down_sem, act_sem, slope_sem = refs[6:]
    place = Place(pos_ref)
    load_unit(place, depth, parts, 0, up, up_sem, False)
    load_unit(place, depth, parts, 1, down, down_sem, True)
    tokens = first_ref.shape[0]
    half = tokens // 2
    first_low[...] = low(first_ref[...])
    shards = down.shape[0] // 4
    out_ref[...] = first_ref[...] + params_ref[5:6, :WIDE]
    act[3, half:, :] = jnp.zeros((half, WIDE), BF16)
    for tile in range(4):
        wait_all(up.at[tile], up_sem.at[tile])
    pre[0] = mm(first_low[...], up[0].reshape(WIDE, WIDE))
    for tile in range(4):
        wait_all(down.at[pl.ds(tile * shards, shards)], down_sem.at[tile])

    def half_rows(step):
        return pl.ds(pl.multiple_of(lax.rem(step, 2) * half, 16), half)

    def below(step):
        tile, rows = step // 2, half_rows(step)
        weight = down[pl.ds(tile * shards, shards)].reshape(WIDE, WIDE)
        out_ref[rows, :] += mm(act[tile, rows, :], weight)

    def half_step(step, carry):
        tile, rows = step // 2, half_rows(step)
        slot, later = lax.rem(tile, 2), lax.rem(tile + 1, 4)
        bias = params_ref[0:1, pl.ds(pl.multiple_of(tile * WIDE, WIDE), WIDE)]
        below(lax.rem(step + 7, 8))
        pre[1 - slot, rows, :] = mm(first_low[rows, :], up[later].reshape(WIDE, WIDE))
        gelu, rise = gelu_and_slope(pre[slot, rows, :] + bias)
        act[tile, rows, :] = low(gelu)
        slope[tile, rows, :] = low(rise)
        copy(slope.at[tile, rows], slope_ref.at[tile, rows], slope_sem)
        copy(act.at[tile, rows], act_ref.at[tile, rows], act_sem)
        return carry

    lax.fori_loop(0, 8, half_step, 0)
    below(7)
    for start, size in chunks(tokens):
        rows = pl.ds(start, size)
        hat, scale = normalize(out_ref[rows, :])
        hat_ref[rows, :] = hat
        scale_ref[rows, :] = jnp.broadcast_to(scale, (size, 128))
        out = hat * params_ref[8:9, :WIDE] + params_ref[6:7, :WIDE]
        out_ref[rows, :] = out
        out_low_ref[rows, :] = low(out)
    wait_all(slope, slope_sem)
    wait_all(act, act_sem)


def load_rows(pairs, sem):
    for at, (start, size) in enumerate(chunks(pairs[0][0].shape[0])):
        for source, target in pairs:
            rows = pl.ds(start, size)
            copy(source.at[rows], target.at[rows], sem.at[at])


def norm_step(grad, hat, scale, gain, out, out_ref, sums_ref, waits, sem, out_sem):
    sums = [0.0, 0.0, 0.0]
    for at, (start, size) in enumerate(chunks(grad.shape[0])):
        rows = pl.ds(start, size)
        for array in waits:
            wait_all(array.at[rows], sem.at[at])
        value, hat_rows = full(grad[rows, :]), hat[rows, :]
        grad_in = norm_backward(value, hat_rows, scale[rows, :][:, :1], gain)
        out[rows, :] = grad_in
        copy(out.at[rows], out_ref.at[rows], out_sem)
        for number, part in enumerate((value * hat_rows, value, full(low(grad_in)))):
            sums[number] += jnp.sum(part, axis=0, keepdims=True)
    sums_ref[...] = jnp.zeros_like(sums_ref)
    for number in range(3):
        sums_ref[number : number + 1, :] = sums[number]


def down_backward(depth, extra, pos_ref, params_ref, grad_ref, hat_ref, scale_ref, act_ref, *refs):
    second_ref, sums_ref, near_ref, far_ref = refs[extra : extra + 4]
    grad, hat, scale, second, act, held, row_sem, act_sem, out_sem, held_sem = refs[extra + 4 :]
    place = Place(pos_ref)
    load_rows([(grad_ref, grad), (hat_ref, hat), (scale_ref, scale)], row_sem)
    for tile in range(4):
        copy(act_ref.at[tile], act.at[tile], act_sem.at[tile])
    norm_step(
        grad, hat, scale, params_ref[8:9, :WIDE], second, second_ref, sums_ref, (grad, hat, scale), row_sem, out_sem
    )
    grad_low = low(second[...])
    for tile in range(4):
        wait_all(act.at[tile], act_sem.at[tile])

    def tile_step(tile, carry):
        held[tile] = low(t_mm(act[tile], grad_low)).reshape(held.shape[1:])
        store_rows(place, tile, held.at[tile], (near_ref, far_ref), held_sem)
        return carry

    lax.fori_loop(0, 4, tile_step, 0)
    wait_all(second, out_sem)
    wait_all(held, held_sem)


def up_backward(
    depth, extra, pos_ref, params_ref, second_ref, slope_ref, first_low_ref, hat_ref, scale_ref, *refs
):
    parts, refs = refs[:10], refs[10 + extra :]
    first_in_ref, sums_ref, up_grad_ref, near_ref, far_ref = refs[:5]
    up, down, slope, total, first_low, hat, scale, held, *sems = refs[5:]
    up_sem, down_sem, slope_sem, second_sem, first_sem, row_sem, out_sem, held_sem = sems
    place = Place(pos_ref)
    copy(second_ref, total, second_sem)
    load_unit(place, depth, parts, 1, down, down_sem, True)
    for tile in range(4):
        copy(slope_ref.at[tile], slope.at[tile], slope_sem.at[tile])
    copy(first_low_ref, first_low, first_sem)
    load_unit(place, depth, parts, 0, up, up_sem, False)
    load_rows([(hat_ref, hat), (scale_ref, scale)], row_sem)
    shards = down.shape[0] // 4
    wait_all(total, second_sem)
    grad_low = low(total[...])
    wait_all(first_low, first_sem)
    for tile in range(4):
        wait_all(down.at[pl.ds(tile * shards, shards)], down_sem.at[tile])
        wait_all(slope.at[tile], slope_sem.at[tile])
        wait_all(up.at[tile], up_sem.at[tile])

    def tile_step(tile, carry):
        below = pl.ds(tile * shards, shards)
        grad = mm_t(grad_low, down[below].reshape(WIDE, WIDE))
        grad = low(grad * full(slope[tile]))
        up_grad_ref[:, pl.ds(pl.multiple_of(tile * WIDE, WIDE), WIDE)] = jnp.sum(
            full(grad), axis=0, keepdims=True
        )
        held[tile] = low(t_mm(first_low[...], grad)).reshape(held.shape[1:])
        total[...] += mm_t(grad, up[tile].reshape(WIDE, WIDE))
        store_columns(place, tile, held.at[tile], (near_ref, far_ref), held_sem)
        return carry

    lax.fori_loop(0, 4, tile_step, 0)
    norm_step(
        total, hat, scale, params_ref[7:8, :WIDE], total, first_in_ref, sums_ref, (hat, scale), row_sem, out_sem
    )
    wait_all(total, out_sem)
    wait_all(held, held_sem)


def attention_backward(depth, seqs, extra, pos_ref, grad_ref, qkv_ref, probs_ref, *refs):
    parts, refs = refs[:10], refs[10 + extra :]
    grads_ref = refs[0]
    weight, grad, qkv, probs, ctx_grad, grads, weight_sem, grad_sem, qkv_sem, probs_sem, out_sem = refs[1:]
    place = Place(pos_ref)
    copy(grad_ref, grad, grad_sem)
    load_block(place, depth, 3, parts, weight, weight_sem)
    copy(qkv_ref, qkv, qkv_sem)
    copy(probs_ref, probs, probs_sem)
    tokens = grad.shape[0]
    slots = tokens // seqs
    wait_all(grad, grad_sem)
    wait_all(weight, weight_sem)
    from_out = low(mm_t(low(grad[...]), weight[...].reshape(WIDE, WIDE)))
    for pair in range(PAIRS):
        ctx_grad[pair] = from_out[:, pair * PAIR : (pair + 1) * PAIR]
    wait_all(qkv, qkv_sem)
    wait_all(probs, probs_sem)
    lane = lax.broadcasted_iota(jnp.int32, (KEYS, PAIR), 1)

    def pair_step(step, carry):
        seq, pair = step // PAIRS, lax.rem(step, PAIRS)
        start = pl.multiple_of(seq * slots, 16)
        rows, key_rows = pl.ds(start, slots), pl.ds(start, KEYS)
        q = qkv[pair, rows, :]
        out_grad = ctx_grad[pair, rows, :]
        weights = probs[seq, pair]
        probs_grad = mm_t(out_grad, head_masks(qkv[2 * PAIRS + pair, key_rows, :], lane))
        halves = []
        for half in range(2):
            lanes = slice(half * KEYS, (half + 1) * KEYS)
            weight_part, grad_part = full(weights[:, lanes]), probs_grad[:, lanes]
            dot = jnp.sum(weight_part * grad_part, axis=-1, keepdims=True)
            halves.append(low(weight_part * (grad_part - dot)))
        scores_grad = jnp.concatenate(halves, 1)
        q_grad = mm(scores_grad, head_masks(qkv[PAIRS + pair, key_rows, :], lane)) * HEAD_DIM**-0.5
        grads[pair, rows, :] = low(q_grad)
        k_grad = t_mm(q, scores_grad) * HEAD_DIM**-0.5
        v_grad = t_mm(out_grad, weights)
        for at, value in ((PAIRS, k_grad), (2 * PAIRS, v_grad)):
            value = jnp.concatenate([value[:HEAD_DIM, :KEYS], value[HEAD_DIM:, KEYS:]], 0)
            grads[at + pair, key_rows, :] = low(value.T)
            grads[at + pair, pl.ds(pl.multiple_of(start + KEYS, 16), slots - KEYS), :] = jnp.zeros(
                (slots - KEYS, PAIR), BF16
            )
        for at in range(3):
            copy(grads.at[at * PAIRS + pair, rows], grads_ref.at[at * PAIRS + pair, rows], out_sem)
        return carry

    lax.fori_loop(0, seqs * PAIRS, pair_step, 0, unroll=2)
    wait_all(grads, out_sem)


def qkv_weights(
    depth, up_size, width, extra, pos_ref, down_sums_ref, up_sums_ref, up_bias_ref, grad_ref, grads_ref, ctx_ref, x_ref,
    *refs,
):
    outs, refs = refs[extra : extra + 2], refs[extra + 2 :]
    grad, grads, ctx, x_low, held, sums, block_rows, small, grad_sem, grads_sem, ctx_sem, x_sem, held_sem, small_sem = refs
    place = Place(pos_ref)
    copy(x_ref, x_low, x_sem)
    for block in range(3):
        panels = pl.ds(block * PAIRS, PAIRS)
        copy(grads_ref.at[panels], grads.at[panels], grads_sem.at[block])
    copy(ctx_ref, ctx, ctx_sem)
    copy(grad_ref, grad, grad_sem)
    wait_all(x_low, x_sem)
    for block in range(3):
        wait_all(grads.at[pl.ds(block * PAIRS, PAIRS)], grads_sem.at[block])

    def block_step(block, carry):
        part = side_by_side(grads, block)
        sums[pl.ds(block, 1), :] = jnp.sum(full(part), axis=0, keepdims=True)
        held[block] = low(t_mm(x_low[...], part)).reshape(held.shape[1:])
        store_columns(place, block, held.at[block], outs, held_sem)
        return carry

    lax.fori_loop(0, 3, block_step, 0)
    sums[1:2, :] = sums[2:3, :]
    block_rows[...] = jnp.zeros_like(block_rows)
    for shard in range(2 * depth):
        lanes = slice(shard * width, (shard + 1) * width)
        block_rows[0:1, :up_size] = up_bias_ref[:, shard * up_size : (shard + 1) * up_size]
        block_rows[1:3, :width] = sums[0:2, lanes]
        for row, (ref, at) in enumerate(
            ((up_sums_ref, 2), (up_sums_ref, 1), (down_sums_ref, 2), (down_sums_ref, 1), (up_sums_ref, 0), (down_sums_ref, 0))
        ):
            block_rows[3 + row : 4 + row, :width] = ref[at : at + 1, lanes]
        small[shard] = low(block_rows[...])
    rows = held.shape[2]
    for out in outs:
        for far_row in range(2):
            for far_side in range(2):
                for level in range(depth):
                    source = small.at[place.shard(level, far_row)]
                    for path in range(2):
                        target = sum_place(out, path, far_row, far_side, level).at[pl.ds(rows, SMALL)]
                        copy(source, target, small_sem)
    wait_all(ctx, ctx_sem)
    wait_all(grad, grad_sem)
    held[3] = low(t_mm(side_by_side(ctx, 0), low(grad[...]))).reshape(held.shape[1:])
    store_columns(place, 3, held.at[3], outs, held_sem)
    wait_all(held, held_sem)
    for _ in range(8):
        wait_all(small, small_sem)


def qkv_backward(depth, extra, pos_ref, grad_ref, grads_ref, *refs):
    parts, refs = refs[:10], refs[10 + extra :]
    x_grad_ref, weight, grads, weight_sem, grads_sem, grad_sem = refs
    place = Place(pos_ref)
    copy(grad_ref, x_grad_ref, grad_sem)
    for block in range(3):
        panels = pl.ds(block * PAIRS, PAIRS)
        copy(grads_ref.at[panels], grads.at[panels], grads_sem.at[block])
        load_block(place, depth, block, parts, weight.at[block], weight_sem.at[block])
    wait_all(x_grad_ref, grad_sem)
    for block in range(3):
        wait_all(grads.at[pl.ds(block * PAIRS, PAIRS)], grads_sem.at[block])
        wait_all(weight.at[block], weight_sem.at[block])

    def block_step(block, carry):
        x_grad_ref[...] += mm_t(side_by_side(grads, block), weight[block].reshape(WIDE, WIDE))
        return carry

    lax.fori_loop(0, 3, block_step, 0)


def finish_first(pos_ref, *refs):
    core, side = pos_ref[0], pos_ref[1]
    quarters, (qkv_ref, out_ref, up_bias_ref, biases_ref, gains_ref) = refs[: 4 * LAYERS], refs[4 * LAYERS :]
    rows = qkv_ref.shape[1]
    for layer in range(LAYERS):
        small = full(quarters[4 * layer][0, rows : rows + SMALL, :])
        up_bias_ref[layer : layer + 1, :] = small[0:1, : up_bias_ref.shape[1]]
        biases_ref[:, layer] = small[1:7, : biases_ref.shape[2]]
        gains_ref[layer] = small[7:9, : gains_ref.shape[2]]
        for far in range(4):
            part = quarters[4 * layer + far]
            at_core, at_side = flip(core, far // 2), flip(side, far % 2)
            half = at_core * HALF
            lanes = pl.ds(pl.multiple_of(at_side * (2 * WIDE) + half, HALF), HALF)
            qkv_ref[layer, :, lanes] = full(part[0, :rows, :])
            last = full(part[1, :rows, :])

            @pl.when(at_side == 0)
            def _():
                qkv_ref[layer, :, pl.ds(pl.multiple_of(WIDE + half, HALF), HALF)] = last

            @pl.when(at_side == 1)
            def _():
                out_ref[layer, :, half_lanes(at_core)] = last


def finish_second(extra, pos_ref, *refs):
    core, side = pos_ref[0], pos_ref[1]
    quarters, (up_ref, down_ref) = refs[: 4 * LAYERS], refs[4 * LAYERS + extra :]
    rows = up_ref.shape[1]
    for layer in range(LAYERS):
        for far in range(4):
            part = quarters[4 * layer + far]
            at_core, at_side = flip(core, far // 2), flip(side, far % 2)
            for block in range(2):
                lanes = pl.ds(
                    pl.multiple_of(at_side * (2 * WIDE) + block * WIDE + at_core * HALF, HALF), HALF
                )
                up_ref[layer, :, lanes] = full(part[block])
                down_rows = pl.ds(pl.multiple_of((at_side * 2 + block) * rows, rows), rows)
                down_ref[layer, down_rows, half_lanes(at_core)] = full(part[2 + block])


def prepare(
    pos_ref, qkv_ref, out_ref, up_ref, down_ref, up_bias_ref, biases_ref, gains_ref,
    first_group, second_group, third_group, rows_of, sem,
):
    core, side = pos_ref[0], pos_ref[1]
    rows = out_ref.shape[1]
    up_size, width = up_bias_ref.shape[1], biases_ref.shape[2]
    for layer in range(LAYERS):
        for block in range(2):
            at = side * 2 + block
            lanes = pl.ds(pl.multiple_of(at * WIDE + core * HALF, HALF), HALF)
            if layer == 0:
                target = first_group.at[block, 0, pl.ds(0, rows)]
                up, down = second_group.at[block, 0], second_group.at[block, 1]
            else:
                target, up, down = (third_group.at[block, unit] for unit in range(3))
            if block == 0:
                pltpu.make_async_copy(qkv_ref.at[layer, :, lanes], target, sem.at[layer, 0, 0]).start()
            else:

                @pl.when(side == 0)
                def _():
                    lanes = pl.ds(pl.multiple_of(WIDE + core * HALF, HALF), HALF)
                    pltpu.make_async_copy(qkv_ref.at[layer, :, lanes], target, sem.at[layer, 0, 1]).start()

                @pl.when(side == 1)
                def _():
                    pltpu.make_async_copy(
                        out_ref.at[layer, :, half_lanes(core)], target, sem.at[layer, 0, 1]
                    ).start()

            pltpu.make_async_copy(up_ref.at[layer, :, lanes], up, sem.at[layer, 1, block]).start()
            down_rows = pl.ds(pl.multiple_of(at * rows, rows), rows)
            pltpu.make_async_copy(
                down_ref.at[layer, down_rows, half_lanes(core)], down, sem.at[layer, 2, block]
            ).start()
    for layer in range(LAYERS):
        rows_of[...] = jnp.zeros_like(rows_of)
        rows_of[0:1, :up_size] = full(up_bias_ref[layer : layer + 1, :])
        rows_of[1:7, :width] = full(biases_ref[:, layer])
        rows_of[7:9, :width] = full(gains_ref[layer])
        first_group[layer, 0, rows : rows + SMALL, :] = low(rows_of[...])
    for layer in range(LAYERS):
        for block in range(2):
            for unit in range(3):
                if layer:
                    part = third_group.at[block, unit]
                elif unit:
                    part = second_group.at[block, unit - 1]
                else:
                    part = first_group.at[block, 0, pl.ds(0, rows)]
                wait_all(part, sem.at[layer, unit, block])


def columns_of(depth, pos_ref, *refs):
    level, out = pos_ref[3], refs[-1]
    for path in range(2):
        for far_level, piece in enumerate(refs[:depth]):
            out[path, lax.rem(level + depth - far_level, depth)] = piece[path]


def split_columns(sizes, column_ref, *refs):
    start = 0
    for size, out in zip(sizes, refs[-len(sizes) :]):
        for path in range(2):
            out[path] = column_ref[:, path, start : start + size]
        start += size


def add_up(jobs, *refs):
    start, out = 0, sum(sum(counts) for counts, _ in jobs)
    for counts, form in jobs:
        for at, count in enumerate(counts):
            total = full(refs[start][...])
            for ref in refs[start + 1 : start + count]:
                total = total + full(ref[...])
            if form == "joined":
                refs[out][at] = low(total)
            elif form == "beside":
                refs[out][:, at] = low(total)
            else:
                refs[out + at][...] = low(total)
            start += count
        out += 1 if form else len(counts)


def add_up_far(depth, count, pos_ref, *refs):
    inputs, outs = refs[: 2 * count], refs[2 * count :]
    step = pl.program_id(0)
    for path in range(2):
        total = full(inputs[path * count][...])
        for ref in inputs[path * count + 1 : (path + 1) * count]:
            total = total + full(ref[...])
        for at in range(depth):

            @pl.when(step == at)
            def _():
                outs[at][path] = total[0].astype(outs[at].dtype)


def add_all(*refs):
    total = full(refs[0][...])
    for ref in refs[1:-1]:
        total = total + full(ref[...])
    refs[-1][...] = low(total)


def spread(depth, up_size, width, path, pos_ref, near_ref, far_ref, params_ref, small, sem):
    place = Place(pos_ref)
    rows = near_ref.shape[3] - SMALL
    for far_row, part in enumerate((near_ref.at[path], far_ref.at[path])):
        for level in range(depth):
            pltpu.make_async_copy(
                part.at[level, 0, pl.ds(rows, SMALL)], small.at[far_row, level], sem
            ).start()
    wait_all(small, sem)
    ups, others = 0.0, 0.0
    for far_row in range(2):
        for level in range(depth):
            shard = place.shard(level, far_row)
            block = full(small[far_row, level])
            up = jnp.concatenate([block, jnp.zeros((SMALL, 4 * WIDE - HALF), F32)], 1)
            ups += pltpu.roll(up, shard * up_size, 1)
            other = jnp.concatenate([block[:, :128], jnp.zeros((SMALL, WIDE - 128), F32)], 1)
            others += pltpu.roll(other, shard * width, 1)
    params_ref[...] = ups
    params_ref[1:9, :WIDE] = others[1:9]


VMEM = pltpu.MemorySpace.VMEM
SMEM = pltpu.MemorySpace.SMEM
ANY = pl.ANY
F32 = jnp.float32
BF16 = jnp.bfloat16


def call(kernel, spaces, outs, scratch, cost, after=(), limit=VMEM_LIMIT):
    run = pl.pallas_call(
        kernel,
        in_specs=[pl.BlockSpec(memory_space=space) for space in spaces + [ANY] * len(after)],
        out_specs=[pl.BlockSpec(memory_space=space) for _, _, space in outs],
        out_shape=[jax.ShapeDtypeStruct(shape, dtype) for shape, dtype, _ in outs],
        scratch_shapes=scratch,
        compiler_params=pltpu.CompilerParams(vmem_limit_bytes=limit),
        cost_estimate=pl.CostEstimate(flops=int(cost * COST), bytes_accessed=0, transcendentals=0),
    )
    return lambda *args: run(*args, *after)


def pass_through(*refs):
    pass


def tie(values, after):
    count = len(values)
    return pl.pallas_call(
        pass_through,
        in_specs=[pl.BlockSpec(memory_space=ANY)] * (count + len(after)),
        out_specs=[pl.BlockSpec(memory_space=ANY)] * count,
        out_shape=[jax.ShapeDtypeStruct(value.shape, value.dtype) for value in values],
        input_output_aliases={at: at for at in range(count)},
    )(*values, *after)


DMA = pltpu.SemaphoreType.DMA


class Sizes:
    def __init__(self, tokens, seqs, shards, rows, up_size, width):
        self.tokens, self.seqs, self.shards, self.rows = tokens, seqs, shards, rows
        self.up_size, self.width = up_size, width
        self.depth = shards // 2
        self.slots = tokens // seqs

    def columns(self, count):
        return pltpu.VMEM((count, self.shards, self.rows, WIDE), BF16)

    def by_rows(self):
        return pltpu.VMEM((self.shards, 4, self.rows, WIDE), BF16)

    def unit_grad(self, more=0):
        return [((2, 2, 2, self.depth, self.rows + more, HALF), BF16, ANY)] * 2


def run_attention_forward(z, pos, counts, x, group, params, after=()):
    t = z.tokens
    return call(
        functools.partial(attention_forward, z.depth, z.seqs, len(after)),
        [SMEM, SMEM] + [VMEM] * 2 + [ANY] * 10,
        [
            ((t, WIDE), F32, VMEM),
            ((t, WIDE), BF16, VMEM),
            ((t, WIDE), F32, VMEM),
            ((t, 128), F32, VMEM),
            ((PAIRS, t, PAIR), BF16, VMEM),
            ((3 * PAIRS, t, PAIR), BF16, VMEM),
            ((z.seqs, PAIRS, z.slots, 2 * KEYS), BF16, ANY),
        ],
        [
            z.columns(4),
            pltpu.VMEM((z.seqs, PAIRS, z.slots, 2 * KEYS), BF16),
            DMA((4,)),
            DMA,
        ],
        21,
        after,
    )(pos, counts, x, params, *group)


def run_mlp_forward(z, pos, first, group, params, after=()):
    t = z.tokens
    return call(
        functools.partial(mlp_forward, z.depth, len(after)),
        [SMEM] + [VMEM] * 2 + [ANY] * 10,
        [
            ((t, WIDE), F32, VMEM),
            ((t, WIDE), BF16, VMEM),
            ((t, WIDE), F32, VMEM),
            ((t, 128), F32, VMEM),
            ((4, t, WIDE), BF16, ANY),
            ((4, t, WIDE), BF16, ANY),
        ],
        [
            z.columns(4),
            z.by_rows(),
            pltpu.VMEM((2, t, WIDE), F32),
            pltpu.VMEM((t, WIDE), BF16),
            pltpu.VMEM((4, t, WIDE), BF16),
            pltpu.VMEM((4, t, WIDE), BF16),
            DMA((4,)),
            DMA((4,)),
            DMA,
            DMA,
        ],
        20,
        after,
    )(pos, first, params, *group)


def run_down_backward(z, pos, grad, hat, scale, params, act, after=()):
    t = z.tokens
    return call(
        functools.partial(down_backward, z.depth, len(after)),
        [SMEM, VMEM] + [ANY] * 4,
        [
            ((t, WIDE), F32, ANY),
            ((8, WIDE), F32, VMEM),
            *z.unit_grad(),
        ],
        [
            pltpu.VMEM((t, WIDE), grad.dtype),
            pltpu.VMEM((t, WIDE), F32),
            pltpu.VMEM((t, 128), F32),
            pltpu.VMEM((t, WIDE), F32),
            pltpu.VMEM((4, t, WIDE), BF16),
            pltpu.VMEM((4, z.shards // 4, 4, z.rows, WIDE), BF16),
            DMA((4,)),
            DMA((4,)),
            DMA,
            DMA,
        ],
        10,
        after,
    )(pos, params, grad, hat, scale, act)


def run_up_backward(z, pos, second, group, slope, first_low, hat, scale, params, after=()):
    t = z.tokens
    return call(
        functools.partial(up_backward, z.depth, len(after)),
        [SMEM, VMEM] + [ANY] * 15,
        [
            ((t, WIDE), F32, ANY),
            ((8, WIDE), F32, VMEM),
            ((1, 4 * WIDE), F32, VMEM),
            *z.unit_grad(),
        ],
        [
            z.columns(4),
            z.by_rows(),
            pltpu.VMEM((4, t, WIDE), BF16),
            pltpu.VMEM((t, WIDE), F32),
            pltpu.VMEM((t, WIDE), BF16),
            pltpu.VMEM((t, WIDE), F32),
            pltpu.VMEM((t, 128), F32),
            pltpu.VMEM((4, z.shards, z.rows, WIDE), BF16),
            DMA((4,)),
            DMA((4,)),
            DMA((4,)),
            DMA,
            DMA,
            DMA((4,)),
            DMA,
            DMA,
        ],
        19,
        after,
    )(pos, params, second, slope, first_low, hat, scale, *group)


def run_attention_backward(z, pos, grad, group, qkv, probs, after=()):
    t = z.tokens
    return call(
        functools.partial(attention_backward, z.depth, z.seqs, len(after)),
        [SMEM] + [ANY] * 13,
        [((3 * PAIRS, t, PAIR), BF16, ANY)],
        [
            pltpu.VMEM((z.shards, z.rows, WIDE), BF16),
            pltpu.VMEM((t, WIDE), F32),
            pltpu.VMEM((3 * PAIRS, t, PAIR), BF16),
            pltpu.VMEM((z.seqs, PAIRS, z.slots, 2 * KEYS), BF16),
            pltpu.VMEM((PAIRS, t, PAIR), BF16),
            pltpu.VMEM((3 * PAIRS, t, PAIR), BF16),
            DMA,
            DMA,
            DMA,
            DMA,
            DMA,
        ],
        13,
        after,
    )(pos, grad, qkv, probs, *group)[0]


def run_qkv_weights(z, pos, grad, grads, ctx, x_low, down_sums, up_sums, up_bias, after=()):
    t = z.tokens
    return call(
        functools.partial(qkv_weights, z.depth, z.up_size, z.width, len(after)),
        [SMEM] + [VMEM] * 3 + [ANY] * 4,
        z.unit_grad(SMALL),
        [
            pltpu.VMEM((t, WIDE), F32),
            pltpu.VMEM((3 * PAIRS, t, PAIR), BF16),
            pltpu.VMEM((PAIRS, t, PAIR), BF16),
            pltpu.VMEM((t, WIDE), BF16),
            pltpu.VMEM((4, z.shards, z.rows, WIDE), BF16),
            pltpu.VMEM((8, WIDE), F32),
            pltpu.VMEM((SMALL, HALF), F32),
            pltpu.VMEM((z.shards, SMALL, HALF), BF16),
            DMA,
            DMA((3,)),
            DMA,
            DMA,
            DMA,
            DMA,
        ],
        8,
        after,
    )(pos, down_sums, up_sums, up_bias, grad, grads, ctx, x_low)


def run_qkv_backward(z, pos, grad, grads, group, after=()):
    t = z.tokens
    return call(
        functools.partial(qkv_backward, z.depth, len(after)),
        [SMEM] + [ANY] * 12,
        [((t, WIDE), F32, VMEM)],
        [
            z.columns(3),
            pltpu.VMEM((3 * PAIRS, t, PAIR), BF16),
            DMA((3,)),
            DMA((3,)),
            DMA,
        ],
        6,
        after,
    )(pos, grad, grads, *group)[0]


def run_finish_first(z, pos, quarters):
    r = z.rows
    return call(
        finish_first,
        [SMEM] + [VMEM] * (4 * LAYERS),
        [
            ((LAYERS, r, 3 * WIDE), F32, VMEM),
            ((LAYERS, r, WIDE), F32, VMEM),
            ((LAYERS, z.up_size), F32, VMEM),
            ((6, LAYERS, z.width), F32, VMEM),
            ((LAYERS, 2, z.width), F32, VMEM),
        ],
        [],
        3,
        limit=SMALL_LIMIT,
    )(pos, *quarters)


def run_finish_second(z, pos, quarters, after=()):
    r = z.rows
    return call(
        functools.partial(finish_second, len(after)),
        [SMEM] + [VMEM] * (4 * LAYERS),
        [
            ((LAYERS, r, 4 * WIDE), F32, VMEM),
            ((LAYERS, 4 * r, WIDE), F32, VMEM),
        ],
        [],
        5,
        after,
        limit=SMALL_LIMIT,
    )(pos, *quarters)


def run_prepare(z, pos, *arrays):
    r = z.rows
    return call(
        prepare,
        [SMEM] + [ANY] * 4 + [VMEM] * 3,
        [
            ((2, 1, r + SMALL, HALF), BF16, VMEM),
            ((2, 2, r, HALF), BF16, VMEM),
            ((2, 3, r, HALF), BF16, VMEM),
        ],
        [
            pltpu.VMEM((SMALL, HALF), F32),
            DMA((LAYERS, 3, 2)),
        ],
        1,
        limit=SMALL_LIMIT,
    )(pos, *arrays)


def run_columns_of(pos, pieces):
    depth, shape = len(pieces), pieces[0].shape
    return call(
        functools.partial(columns_of, depth),
        [SMEM] + [VMEM] * depth,
        [((2, depth) + shape[1:], BF16, VMEM)],
        [],
        2,
    )(pos, *pieces)[0]


def run_split_columns(column, sizes):
    depth, _, _, *rest = column.shape
    outs = [((2, depth, size, *rest), BF16, VMEM) for size in sizes]
    return call(functools.partial(split_columns, sizes), [VMEM], outs, [], 2)(column)


def add_specs(sums, size, place):
    specs = []
    for parts in sums:
        for array, lead in parts:
            rest = array.shape[len(lead) + 1 :]
            specs.append(
                pl.BlockSpec(
                    (None,) * len(lead) + (size,) + rest,
                    lambda *at, lead=lead, rest=len(rest): lead + (place(*at),) + (0,) * rest,
                )
            )
    return specs


def run_add_up(jobs):
    specs, arrays, outs, out_specs = [], [], [], []
    for sums, form in jobs:
        array, lead = sums[0][0]
        depth, *rest = array.shape[len(lead) :]
        size, count = depth // 2, len(sums)
        specs += add_specs(sums, size, lambda step: step)
        arrays += [array for parts in sums for array, _ in parts]
        if form == "joined":
            outs.append((count, depth, *rest))
            out_specs.append(pl.BlockSpec((count, size, *rest), lambda step: (0, step, 0, 0)))
        elif form == "beside":
            outs.append((depth, count, *rest))
            out_specs.append(pl.BlockSpec((size, count, *rest), lambda step: (step, 0, 0, 0)))
        else:
            outs += [(depth, *rest)] * count
            out_specs += [
                pl.BlockSpec((size, *rest), lambda step, zeros=(0,) * len(rest): (step,) + zeros)
            ] * count
    results = list(
        pl.pallas_call(
            functools.partial(add_up, [([len(parts) for parts in sums], form) for sums, form in jobs]),
            grid=(2,),
            in_specs=specs,
            out_specs=out_specs,
            out_shape=[jax.ShapeDtypeStruct(out, BF16) for out in outs],
            compiler_params=pltpu.CompilerParams(vmem_limit_bytes=SMALL_LIMIT),
            cost_estimate=pl.CostEstimate(flops=int(3 * COST), bytes_accessed=0, transcendentals=0),
        )(*arrays)
    )
    grouped = []
    for sums, form in jobs:
        count = 1 if form else len(sums)
        grouped.append(results[:count])
        results = results[count:]
    return grouped


def run_add_up_far(pos, sums):
    array, lead = sums[0][0]
    depth, *rest = array.shape[len(lead) :]
    outs = [jax.ShapeDtypeStruct((2, *rest), F32 if at == 0 else BF16) for at in range(depth)]
    return pl.pallas_call(
        functools.partial(add_up_far, depth, len(sums[0])),
        grid_spec=pltpu.PrefetchScalarGridSpec(
            num_scalar_prefetch=1,
            grid=(depth,),
            in_specs=add_specs(sums, 1, lambda step, pos_ref: lax.rem(pos_ref[3] + step, depth)),
            out_specs=[pl.BlockSpec(out.shape, lambda step, pos_ref: (0, 0, 0)) for out in outs],
        ),
        out_shape=outs,
        compiler_params=pltpu.CompilerParams(vmem_limit_bytes=SMALL_LIMIT),
        cost_estimate=pl.CostEstimate(flops=int(3 * COST), bytes_accessed=0, transcendentals=0),
    )(pos, *[array for parts in sums for array, _ in parts])


def run_add_all(arrays):
    return call(add_all, [VMEM] * len(arrays), [(arrays[0].shape, BF16, VMEM)], [], 1, limit=SMALL_LIMIT)(*arrays)[0]


def run_spread(z, pos, near, far, path):
    return call(
        functools.partial(spread, z.depth, z.up_size, z.width, path),
        [SMEM, ANY, ANY],
        [((SMALL, 4 * WIDE), F32, VMEM)],
        [pltpu.VMEM((2, z.depth, SMALL, HALF), BF16), DMA],
        2,
        limit=SMALL_LIMIT,
    )(pos, near, far)[0]


class Links:
    def __init__(self, rep_size, fsdp_size):
        self.rep_size, self.fsdp_size = rep_size, fsdp_size
        self.depth = fsdp_size // 2
        rep_at, fsdp_at = lax.axis_index("rep"), lax.axis_index("fsdp")
        self.core, self.side = rep_at % 2, (rep_at // 2) % 2
        self.row, self.level = fsdp_at % 2, fsdp_at // 2

    def permute(self, value, target):
        pairs = []
        for rep_at in range(self.rep_size):
            for fsdp_at in range(self.fsdp_size):
                to_rep, to_fsdp = target(rep_at, fsdp_at)
                pairs.append((rep_at * self.fsdp_size + fsdp_at, to_rep * self.fsdp_size + to_fsdp))
        return lax.ppermute(value, AXES, pairs)

    def other_core(self, value):
        return self.permute(value, lambda r, f: (r ^ 1, f))

    def other_side(self, value):
        return self.permute(value, lambda r, f: (r ^ 2, f))

    def other_row(self, value):
        return self.permute(value, lambda r, f: (r, f ^ 1))

    def level_up(self, value, step):
        return self.permute(value, lambda r, f: (r, ((f // 2 + step) % self.depth) * 2 + f % 2))

    def levels(self):
        return [list(range(row, self.fsdp_size, 2)) for row in range(2)]


class Gather:
    def __init__(self, name, links, columns):
        self.name, self.links, self.live, self.moving = name, links, [columns], []

    def scope(self, stage):
        return jax.named_scope("gather_" + self.name + "_" + stage)

    def first(self):
        with self.scope("first"):
            self.moving = [self.links.other_row(self.live[0]), self.links.other_side(self.live[0])]

    def second(self):
        self.live += self.moving
        with self.scope("second"):
            rows, sides = self.live[1:3]
            self.moving = [self.links.other_side(rows[0]), self.links.other_row(sides[1])]
        with self.scope("cores"):
            self.moving += [self.links.other_core(part) for part in self.live[:3]]

    def last(self):
        self.live += self.moving[:2]
        self.far = self.moving[2:]
        with self.scope("last"):
            self.moving = [self.links.other_core(part) for part in self.live[3:5]]

    def arrays(self):
        return self.live + self.far + self.moving


class Sum:
    def __init__(self, name, links, near, far):
        self.name, self.links, self.near, self.sends = name, links, near, [far]
        self.hops = ((links.other_row, links.other_side), (links.other_side, links.other_row))

    def scope(self, stage):
        return jax.named_scope("sum_" + self.name + "_" + stage)

    def cores(self):
        with self.scope("cores"):
            self.moving = [self.links.other_core(self.sends[0])]

    def at(self, far):
        return [[(array, lead + (far,)) for array, lead in parts] for parts in self.parts]

    def came(self):
        self.parts = [[(self.near, (path,)), (self.moving[0], (path,))] for path in range(2)]
        return [(self.at(1), None)]

    def first(self):
        with self.scope("first"):
            self.moving = [self.hops[path][0](self.sends[path]) for path in range(2)]


class Second:
    def __init__(self, name, links, sums):
        self.name, self.links, self.sums = name, links, sums

    def came(self):
        for one in self.sums:
            one.parts = [parts + [(move, ())] for parts, move in zip(one.at(0), one.moving)]
        return [([one.at(1)[path] for one in self.sums], "joined") for path in range(2)]

    def second(self):
        with jax.named_scope("sum_" + self.name + "_second"):
            self.moving = [hops[1](send) for hops, send in zip(self.sums[0].hops, self.sends)]


def add(*steps):
    jobs = [step.came() for step in steps]
    with jax.named_scope("add_" + "_".join(step.name for step in steps)):
        outs = run_add_up([job for step_jobs in jobs for job in step_jobs])
    for step, step_jobs in zip(steps, jobs):
        step.sends = [out for group in outs[: len(step_jobs)] for out in group]
        outs = outs[len(step_jobs) :]


class Share:
    def __init__(self, name, links, second):
        self.name, self.links, self.second = name, links, second

    def scope(self):
        return jax.named_scope("share_" + self.name)

    def parts(self):
        return [
            one.at(0)[path] + [(self.second.moving[path], (unit,))]
            for unit, one in enumerate(self.second.sums)
            for path in range(2)
        ]

    def came(self):
        return [(self.parts(), "beside")]

    def scatter(self):
        with self.scope():
            self.sends = [
                lax.psum_scatter(
                    self.sends[0], "fsdp", scatter_dimension=0, axis_index_groups=self.links.levels()
                )
            ]

    def add_far(self, pos):
        with self.scope():
            self.kept, *self.sends = run_add_up_far(pos, self.parts())

    def levels(self):
        with self.scope():
            self.moving = [self.links.level_up(send, at + 1) for at, send in enumerate(self.sends)]

    def after_levels(self):
        with self.scope():
            self.sends = [run_add_all([self.kept] + self.moving)]

    def copies(self):
        if self.links.rep_size > 4:
            groups = [list(range(first, self.links.rep_size, 4)) for first in range(4)]
            self.sends = [lax.psum(self.sends[0], "rep", axis_index_groups=groups)]

    def sides(self):
        with self.scope():
            self.sends += [self.links.other_side(self.sends[0])]

    def last(self):
        with self.scope():
            self.moving = [self.links.other_core(send) for send in self.sends]

    def quarters(self):
        return self.sends + self.moving


def order(steps, after=()):
    names = ("live", "moving", "sends")
    held = [(step, name) for step in steps for name in (names[:2] if hasattr(step, "live") else names[2:])]
    values = [value for step, name in held for value in getattr(step, name)]
    values = list(tie(values, list(after)))
    token = min(values, key=lambda value: value.size)
    for step, name in held:
        size = len(getattr(step, name))
        setattr(step, name, values[:size])
        values = values[size:]
    return [token]


def shards(
    rep_size, fsdp_size, hidden, region_counts, w_qkv, w_out, w_up, w_down, bias_up, biases, norm_gains, cotangent
):
    links = Links(rep_size, fsdp_size)
    z = Sizes(
        hidden.shape[0], region_counts.shape[0], fsdp_size, w_qkv.shape[1], bias_up.shape[1], biases.shape[2]
    )
    pos = jnp.stack([links.core, links.side, links.row, links.level]).astype(jnp.int32)
    quarters = run_prepare(
        z, pos, w_qkv, w_out, w_up, w_down, bias_up, jnp.transpose(biases, (1, 0, 2)), norm_gains
    )
    kept, groups, params = [], [None] * 4, [None] * 2

    def run_first(layer, states, after):
        return run_attention_forward(z, pos, region_counts, states, groups[2 * layer], params[layer], after)

    def run_second(layer, first, after):
        return run_mlp_forward(z, pos, first, groups[2 * layer + 1], params[layer], after)

    def columns(name, quarter, after=()):
        with jax.named_scope("columns_" + name):
            if after:
                quarter = tie([quarter], list(after))[0]
            pieces = [quarter] + [links.level_up(quarter, step) for step in range(1, links.depth)]
            return run_columns_of(pos, pieces)

    first_0 = Gather("first0", links, columns("first0", quarters[0]))
    first_0.first()
    second_0 = Gather("second0", links, columns("second0", quarters[1], first_0.live))

    order([first_0])
    first_0.second()

    order([first_0, second_0])
    first_0.last()
    second_0.first()
    with jax.named_scope("columns_third"):
        third = tie([quarters[2]], first_0.live[1:3])[0]
        third = lax.all_gather(third, "fsdp", axis_index_groups=links.levels())
    params = [run_spread(z, pos, *first_0.live[:2], layer) for layer in range(LAYERS)]
    groups[0] = first_0.arrays()
    one = run_first(0, hidden, params[1:])

    order([second_0], one[3:4])
    second_0.second()
    with jax.named_scope("columns_third"):
        third = run_split_columns(third, (1, 2))
    first_1, second_1 = (Gather(name, links, part) for name, part in zip(("first1", "second1"), third))

    first_1.first()

    order([second_0, second_1])
    second_0.last()
    second_1.first()
    groups[1] = second_0.arrays()
    two = run_second(0, one[0], ())
    kept.append((hidden, one, two))

    order([first_1], two[3:4])
    first_1.second()

    order([first_1, second_1])
    first_1.last()
    second_1.second()
    groups[2] = first_1.arrays()
    one = run_first(1, two[0], ())

    order([second_1], one[3:4])
    second_1.last()
    groups[3] = second_1.arrays()
    low_states = two[1]
    two = run_second(1, one[0], ())
    kept.append((low_states, one, two))
    output = two[1]

    def run_down(layer, gradient, after):
        _, _, hat, scale, act, _ = kept[layer][2]
        return run_down_backward(z, pos, gradient, hat, scale, params[layer], act, after)

    def run_up(layer, second, after):
        _, first_low, hat, scale, *_ = kept[layer][1]
        return run_up_backward(
            z, pos, second, groups[2 * layer + 1], kept[layer][2][5], first_low, hat, scale, params[layer], after
        )

    def run_attention(layer, first_in, after):
        qkv, probs = kept[layer][1][5:7]
        return run_attention_backward(z, pos, first_in, groups[2 * layer], qkv, probs, after)

    def run_weights(layer, first_in, grads, small, after):
        return run_qkv_weights(z, pos, first_in, grads, kept[layer][1][4], kept[layer][0], *small, after)

    def run_states(layer, first_in, grads, after):
        return run_qkv_backward(z, pos, first_in, grads, groups[2 * layer], after)

    second, down_sums, near, far = run_down(1, cotangent, ())
    down_1 = Sum("down1", links, near, far)

    token = order([down_1])
    down_1.cores()
    first_in, up_sums, up_bias, near, far = run_up(1, second, token)
    up_1 = Sum("up1", links, near, far)

    add(down_1)
    token = order([down_1, up_1])
    down_1.first()
    up_1.cores()
    grads = run_attention(1, first_in, token)

    add(up_1)
    token = order([up_1], [grads] + down_1.moving)
    up_1.first()
    near, far = run_weights(1, first_in, grads, (down_sums, up_sums, up_bias), token)
    first_1 = Sum("first1", links, near, far)
    gradient = run_states(1, first_in, grads, first_1.sends)

    second_1 = Second("second1", links, [up_1, down_1])
    add(second_1)
    token = order([second_1, first_1], [gradient])
    second_1.second()
    first_1.cores()
    second, down_sums, near, far = run_down(0, gradient, token)
    down_0 = Sum("down0", links, near, far)

    share_second_1 = Share("second1", links, second_1)
    order([down_0], second_1.moving + first_1.moving)
    down_0.cores()
    add(first_1, share_second_1)
    order([first_1, share_second_1])
    first_1.first()
    share_second_1.scatter()
    add(down_0)
    token = order([down_0])
    down_0.first()
    first_in, up_sums, up_bias, near, far = run_up(0, second, token)
    up_0 = Sum("up0", links, near, far)

    first_second_1 = Second("first1", links, [first_1])
    order([up_0], first_1.moving + down_0.moving)
    up_0.cores()
    add(first_second_1)
    order([first_second_1])
    first_second_1.second()
    add(up_0)
    token = order([up_0])
    up_0.first()
    grads = run_attention(0, first_in, token)

    second_0 = Second("second0", links, [up_0, down_0])
    share_first_1 = Share("first1", links, first_second_1)
    add(second_0, share_first_1)
    token = order([second_0, share_first_1], [grads])
    second_0.second()
    share_first_1.scatter()
    near, far = run_weights(0, first_in, grads, (down_sums, up_sums, up_bias), token)
    first_0 = Sum("first0", links, near, far)

    share_second_0 = Share("second0", links, second_0)
    order([first_0], second_0.moving)
    first_0.cores()
    add(share_second_0)
    share_second_1.copies()
    token = order([share_second_0, share_second_1], [first_0.near])
    share_second_0.scatter()
    share_second_1.sides()
    gradient = run_states(0, first_in, grads, token)

    add(first_0)
    order([first_0, share_second_1], [gradient])
    first_0.first()
    share_second_1.last()

    first_second_0 = Second("first0", links, [first_0])
    add(first_second_0)
    share_first_1.copies()
    order([first_second_0, share_first_1], share_second_1.moving)
    first_second_0.second()
    share_first_1.sides()

    share_first_0 = Share("first0", links, first_second_0)
    share_first_0.add_far(pos)
    share_second_0.copies()
    order([share_first_0, share_second_0, share_first_1])
    share_first_0.levels()
    share_second_0.sides()
    share_first_1.last()

    share_first_0.after_levels()
    share_first_0.copies()
    order([share_first_0, share_second_0], share_first_1.moving)
    share_first_0.sides()
    share_second_0.last()
    up_grad, down_grad = run_finish_second(z, pos, share_second_0.quarters() + share_second_1.quarters())

    order([share_first_0], [up_grad])
    share_first_0.last()
    qkv_grad, out_grad, up_bias_grad, biases_grad, gains_grad = run_finish_first(
        z, pos, share_first_0.quarters() + share_first_1.quarters()
    )
    biases_grad = jnp.transpose(biases_grad, (1, 0, 2))
    return output, gradient, qkv_grad, out_grad, up_grad, down_grad, up_bias_grad, biases_grad, gains_grad


def solution(mesh):
    in_specs = (
        P(("rep", "fsdp"), None),
        P(("rep", "fsdp")),
        P(None, "fsdp", None),
        P(None, "fsdp", None),
        P(None, "fsdp", None),
        P(None, "fsdp", None),
        P(None, "fsdp"),
        P(None, None, "fsdp"),
        P(None, None, "fsdp"),
        P(("rep", "fsdp"), None),
    )
    out_specs = (
        P(("rep", "fsdp"), None),
        P(("rep", "fsdp"), None),
        P(None, "fsdp", None),
        P(None, "fsdp", None),
        P(None, "fsdp", None),
        P(None, "fsdp", None),
        P(None, "fsdp"),
        P(None, None, "fsdp"),
        P(None, None, "fsdp"),
    )
    local = functools.partial(shards, mesh.shape["rep"], mesh.shape["fsdp"])
    return jax.shard_map(local, mesh=mesh, in_specs=in_specs, out_specs=out_specs, check_vma=False)
```

time: 557 us -> 489 us (0.88)
  local copies, waits for them, and re-layouts: 85.9 us -> 14.9 us
  waiting for transfers between devices: 128 us -> 135 us
    unnamed x278 -> x14, local copies, waits for them, and re-layouts: 85.9 us -> 1.66 us
    squeeze x0 -> x8, local copies, waits for them, and re-layouts: none -> 13.2 us  [the longest x4 6.61 us: second(): sides[1]]
    pallas_call x27 -> x23, Pallas kernels: 225 us -> 217 us  [call(): return lambda *args: run(*args, *after)]
    all_gather x1, waiting for transfers between devices: 2.46 us -> 9.86 us  [shards(): third = lax.all_gather(third, 'fsdp', axis_index_groups=links.levels())]
    pallas_call x15 -> x11, Pallas kernels: 26.2 us -> 33.3 us  [run_add_up(): pl.pallas_call(functools.partial(add_up, [([len(parts) for parts in sums]...]
  transfers between devices with their start and end apart: 87 -> 87, of which waited for: 34 -> 36; matrix products, arithmetic and copies ran while one was open for 0% -> 3% of each run, Pallas kernels for 39% -> 44%
where the time goes in v3:
time: 489 us; the launch traced here: 483 us
  Pallas kernels  255 us (52%)
  waiting for transfers between devices  135 us (28%)
  starting transfers between devices  62.3 us (13%)
  local copies, waits for them, and re-layouts  14.9 us (3%)
  between operations  14.6 us (3%)
    pallas_call x23, Pallas kernels, call(): return lambda *args: run(*args, *after)  217 us
    ppermute x83, waiting for transfers between devices, permute(): return lax.ppermute(value, AXES, pairs)  123 us
    ppermute x83, starting transfers between devices, permute(): return lax.ppermute(value, AXES, pairs)  62.2 us
    pallas_call x11, Pallas kernels, run_add_up(): pl.pallas_call(functools.partial(add_up, [([len(parts) for parts in sums]...  33.3 us
    all_gather x1, waiting for transfers between devices, shards(): third = lax.all_gather(third, 'fsdp', axis_index_groups=links.levels())  9.86 us
  transfers between devices with their start and end apart: 87, of which 36 were waited for; matrix products, arithmetic and copies ran while one was open for 3% of the time, Pallas kernels for 44%

profile of v3, /device:TPU:0, one launch (start us, length us, event | category | flops | bytes accessed | tf_op | source)
XLA Modules:
  0.0 483.1 jit_solution(413944726439416578)
XLA Ops:
  7.9 3.1 shard_map.169
  11.0 5.1 %collective-permute-start.2 = (bf16[2,1,112,384]{3,2,1,0:T(8,128)(2,1)}, bf16[2,1,112,384]{3,2,1,0:T(8,128)(2,1)}, u32[]{:S(2)}, u32[]{:S(2)}) collective-permute-start(bf16[2,1,112,384]{3,2,1,0:T(8,128)(2,1)} %get-tuple-element.180.refs_0_), channel_id=1, source_target_pairs={{0,6},{1,7},{2,0},{3,1},{4,2},{5,3},{6,4},{7,5},{8,14},{9,15},{10,... | collective-permute-start | bytes 516104 | tf_op jit(solution)/shard_map/columns_first0/ppermute | solution.py:1112
  17.1 4.1 collective-permute-done.2.refs_3_
  21.2 9.8 %collective-permute-done.1.refs_2_ = bf16[2,1,112,384]{3,2,1,0:T(8,128)(2,1)} collective-permute-done((bf16[2,1,112,384]{3,2,1,0:T(8,128)(2,1)}, bf16[2,1,112,384]{3,2,1,0:T(8,128)(2,1)}, u32[]{:S(2)}, u32[]{:S(2)}) %collective-permute-start.1) | collective-permute-done | bytes 172064 | tf_op jit(solution)/shard_map/columns_first0/ppermute | solution.py:1112
  40.9 9.4 %collective-permute-done.4.refs_2_ = bf16[2,4,1,112,384]{4,3,2,1,0:T(8,128)(2,1)S(1)} collective-permute-done((bf16[2,4,1,112,384]{4,3,2,1,0:T(8,128)(2,1)}, bf16[2,4,1,112,384]{4,3,2,1,0:T(8,128)(2,1)S(1)}, u32[]{:S(2)}, u32[]{:S(2)}) %collective-permute-start.4) | collective-permute-done | bytes 688160 | tf_op jit(solution)/shard_map/gather_first0_first/ppermute | solution.py:1112
  56.4 7.6 %collective-permute-done.11.refs_2_ = bf16[2,2,96,384]{3,2,1,0:T(8,128)(2,1)} collective-permute-done((bf16[2,2,96,384]{3,2,1,0:T(8,128)(2,1)}, bf16[2,2,96,384]{3,2,1,0:T(8,128)(2,1)}, u32[]{:S(2)}, u32[]{:S(2)}) %collective-permute-start.11) | collective-permute-done | bytes 294944 | tf_op jit(solution)/shard_map/columns_second0/ppermute | solution.py:1112
  67.4 4.9 %collective-permute-done.5.refs_3_ = bf16[4,1,112,384]{3,2,1,0:T(8,128)(2,1)} collective-permute-done((bf16[4,1,112,384]{3,2,1,0:T(8,128)(2,1)}, bf16[4,1,112,384]{3,2,1,0:T(8,128)(2,1)}, u32[]{:S(2)}, u32[]{:S(2)}) %collective-permute-start.5) | collective-permute-done | bytes 344096 | tf_op jit(solution)/shard_map/gather_first0_second/ppermute | solution.py:1112
  75.3 2.5 shard_map.173.refs_10_.params_ref
  77.9 2.5 shard_map.172.params_ref
  80.5 16.3 %shard_map.174 = (f32[544,768]{1,0:T(8,128)}, bf16[544,768]{1,0:T(8,128)(2,1)}, f32[544,768]{1,0:T(8,128)}, f32[544,128]{1,0:T(8,128)}, bf16[6,544,128]{2,1,0:T(...) custom-call(s32[4]{0:T(128)} %pad_add_fusion.pos_ref, s32[2]{0:T(128)} %counts_ref.3, ...), custom_call_target="tpu_custom_call" | custom-call | flops 24149999616 | tf_op jit(solution)/shard_map/pallas_call | solution.py:720
  104.4 9.9 %all-gather.3.cloned.1.call-done = bf16[8,3,96,384]{3,2,1,0:T(8,128)(2,1)} async-done(((bf16[2,3,96,384]{3,2,1,0:T(8,128)(2,1)}), bf16[8,3,96,384]{3,2,1,0:T(8,128)(2,1)}) %all-gather.3.cloned.1.call-update) | async-done | bytes 1769488 | tf_op jit(solution)/shard_map/columns_third/all_gather | solution.py:1311
  114.3 2.8 columns_third.3
  124.3 20.6 %shard_map.177 = (f32[544,768]{1,0:T(8,128)}, bf16[544,768]{1,0:T(8,128)(2,1)}, f32[544,768]{1,0:T(8,128)}, f32[544,128]{1,0:T(8,128)}, bf16[4,544,768]{2,1,0:T(8,128)(2,1)}, /*index=5*/bf16[4,544,768]{2,1,0:T(8,128)(2,1)}) custom-call(s32[4]{0:T(128)} %pad_add_fusion.pos_ref, f32[544,768]{1,0:T(8,128)} %get-tuple-element.193.first_ref, ...), custom_call_target="tpu_custom_call" | custom-call | flops 23000000512 | tf_op jit(solution)/shard_map/pallas_call | solution.py:720
  149.1 18.2 %collective-permute-done.26.refs_3_ = bf16[4,1,96,384]{3,2,1,0:T(8,128)(2,1)S(1)} collective-permute-done((bf16[4,1,96,384]{3,2,1,0:T(8,128)(2,1)S(1)}, bf16[4,1,96,384]{3,2,1,0:T(8,128)(2,1)S(1)}, u32[]{:S(2)}, u32[]{:S(2)}) %collective-permute-start.26) | collective-permute-done | bytes 294944 | tf_op jit(solution)/shard_map/gather_first1_second/ppermute | solution.py:1112
  178.5 16.0 %shard_map.180 = (f32[544,768]{1,0:T(8,128)}, bf16[544,768]{1,0:T(8,128)(2,1)}, f32[544,768]{1,0:T(8,128)}, f32[544,128]{1,0:T(8,128)}, bf16[6,544,128]{2,1,0:T(...) custom-call(s32[4]{0:T(128)} %pad_add_fusion.pos_ref, s32[2]{0:T(128)} %counts_ref.3, ...), custom_call_target="tpu_custom_call" | custom-call | flops 24149999616 | tf_op jit(solution)/shard_map/pallas_call | solution.py:720
  197.8 20.8 %shard_map.182 = (f32[544,768]{1,0:T(8,128)}, bf16[544,768]{1,0:T(8,128)(2,1)}, f32[544,768]{1,0:T(8,128)}, f32[544,128]{1,0:T(8,128)}, bf16[4,544,768]{2,1,0:T(8,128)(2,1)}, /*index=5*/bf16[4,544,768]{2,1,0:T(8,128)(2,1)}) custom-call(s32[4]{0:T(128)} %pad_add_fusion.pos_ref, f32[544,768]{1,0:T(8,128)} %get-tuple-element.224.first_ref, ...), custom_call_target="tpu_custom_call" | custom-call | flops 23000000512 | tf_op jit(solution)/shard_map/pallas_call | solution.py:720
  218.6 10.5 %shard_map.183 = (f32[544,768]{1,0:T(8,128)}, f32[8,768]{1,0:T(8,128)}, bf16[2,2,2,4,96,384]{5,4,3,2,1,0:T(8,128)(2,1)}, bf16[2,2,2,4,96,384]{5,4,3,2,1,0:T(8,128)(2,1)}) custom-call(s32[4]{0:T(128)} %pad_add_fusion.pos_ref, f32[16,3072]{1,0:T(8,128)} %shard_map.173.refs_10_.params_ref, bf16[544,768]{1,0:T(8,128)(2,1)} %grad_ref.1, ...), custom_call_target="tpu_custom_call" | custom-call | flops 11500000256 | tf_op jit(solution)/shard_map/pallas_call | solution.py:720
  229.5 19.5 %shard_map.185 = (f32[544,768]{1,0:T(8,128)}, f32[8,768]{1,0:T(8,128)}, f32[1,3072]{1,0:T(1,128)}, bf16[2,2,2,4,96,384]{5,4,3,2,1,0:T(8,128)(2,1)}, bf16[2,2,2,4,96,384]{5,4,3,2,1,0:T(8,128)(2,1)}) custom-call(s32[4]{0:T(128)} %pad_add_fusion.pos_ref, f32[16,3072]{1,0:T(8,128)} %shard_map.173.refs_10_.params_ref, f32[544,768]{1,0:T(8,128)} %get-tuple-element.241.second_ref, ...), custom_call_target="tpu_custom_call" | custom-call | flops 21849999360 | tf_op jit(solution)/shard_map/pallas_call | solution.py:720
  249.0 2.5 add_down1.1
  253.6 12.9 %shard_map.187.refs_2_.grads_ref = bf16[18,544,128]{2,1,0:T(8,128)(2,1)} custom-call(s32[4]{0:T(128)} %pad_add_fusion.pos_ref, f32[544,768]{1,0:T(8,128)} %get-tuple-element.246.grad_ref, bf16[18,544,128]{2,1,0:T(8,128)(2,1)} %get-tuple-element.247.qkv_ref, bf16[2,6,272,512]{3,2,1,0:T(8,128)(2,1)} %get-tuple-element.248.probs_ref, ...), custom_call_target="tpu_custom_call" | custom-call | flops 14949999616 | tf_op jit(solution)/shard_map/pallas_call | solution.py:720
  266.5 2.5 add_up1.1
  271.1 9.0 %shard_map.189 = (bf16[2,2,2,4,112,384]{5,4,3,2,1,0:T(8,128)(2,1)}, bf16[2,2,2,4,112,384]{5,4,3,2,1,0:T(8,128)(2,1)}) custom-call(s32[4]{0:T(128)} %pad_add_fusion.pos_ref, f32[8,768]{1,0:T(8,128)} %get-tuple-element.254.down_sums_ref, f32[8,768]{1,0:T(8,128)} %get-tuple-element.255.up_sums_ref, f32[1,3072]{1,0:T(1,128)} %get-tuple-element.256.up_bias_ref, ...), custom_call_target="tpu_custom_call" | custom-call | flops 9200000000 | tf_op jit(solution)/shard_map/pallas_call | solution.py:720
  280.1 7.9 %shard_map.190.refs_3_.grad_ref = f32[544,768]{1,0:T(8,128)} custom-call(s32[4]{0:T(128)} %pad_add_fusion.pos_ref, f32[544,768]{1,0:T(8,128)} %get-tuple-element.246.grad_ref, bf16[18,544,128]{2,1,0:T(8,128)(2,1)} %shard_map.187.refs_2_.grads_ref, bf16[2,4,1,96,384]{4,3,2,1,0:T(8,128)(2,1)} %get-tuple-element.216.refs_0_, ...), custom_call_target="tpu_custom_call" | custom-call | flops 6899999744 | tf_op jit(solution)/shard_map/pallas_call | solution.py:720
  288.1 3.1 add_second1.1
  293.3 10.7 %shard_map.192 = (f32[544,768]{1,0:T(8,128)}, f32[8,768]{1,0:T(8,128)}, bf16[2,2,2,4,96,384]{5,4,3,2,1,0:T(8,128)(2,1)}, bf16[2,2,2,4,96,384]{5,4,3,2,1,0:T(8,128)(2,1)}) custom-call(s32[4]{0:T(128)} %pad_add_fusion.pos_ref, f32[16,3072]{1,0:T(8,128)} %shard_map.172.params_ref, f32[544,768]{1,0:T(8,128)} %shard_map.190.refs_3_.grad_ref, ...), custom_call_target="tpu_custom_call" | custom-call | flops 11500000256 | tf_op jit(solution)/shard_map/pallas_call | solution.py:720
  304.0 3.3 collective-permute-done.49.refs_2_.refs_11_.refs_19_
  307.6 4.6 add_first1_second1.1
  315.3 2.5 add_down0.1
  318.8 19.4 %shard_map.195 = (f32[544,768]{1,0:T(8,128)}, f32[8,768]{1,0:T(8,128)}, f32[1,3072]{1,0:T(1,128)}, bf16[2,2,2,4,96,384]{5,4,3,2,1,0:T(8,128)(2,1)}, bf16[2,2,2,4,96,384]{5,4,3,2,1,0:T(8,128)(2,1)}) custom-call(s32[4]{0:T(128)} %pad_add_fusion.pos_ref, f32[16,3072]{1,0:T(8,128)} %shard_map.172.params_ref, f32[544,768]{1,0:T(8,128)} %get-tuple-element.272.second_ref, ...), custom_call_target="tpu_custom_call" | custom-call | flops 21849999360 | tf_op jit(solution)/shard_map/pallas_call | solution.py:720
  338.2 6.0 %collective-permute-done.55.refs_4_.refs_11_.refs_14_ = bf16[2,4,96,384]{3,2,1,0:T(8,128)(2,1)} collective-permute-done((bf16[2,4,96,384]{3,2,1,0:T(8,128)(2,1)}, bf16[2,4,96,384]{3,2,1,0:T(8,128)(2,1)}, u32[]{:S(2)}, u32[]{:S(2)}) %collective-permute-start.55) | collective-permute-done | bytes 589856 | tf_op jit(solution)/shard_map/sum_down0_first/ppermute | solution.py:1112
  344.4 2.6 add_first1.1
  349.2 2.5 add_up0.1
  353.6 12.9 %shard_map.199.refs_3_.grads_ref = bf16[18,544,128]{2,1,0:T(8,128)(2,1)} custom-call(s32[4]{0:T(128)} %pad_add_fusion.pos_ref, f32[544,768]{1,0:T(8,128)} %get-tuple-element.283.grad_ref, bf16[18,544,128]{2,1,0:T(8,128)(2,1)} %get-tuple-element.284.qkv_ref, bf16[2,6,272,512]{3,2,1,0:T(8,128)(2,1)} %get-tuple-element.285.probs_ref, ...), custom_call_target="tpu_custom_call" | custom-call | flops 14949999616 | tf_op jit(solution)/shard_map/pallas_call | solution.py:720
  366.5 3.9 collective-permute-done.58.refs_8_.refs_6_
  371.7 4.3 add_second0_first1.1
  377.1 8.7 %shard_map.202 = (bf16[2,2,2,4,112,384]{5,4,3,2,1,0:T(8,128)(2,1)}, bf16[2,2,2,4,112,384]{5,4,3,2,1,0:T(8,128)(2,1)}) custom-call(s32[4]{0:T(128)} %pad_add_fusion.pos_ref, f32[8,768]{1,0:T(8,128)} %get-tuple-element.309.down_sums_ref, f32[8,768]{1,0:T(8,128)} %get-tuple-element.310.up_sums_ref, f32[1,3072]{1,0:T(1,128)} %get-tuple-element.311.up_bias_ref, ...), custom_call_target="tpu_custom_call" | custom-call | flops 9200000000 | tf_op jit(solution)/shard_map/pallas_call | solution.py:720
  385.7 5.3 %collective-permute-done.62.refs_7_.refs_15_.refs_2_ = bf16[2,4,96,384]{3,2,1,0:T(8,128)(2,1)} collective-permute-done((bf16[2,4,96,384]{3,2,1,0:T(8,128)(2,1)}, bf16[2,4,96,384]{3,2,1,0:T(8,128)(2,1)}, u32[]{:S(2)}, u32[]{:S(2)}) %collective-permute-start.62) | collective-permute-done | bytes 589856 | tf_op jit(solution)/shard_map/sum_second0_second/ppermute | solution.py:1112
  391.3 3.6 add_second0.1.refs_0_
  395.6 8.0 %shard_map.204.refs_4_ = f32[544,768]{1,0:T(8,128)} custom-call(s32[4]{0:T(128)} %pad_add_fusion.pos_ref, f32[544,768]{1,0:T(8,128)} %get-tuple-element.283.grad_ref, bf16[18,544,128]{2,1,0:T(8,128)(2,1)} %shard_map.199.refs_3_.grads_ref, bf16[2,4,1,112,384]{4,3,2,1,0:T(8,128)(2,1)} %get-tuple-element.185.near_ref.refs_0_, ...), custom_call_target="tpu_custom_call" | custom-call | flops 6899999744 | tf_op jit(solution)/shard_map/pallas_call | solution.py:720
  403.6 2.7 add_first0.2
  409.8 14.4 %collective-permute-done.65.refs_2_ = bf16[2,4,112,384]{3,2,1,0:T(8,128)(2,1)} collective-permute-done((bf16[2,4,112,384]{3,2,1,0:T(8,128)(2,1)}, bf16[2,4,112,384]{3,2,1,0:T(8,128)(2,1)}, u32[]{:S(2)}, u32[]{:S(2)}) %collective-permute-start.65) | collective-permute-done | bytes 688160 | tf_op jit(solution)/shard_map/sum_first0_first/ppermute | solution.py:1112
  430.5 8.7 %collective-permute-done.69.refs_3_ = bf16[1,4,112,384]{3,2,1,0:T(8,128)(2,1)} collective-permute-done((bf16[1,4,112,384]{3,2,1,0:T(8,128)(2,1)}, bf16[1,4,112,384]{3,2,1,0:T(8,128)(2,1)}, u32[]{:S(2)}, u32[]{:S(2)}) %collective-permute-start.69) | collective-permute-done | bytes 344096 | tf_op jit(solution)/shard_map/sum_first0_second/ppermute | solution.py:1112
  439.2 4.6 share_first0.2
  443.8 2.8 reduce-scatter.8.cloned.1.call-done
  452.6 3.5 collective-permute-done.72.refs_1_
  456.1 6.0 %collective-permute-done.73.refs_2_ = bf16[2,112,384]{2,1,0:T(8,128)(2,1)} collective-permute-done((bf16[2,112,384]{2,1,0:T(8,128)(2,1)}, bf16[2,112,384]{2,1,0:T(8,128)(2,1)}, u32[]{:S(2)}, u32[]{:S(2)}) %collective-permute-start.73) | collective-permute-done | bytes 172064 | tf_op jit(solution)/shard_map/share_first0/ppermute | solution.py:1112
  466.5 4.1 shard_map.210
  473.4 3.0 shard_map.212
  (215 shorter events, 99.1 us)
Async XLA Ops:
  7.2 107.1 %all-gather.3.cloned.1.call-start = ((), (), s32[]{:S(2)}) async-start(), calls=%async_computation.6 | async-start | bytes 2211840 | tf_op jit(solution)/shard_map/columns_third/all_gather | solution.py:1311
  33.1 17.2 %collective-permute-start.4 = (bf16[2,4,1,112,384]{4,3,2,1,0:T(8,128)(2,1)}, bf16[2,4,1,112,384]{4,3,2,1,0:T(8,128)(2,1)S(1)}, u32[]{:S(2)}, u32[]{:S(2)}) collective-permute-start(bf16[2,4,1,112,384]{4,3,2,1,0:T(8,128)(2,1)} %columns_first0.1.refs_0_.refs_1_), channel_id=1, source_target_pairs={{0,16},{1,17},{2,18},{3,19},{4,20},{5,21},{6,22},{7,23},{8,24},{9,... | collective-permute-start | bytes 2064392 | tf_op jit(solution)/shard_map/gather_first0_first/ppermute | solution.py:1112
  34.6 17.0 %collective-permute-start.3 = (bf16[2,4,1,112,384]{4,3,2,1,0:T(8,128)(2,1)}, bf16[2,4,1,112,384]{4,3,2,1,0:T(8,128)(2,1)S(1)}, u32[]{:S(2)}, u32[]{:S(2)}) collective-permute-start(bf16[2,4,1,112,384]{4,3,2,1,0:T(8,128)(2,1)} %columns_first0.1.refs_0_.refs_1_), channel_id=1, source_target_pairs={{0,1},{1,0},{2,3},{3,2},{4,5},{5,4},{6,7},{7,6},{8,9},{9,8},{10,11... | collective-permute-start | bytes 2064392 | tf_op jit(solution)/shard_map/gather_first0_first/ppermute | solution.py:1112
  36.1 16.8 %collective-permute-start.12 = (bf16[2,2,96,384]{3,2,1,0:T(8,128)(2,1)}, bf16[2,2,96,384]{3,2,1,0:T(8,128)(2,1)}, u32[]{:S(2)}, u32[]{:S(2)}) collective-permute-start(bf16[2,2,96,384]{3,2,1,0:T(8,128)(2,1)} %columns_second0.2.refs_0_), channel_id=1, source_target_pairs={{0,6},{1,7},{2,0},{3,1},{4,2},{5,3},{6,4},{7,5},{8,14},{9,15},{10,... | collective-permute-start | bytes 884744 | tf_op jit(solution)/shard_map/columns_second0/ppermute | solution.py:1112
  37.0 27.0 %collective-permute-start.11 = (bf16[2,2,96,384]{3,2,1,0:T(8,128)(2,1)}, bf16[2,2,96,384]{3,2,1,0:T(8,128)(2,1)}, u32[]{:S(2)}, u32[]{:S(2)}) collective-permute-start(bf16[2,2,96,384]{3,2,1,0:T(8,128)(2,1)} %columns_second0.2.refs_0_), channel_id=1, source_target_pairs={{0,4},{1,5},{2,6},{3,7},{4,0},{5,1},{6,2},{7,3},{8,12},{9,13},{10,... | collective-permute-start | bytes 884744 | tf_op jit(solution)/shard_map/columns_second0/ppermute | solution.py:1112
  38.9 25.7 %collective-permute-start.10 = (bf16[2,2,96,384]{3,2,1,0:T(8,128)(2,1)}, bf16[2,2,96,384]{3,2,1,0:T(8,128)(2,1)}, u32[]{:S(2)}, u32[]{:S(2)}) collective-permute-start(bf16[2,2,96,384]{3,2,1,0:T(8,128)(2,1)} %columns_second0.2.refs_0_), channel_id=1, source_target_pairs={{0,2},{1,3},{2,4},{3,5},{4,6},{5,7},{6,0},{7,1},{8,10},{9,11},{10,... | collective-permute-start | bytes 884744 | tf_op jit(solution)/shard_map/columns_second0/ppermute | solution.py:1112
  52.4 20.2 %collective-permute-start.7 = (bf16[2,4,1,112,384]{4,3,2,1,0:T(8,128)(2,1)}, bf16[2,4,1,112,384]{4,3,2,1,0:T(8,128)(2,1)}, u32[]{:S(2)}, u32[]{:S(2)}) collective-permute-start(bf16[2,4,1,112,384]{4,3,2,1,0:T(8,128)(2,1)} %get-tuple-element.181.refs_0_), channel_id=1, source_target_pairs={{0,8},{1,9},{2,10},{3,11},{4,12},{5,13},{6,14},{7,15},{8,0},{9,1},... | collective-permute-start | bytes 2064392 | tf_op jit(solution)/shard_map/gather_first0_cores/ppermute | solution.py:1112
  52.4 20.2 %collective-permute-start.8 = (bf16[2,4,1,112,384]{4,3,2,1,0:T(8,128)(2,1)}, bf16[2,4,1,112,384]{4,3,2,1,0:T(8,128)(2,1)}, u32[]{:S(2)}, u32[]{:S(2)}) collective-permute-start(bf16[2,4,1,112,384]{4,3,2,1,0:T(8,128)(2,1)} %get-tuple-element.182.refs_1_), channel_id=1, source_target_pairs={{0,8},{1,9},{2,10},{3,11},{4,12},{5,13},{6,14},{7,15},{8,0},{9,1},... | collective-permute-start | bytes 2064392 | tf_op jit(solution)/shard_map/gather_first0_cores/ppermute | solution.py:1112
  52.9 19.7 %collective-permute-start.9 = (bf16[2,4,1,112,384]{4,3,2,1,0:T(8,128)(2,1)}, bf16[2,4,1,112,384]{4,3,2,1,0:T(8,128)(2,1)}, u32[]{:S(2)}, u32[]{:S(2)}) collective-permute-start(bf16[2,4,1,112,384]{4,3,2,1,0:T(8,128)(2,1)} %get-tuple-element.183.refs_2_), channel_id=1, source_target_pairs={{0,8},{1,9},{2,10},{3,11},{4,12},{5,13},{6,14},{7,15},{8,0},{9,1},... | collective-permute-start | bytes 2064392 | tf_op jit(solution)/shard_map/gather_first0_cores/ppermute | solution.py:1112
  72.6 25.1 %collective-permute-start.16 = (bf16[2,4,2,96,384]{4,3,2,1,0:T(8,128)(2,1)}, bf16[2,4,2,96,384]{4,3,2,1,0:T(8,128)(2,1)}, u32[]{:S(2)}, u32[]{:S(2)}) collective-permute-start(bf16[2,4,2,96,384]{4,3,2,1,0:T(8,128)(2,1)} %get-tuple-element.194.refs_0_), channel_id=1, source_target_pairs={{0,16},{1,17},{2,18},{3,19},{4,20},{5,21},{6,22},{7,23},{8,24},{9,... | collective-permute-start | bytes 3538952 | tf_op jit(solution)/shard_map/gather_second0_first/ppermute | solution.py:1112
  74.2 24.7 %collective-permute-start.15 = (bf16[2,4,2,96,384]{4,3,2,1,0:T(8,128)(2,1)}, bf16[2,4,2,96,384]{4,3,2,1,0:T(8,128)(2,1)}, u32[]{:S(2)}, u32[]{:S(2)}) collective-permute-start(bf16[2,4,2,96,384]{4,3,2,1,0:T(8,128)(2,1)} %get-tuple-element.194.refs_0_), channel_id=1, source_target_pairs={{0,1},{1,0},{2,3},{3,2},{4,5},{5,4},{6,7},{7,6},{8,9},{9,8},{10,11... | collective-permute-start | bytes 3538952 | tf_op jit(solution)/shard_map/gather_second0_first/ppermute | solution.py:1112
  74.7 320.1 %reduce-scatter.4.cloned.1.call-start = ((), (), s32[]{:S(2)}) async-start(), calls=%async_computation.3 | async-start | bytes 1474560 | tf_op jit(solution)/shard_map/share_second1/reduce_scatter | solution.py:1226
  98.9 20.7 %collective-permute-start.19 = (bf16[2,4,2,96,384]{4,3,2,1,0:T(8,128)(2,1)}, bf16[2,4,2,96,384]{4,3,2,1,0:T(8,128)(2,1)}, u32[]{:S(2)}, u32[]{:S(2)}) collective-permute-start(bf16[2,4,2,96,384]{4,3,2,1,0:T(8,128)(2,1)} %get-tuple-element.196.refs_0_), channel_id=1, source_target_pairs={{0,8},{1,9},{2,10},{3,11},{4,12},{5,13},{6,14},{7,15},{8,0},{9,1},... | collective-permute-start | bytes 3538952 | tf_op jit(solution)/shard_map/gather_second0_cores/ppermute | solution.py:1112
  98.9 20.7 %collective-permute-start.20 = (bf16[2,4,2,96,384]{4,3,2,1,0:T(8,128)(2,1)}, bf16[2,4,2,96,384]{4,3,2,1,0:T(8,128)(2,1)}, u32[]{:S(2)}, u32[]{:S(2)}) collective-permute-start(bf16[2,4,2,96,384]{4,3,2,1,0:T(8,128)(2,1)} %get-tuple-element.197.refs_1_), channel_id=1, source_target_pairs={{0,8},{1,9},{2,10},{3,11},{4,12},{5,13},{6,14},{7,15},{8,0},{9,1},... | collective-permute-start | bytes 3538952 | tf_op jit(solution)/shard_map/gather_second0_cores/ppermute | solution.py:1112
  99.4 20.2 %collective-permute-start.21 = (bf16[2,4,2,96,384]{4,3,2,1,0:T(8,128)(2,1)}, bf16[2,4,2,96,384]{4,3,2,1,0:T(8,128)(2,1)}, u32[]{:S(2)}, u32[]{:S(2)}) collective-permute-start(bf16[2,4,2,96,384]{4,3,2,1,0:T(8,128)(2,1)} %get-tuple-element.198.refs_2_), channel_id=1, source_target_pairs={{0,8},{1,9},{2,10},{3,11},{4,12},{5,13},{6,14},{7,15},{8,0},{9,1},... | collective-permute-start | bytes 3538952 | tf_op jit(solution)/shard_map/gather_second0_cores/ppermute | solution.py:1112
  103.3 16.1 %collective-permute-start.18 = (bf16[4,2,96,384]{3,2,1,0:T(8,128)(2,1)}, bf16[4,2,96,384]{3,2,1,0:T(8,128)(2,1)}, u32[]{:S(2)}, u32[]{:S(2)}) collective-permute-start(bf16[4,2,96,384]{3,2,1,0:T(8,128)(2,1)} %slice_bitcast_fusion.2), channel_id=1, source_target_pairs={{0,1},{1,0},{2,3},{3,2},{4,5},{5,4},{6,7},{7,6},{8,9},{9,8},{10,11... | collective-permute-start | bytes 1769480 | tf_op jit(solution)/shard_map/gather_second0_second/ppermute | solution.py:1112
  120.2 24.7 %collective-permute-start.25 = (bf16[2,4,1,96,384]{4,3,2,1,0:T(8,128)(2,1)}, bf16[2,4,1,96,384]{4,3,2,1,0:T(8,128)(2,1)}, u32[]{:S(2)}, u32[]{:S(2)}) collective-permute-start(bf16[2,4,1,96,384]{4,3,2,1,0:T(8,128)(2,1)} %get-tuple-element.210.refs_0_), channel_id=1, source_target_pairs={{0,16},{1,17},{2,18},{3,19},{4,20},{5,21},{6,22},{7,23},{8,24},{9,... | collective-permute-start | bytes 1769480 | tf_op jit(solution)/shard_map/gather_first1_first/ppermute | solution.py:1112
  120.8 24.1 %collective-permute-start.24 = (bf16[2,4,1,96,384]{4,3,2,1,0:T(8,128)(2,1)}, bf16[2,4,1,96,384]{4,3,2,1,0:T(8,128)(2,1)}, u32[]{:S(2)}, u32[]{:S(2)}) collective-permute-start(bf16[2,4,1,96,384]{4,3,2,1,0:T(8,128)(2,1)} %get-tuple-element.210.refs_0_), channel_id=1, source_target_pairs={{0,1},{1,0},{2,3},{3,2},{4,5},{5,4},{6,7},{7,6},{8,9},{9,8},{10,11... | collective-permute-start | bytes 1769480 | tf_op jit(solution)/shard_map/gather_first1_first/ppermute | solution.py:1112
  122.3 48.1 %collective-permute-start.32 = (bf16[2,4,2,96,384]{4,3,2,1,0:T(8,128)(2,1)}, bf16[2,4,2,96,384]{4,3,2,1,0:T(8,128)(2,1)}, u32[]{:S(2)}, u32[]{:S(2)}) collective-permute-start(bf16[2,4,2,96,384]{4,3,2,1,0:T(8,128)(2,1)} %get-tuple-element.215.refs_8_), channel_id=1, source_target_pairs={{0,16},{1,17},{2,18},{3,19},{4,20},{5,21},{6,22},{7,23},{8,24},{9,... | collective-permute-start | bytes 3538952 | tf_op jit(solution)/shard_map/gather_second1_first/ppermute | solution.py:1112
  123.8 46.6 %collective-permute-start.31 = (bf16[2,4,2,96,384]{4,3,2,1,0:T(8,128)(2,1)}, bf16[2,4,2,96,384]{4,3,2,1,0:T(8,128)(2,1)}, u32[]{:S(2)}, u32[]{:S(2)}) collective-permute-start(bf16[2,4,2,96,384]{4,3,2,1,0:T(8,128)(2,1)} %get-tuple-element.215.refs_8_), channel_id=1, source_target_pairs={{0,1},{1,0},{2,3},{3,2},{4,5},{5,4},{6,7},{7,6},{8,9},{9,8},{10,11... | collective-permute-start | bytes 3538952 | tf_op jit(solution)/shard_map/gather_second1_first/ppermute | solution.py:1112
  145.9 21.4 %collective-permute-start.26 = (bf16[4,1,96,384]{3,2,1,0:T(8,128)(2,1)S(1)}, bf16[4,1,96,384]{3,2,1,0:T(8,128)(2,1)S(1)}, u32[]{:S(2)}, u32[]{:S(2)}) collective-permute-start(bf16[4,1,96,384]{3,2,1,0:T(8,128)(2,1)S(1)} %slice_bitcast_fusion.7), channel_id=1, source_target_pairs={{0,16},{1,17},{2,18},{3,19},{4,20},{5,21},{6,22},{7,23},{8,24},{9,... | collective-permute-start | bytes 884744 | tf_op jit(solution)/shard_map/gather_first1_second/ppermute | solution.py:1112
  147.5 20.1 %collective-permute-start.27 = (bf16[4,1,96,384]{3,2,1,0:T(8,128)(2,1)S(1)}, bf16[4,1,96,384]{3,2,1,0:T(8,128)(2,1)S(1)}, u32[]{:S(2)}, u32[]{:S(2)}) collective-permute-start(bf16[4,1,96,384]{3,2,1,0:T(8,128)(2,1)S(1)} %slice_bitcast_fusion.6), channel_id=1, source_target_pairs={{0,1},{1,0},{2,3},{3,2},{4,5},{5,4},{6,7},{7,6},{8,9},{9,8},{10,11... | collective-permute-start | bytes 884744 | tf_op jit(solution)/shard_map/gather_first1_second/ppermute | solution.py:1112
  149.1 20.4 %collective-permute-start.29 = (bf16[2,4,1,96,384]{4,3,2,1,0:T(8,128)(2,1)}, bf16[2,4,1,96,384]{4,3,2,1,0:T(8,128)(2,1)S(1)}, u32[]{:S(2)}, u32[]{:S(2)}) collective-permute-start(bf16[2,4,1,96,384]{4,3,2,1,0:T(8,128)(2,1)} %get-tuple-element.213.refs_1_), channel_id=1, source_target_pairs={{0,8},{1,9},{2,10},{3,11},{4,12},{5,13},{6,14},{7,15},{8,0},{9,1},... | collective-permute-start | bytes 1769480 | tf_op jit(solution)/shard_map/gather_first1_cores/ppermute | solution.py:1112
  173.7 20.9 %collective-permute-start.39 = (bf16[2,4,2,96,384]{4,3,2,1,0:T(8,128)(2,1)}, bf16[2,4,2,96,384]{4,3,2,1,0:T(8,128)(2,1)}, u32[]{:S(2)}, u32[]{:S(2)}) collective-permute-start(bf16[2,4,2,96,384]{4,3,2,1,0:T(8,128)(2,1)} %get-tuple-element.227.refs_2_), channel_id=1, source_target_pairs={{0,8},{1,9},{2,10},{3,11},{4,12},{5,13},{6,14},{7,15},{8,0},{9,1},... | collective-permute-start | bytes 3538952 | tf_op jit(solution)/shard_map/gather_second1_cores/ppermute | solution.py:1112
  173.8 20.7 %collective-permute-start.36 = (bf16[4,2,96,384]{3,2,1,0:T(8,128)(2,1)}, bf16[4,2,96,384]{3,2,1,0:T(8,128)(2,1)}, u32[]{:S(2)}, u32[]{:S(2)}) collective-permute-start(bf16[4,2,96,384]{3,2,1,0:T(8,128)(2,1)} %slice_bitcast_fusion), channel_id=1, source_target_pairs={{0,1},{1,0},{2,3},{3,2},{4,5},{5,4},{6,7},{7,6},{8,9},{9,8},{10,11... | collective-permute-start | bytes 1769480 | tf_op jit(solution)/shard_map/gather_second1_second/ppermute | solution.py:1112
  175.4 19.2 %collective-permute-start.38 = (bf16[2,4,2,96,384]{4,3,2,1,0:T(8,128)(2,1)}, bf16[2,4,2,96,384]{4,3,2,1,0:T(8,128)(2,1)}, u32[]{:S(2)}, u32[]{:S(2)}) collective-permute-start(bf16[2,4,2,96,384]{4,3,2,1,0:T(8,128)(2,1)} %get-tuple-element.226.refs_1_), channel_id=1, source_target_pairs={{0,8},{1,9},{2,10},{3,11},{4,12},{5,13},{6,14},{7,15},{8,0},{9,1},... | collective-permute-start | bytes 3538952 | tf_op jit(solution)/shard_map/gather_second1_cores/ppermute | solution.py:1112
  177.4 17.1 %collective-permute-start.35 = (bf16[4,2,96,384]{3,2,1,0:T(8,128)(2,1)}, bf16[4,2,96,384]{3,2,1,0:T(8,128)(2,1)}, u32[]{:S(2)}, u32[]{:S(2)}) collective-permute-start(bf16[4,2,96,384]{3,2,1,0:T(8,128)(2,1)} %slice_bitcast_fusion.1), channel_id=1, source_target_pairs={{0,16},{1,17},{2,18},{3,19},{4,20},{5,21},{6,22},{7,23},{8,24},{9,... | collective-permute-start | bytes 1769480 | tf_op jit(solution)/shard_map/gather_second1_second/ppermute | solution.py:1112
  178.3 16.2 %collective-permute-start.37 = (bf16[2,4,2,96,384]{4,3,2,1,0:T(8,128)(2,1)}, bf16[2,4,2,96,384]{4,3,2,1,0:T(8,128)(2,1)}, u32[]{:S(2)}, u32[]{:S(2)}) collective-permute-start(bf16[2,4,2,96,384]{4,3,2,1,0:T(8,128)(2,1)} %get-tuple-element.225.refs_0_), channel_id=1, source_target_pairs={{0,8},{1,9},{2,10},{3,11},{4,12},{5,13},{6,14},{7,15},{8,0},{9,1},... | collective-permute-start | bytes 3538952 | tf_op jit(solution)/shard_map/gather_second1_cores/ppermute | solution.py:1112
  229.1 19.9 %collective-permute-start.42 = (bf16[2,2,2,4,96,384]{5,4,3,2,1,0:T(8,128)(2,1)}, bf16[2,2,2,4,96,384]{5,4,3,2,1,0:T(8,128)(2,1)}, u32[]{:S(2)}, u32[]{:S(2)}) collective-permute-start(bf16[2,2,2,4,96,384]{5,4,3,2,1,0:T(8,128)(2,1)} %shard_map.184.refs_10_), channel_id=1, source_target_pairs={{0,8},{1,9},{2,10},{3,11},{4,12},{5,13},{6,14},{7,15},{8,0},{9,1},... | collective-permute-start | bytes 7077896 | tf_op jit(solution)/shard_map/sum_down1_cores/ppermute | solution.py:1112
  251.6 17.3 %collective-permute-start.45 = (bf16[2,4,96,384]{3,2,1,0:T(8,128)(2,1)}, bf16[2,4,96,384]{3,2,1,0:T(8,128)(2,1)}, u32[]{:S(2)}, u32[]{:S(2)}) collective-permute-start(bf16[2,4,96,384]{3,2,1,0:T(8,128)(2,1)} %get-tuple-element.263), channel_id=1, source_target_pairs={{0,16},{1,17},{2,18},{3,19},{4,20},{5,21},{6,22},{7,23},{8,24},{9,... | collective-permute-start | bytes 1769480 | tf_op jit(solution)/shard_map/sum_down1_first/ppermute | solution.py:1112
  269.0 19.0 %collective-permute-start.47 = (bf16[2,4,96,384]{3,2,1,0:T(8,128)(2,1)}, bf16[2,4,96,384]{3,2,1,0:T(8,128)(2,1)}, u32[]{:S(2)}, u32[]{:S(2)}) collective-permute-start(bf16[2,4,96,384]{3,2,1,0:T(8,128)(2,1)} %get-tuple-element.268), channel_id=1, source_target_pairs={{0,16},{1,17},{2,18},{3,19},{4,20},{5,21},{6,22},{7,23},{8,24},{9,... | collective-permute-start | bytes 1769480 | tf_op jit(solution)/shard_map/sum_up1_first/ppermute | solution.py:1112
  269.6 18.5 %collective-permute-start.46 = (bf16[2,4,96,384]{3,2,1,0:T(8,128)(2,1)}, bf16[2,4,96,384]{3,2,1,0:T(8,128)(2,1)}, u32[]{:S(2)}, u32[]{:S(2)}) collective-permute-start(bf16[2,4,96,384]{3,2,1,0:T(8,128)(2,1)} %get-tuple-element.264.refs_0_), channel_id=1, source_target_pairs={{0,1},{1,0},{2,3},{3,2},{4,5},{5,4},{6,7},{7,6},{8,9},{9,8},{10,11... | collective-permute-start | bytes 1769480 | tf_op jit(solution)/shard_map/sum_up1_first/ppermute | solution.py:1112
  291.2 16.4 %collective-permute-start.50 = (bf16[2,2,2,4,112,384]{5,4,3,2,1,0:T(8,128)(2,1)}, bf16[2,2,2,4,112,384]{5,4,3,2,1,0:T(8,128)(2,1)}, u32[]{:S(2)}, u32[]{:S(2)}) collective-permute-start(bf16[2,2,2,4,112,384]{5,4,3,2,1,0:T(8,128)(2,1)} %get-tuple-element.279), channel_id=1, source_target_pairs={{0,8},{1,9},{2,10},{3,11},{4,12},{5,13},{6,14},{7,15},{8,0},{9,1},... | collective-permute-start | bytes 8257544 | tf_op jit(solution)/shard_map/sum_first1_cores/ppermute | solution.py:1112
  312.2 26.1 %collective-permute-start.52 = (bf16[2,4,112,384]{3,2,1,0:T(8,128)(2,1)}, bf16[2,4,112,384]{3,2,1,0:T(8,128)(2,1)}, u32[]{:S(2)}, u32[]{:S(2)}) collective-permute-start(bf16[2,4,112,384]{3,2,1,0:T(8,128)(2,1)} %get-tuple-element.292), channel_id=1, source_target_pairs={{0,1},{1,0},{2,3},{3,2},{4,5},{5,4},{6,7},{7,6},{8,9},{9,8},{10,11... | collective-permute-start | bytes 2064392 | tf_op jit(solution)/shard_map/sum_first1_first/ppermute | solution.py:1112
  313.8 24.5 %collective-permute-start.53 = (bf16[2,4,112,384]{3,2,1,0:T(8,128)(2,1)}, bf16[2,4,112,384]{3,2,1,0:T(8,128)(2,1)}, u32[]{:S(2)}, u32[]{:S(2)}) collective-permute-start(bf16[2,4,112,384]{3,2,1,0:T(8,128)(2,1)} %get-tuple-element.293), channel_id=1, source_target_pairs={{0,16},{1,17},{2,18},{3,19},{4,20},{5,21},{6,22},{7,23},{8,24},{9,... | collective-permute-start | bytes 2064392 | tf_op jit(solution)/shard_map/sum_first1_first/ppermute | solution.py:1112
  317.8 26.5 %collective-permute-start.55 = (bf16[2,4,96,384]{3,2,1,0:T(8,128)(2,1)}, bf16[2,4,96,384]{3,2,1,0:T(8,128)(2,1)}, u32[]{:S(2)}, u32[]{:S(2)}) collective-permute-start(bf16[2,4,96,384]{3,2,1,0:T(8,128)(2,1)} %get-tuple-element.294), channel_id=1, source_target_pairs={{0,16},{1,17},{2,18},{3,19},{4,20},{5,21},{6,22},{7,23},{8,24},{9,... | collective-permute-start | bytes 1769480 | tf_op jit(solution)/shard_map/sum_down0_first/ppermute | solution.py:1112
  318.3 26.0 %collective-permute-start.54 = (bf16[2,4,96,384]{3,2,1,0:T(8,128)(2,1)}, bf16[2,4,96,384]{3,2,1,0:T(8,128)(2,1)}, u32[]{:S(2)}, u32[]{:S(2)}) collective-permute-start(bf16[2,4,96,384]{3,2,1,0:T(8,128)(2,1)} %get-tuple-element.282.refs_10_), channel_id=1, source_target_pairs={{0,1},{1,0},{2,3},{3,2},{4,5},{5,4},{6,7},{7,6},{8,9},{9,8},{10,11... | collective-permute-start | bytes 1769480 | tf_op jit(solution)/shard_map/sum_down0_first/ppermute | solution.py:1112
  344.3 83.6 %reduce-scatter.6.cloned.1.call-start = ((), (), s32[]{:S(2)}) async-start(), calls=%async_computation.4 | async-start | bytes 860160 | tf_op jit(solution)/shard_map/share_first1/reduce_scatter | solution.py:1226
  347.0 19.5 %collective-permute-start.59 = (bf16[1,4,112,384]{3,2,1,0:T(8,128)(2,1)}, bf16[1,4,112,384]{3,2,1,0:T(8,128)(2,1)}, u32[]{:S(2)}, u32[]{:S(2)}) collective-permute-start(bf16[1,4,112,384]{3,2,1,0:T(8,128)(2,1)} %get-tuple-element.301), channel_id=1, source_target_pairs={{0,16},{1,17},{2,18},{3,19},{4,20},{5,21},{6,22},{7,23},{8,24},{9,... | collective-permute-start | bytes 1032200 | tf_op jit(solution)/shard_map/sum_first1_second/ppermute | solution.py:1112
  348.5 18.0 %collective-permute-start.60 = (bf16[1,4,112,384]{3,2,1,0:T(8,128)(2,1)}, bf16[1,4,112,384]{3,2,1,0:T(8,128)(2,1)}, u32[]{:S(2)}, u32[]{:S(2)}) collective-permute-start(bf16[1,4,112,384]{3,2,1,0:T(8,128)(2,1)} %get-tuple-element.302), channel_id=1, source_target_pairs={{0,1},{1,0},{2,3},{3,2},{4,5},{5,4},{6,7},{7,6},{8,9},{9,8},{10,11... | collective-permute-start | bytes 1032200 | tf_op jit(solution)/shard_map/sum_first1_second/ppermute | solution.py:1112
  351.6 18.8 %collective-permute-start.58 = (bf16[2,4,96,384]{3,2,1,0:T(8,128)(2,1)}, bf16[2,4,96,384]{3,2,1,0:T(8,128)(2,1)}, u32[]{:S(2)}, u32[]{:S(2)}) collective-permute-start(bf16[2,4,96,384]{3,2,1,0:T(8,128)(2,1)} %get-tuple-element.298), channel_id=1, source_target_pairs={{0,16},{1,17},{2,18},{3,19},{4,20},{5,21},{6,22},{7,23},{8,24},{9,... | collective-permute-start | bytes 1769480 | tf_op jit(solution)/shard_map/sum_up0_first/ppermute | solution.py:1112
  353.1 18.5 %collective-permute-start.57 = (bf16[2,4,96,384]{3,2,1,0:T(8,128)(2,1)}, bf16[2,4,96,384]{3,2,1,0:T(8,128)(2,1)}, u32[]{:S(2)}, u32[]{:S(2)}) collective-permute-start(bf16[2,4,96,384]{3,2,1,0:T(8,128)(2,1)} %get-tuple-element.297.refs_10_), channel_id=1, source_target_pairs={{0,1},{1,0},{2,3},{3,2},{4,5},{5,4},{6,7},{7,6},{8,9},{9,8},{10,11... | collective-permute-start | bytes 1769480 | tf_op jit(solution)/shard_map/sum_up0_first/ppermute | solution.py:1112
  391.2 55.4 %reduce-scatter.8.cloned.1.call-start = ((), (), s32[]{:S(2)}) async-start(), calls=%async_computation.5 | async-start | bytes 1474560 | tf_op jit(solution)/shard_map/share_second0/reduce_scatter | solution.py:1226
  406.3 17.9 %collective-permute-start.65 = (bf16[2,4,112,384]{3,2,1,0:T(8,128)(2,1)}, bf16[2,4,112,384]{3,2,1,0:T(8,128)(2,1)}, u32[]{:S(2)}, u32[]{:S(2)}) collective-permute-start(bf16[2,4,112,384]{3,2,1,0:T(8,128)(2,1)} %get-tuple-element.318), channel_id=1, source_target_pairs={{0,1},{1,0},{2,3},{3,2},{4,5},{5,4},{6,7},{7,6},{8,9},{9,8},{10,11... | collective-permute-start | bytes 2064392 | tf_op jit(solution)/shard_map/sum_first0_first/ppermute | solution.py:1112
  407.8 17.6 %collective-permute-start.66 = (bf16[2,4,112,384]{3,2,1,0:T(8,128)(2,1)}, bf16[2,4,112,384]{3,2,1,0:T(8,128)(2,1)}, u32[]{:S(2)}, u32[]{:S(2)}) collective-permute-start(bf16[2,4,112,384]{3,2,1,0:T(8,128)(2,1)} %get-tuple-element.319), channel_id=1, source_target_pairs={{0,16},{1,17},{2,18},{3,19},{4,20},{5,21},{6,22},{7,23},{8,24},{9,... | collective-permute-start | bytes 2064392 | tf_op jit(solution)/shard_map/sum_first0_first/ppermute | solution.py:1112
  409.3 18.6 %collective-permute-start.67 = (bf16[4,96,384]{2,1,0:T(8,128)(2,1)}, bf16[4,96,384]{2,1,0:T(8,128)(2,1)}, u32[]{:S(2)}, u32[]{:S(2)}) collective-permute-start(bf16[4,96,384]{2,1,0:T(8,128)(2,1)} %get-tuple-element.323.refs_4_), channel_id=1, source_target_pairs={{0,8},{1,9},{2,10},{3,11},{4,12},{5,13},{6,14},{7,15},{8,0},{9,1},... | collective-permute-start | bytes 884744 | tf_op jit(solution)/shard_map/share_second1/ppermute | solution.py:1112
  409.3 18.6 %collective-permute-start.68 = (bf16[4,96,384]{2,1,0:T(8,128)(2,1)}, bf16[4,96,384]{2,1,0:T(8,128)(2,1)}, u32[]{:S(2)}, u32[]{:S(2)}) collective-permute-start(bf16[4,96,384]{2,1,0:T(8,128)(2,1)} %get-tuple-element.324.refs_5_), channel_id=1, source_target_pairs={{0,8},{1,9},{2,10},{3,11},{4,12},{5,13},{6,14},{7,15},{8,0},{9,1},... | collective-permute-start | bytes 884744 | tf_op jit(solution)/shard_map/share_second1/ppermute | solution.py:1112
  429.9 16.7 %collective-permute-start.71 = (bf16[2,112,384]{2,1,0:T(8,128)(2,1)}, bf16[2,112,384]{2,1,0:T(8,128)(2,1)}, u32[]{:S(2)}, u32[]{:S(2)}) collective-permute-start(bf16[2,112,384]{2,1,0:T(8,128)(2,1)} %get-tuple-element.332.refs_4_), channel_id=1, source_target_pairs={{0,16},{1,17},{2,18},{3,19},{4,20},{5,21},{6,22},{7,23},{8,24},{9,... | collective-permute-start | bytes 516104 | tf_op jit(solution)/shard_map/share_first1/ppermute | solution.py:1112
  (46 other events, 359.2 us)
Sparse Core Ops, SparseCore 0:
  74.8 39.3 all-gather.2
  344.4 30.8 reduce-scatter.3
  391.3 24.2 reduce-scatter.5
  418.5 28.0 reduce-scatter.7
